TPU v7x, 32 devices: a whole 2x2x4 slice. The times are simulated.
32 devices in a mesh: expert: 16 (over z, y, x), dp: 2 (over core).
Axes of the slice: x: 2, y: 2, z: 4, core: 2. Of those that a mesh axis runs over, the one named last changes fastest.
Arguments:
- layer_input: bfloat16 [4096, 3584], P(('expert', 'dp')), may hold values from -6 to 6
- out_grad: bfloat16 [4096, 3584], P(('expert', 'dp')), may hold values from -6 to 6
- routes: int32 [4096, 8], P(('expert', 'dp')), may hold values from 0 to 255, as said below
- gate_values: float32 [4096, 8], P(('expert', 'dp')), may hold values from 0.1 to 1
- keep_mask: int32 [4096, 8], P(('expert', 'dp')), may hold values 0 or 1
- gate_weight: bfloat16 [3584, 6144], P('dp', 'expert'), may hold values from -0.09375 to 0.09375
- up_weight: bfloat16 [3584, 6144], P('dp', 'expert'), may hold values from -0.09375 to 0.09375
- down_transposed: bfloat16 [3584, 6144], P('dp', 'expert'), may hold values from -0.15625 to 0.15625
Outputs:
- input_grad: bfloat16 [4096, 3584], P(('expert', 'dp'))
- gate_grad: bfloat16 [3584, 6144], P('dp', 'expert')
- up_grad: bfloat16 [3584, 6144], P('dp', 'expert')
- down_grad: bfloat16 [3584, 6144], P('dp', 'expert')
Inputs may be any that keep to these rules, and one draw needn't show every extreme that they name: `routes`: each token names 8 different experts. Among one device's 128 tokens no expert is named more than 5 times; on every device some expert below 4 is named exactly 5 times, and one expert below 4 is named 5 times on every device.
All inputs are finite; a program needn't handle non-finite values. No bound on the sum of `keep_mask` on one device may be relied on, other than what follows from the above.
Results may differ from a plain program's by a relative error of at most 0.0065.
Values may be sent and summed in bfloat16 or wider, within the bound.
No kernel may reach another device: no remote copies, remote signals or barrier semaphores. Data moves between devices by JAX's collectives and lax.ppermute only.
A program may use at most 128 MiB of HBM per device.

v0:
```python
import functools

import jax
import jax.numpy as jnp
from jax import lax
from jax.experimental import pallas as pl
from jax.experimental.pallas import tpu as pltpu
from jax.sharding import PartitionSpec as P

SPLIT = 4
MOST = 5
TOP = 8
SIDES = 2
CORES = 2
TOKEN_GROUP = 1
GROUPS = 2
FOLDS = 2
FIRST_MIB = 60
CHUNKS = 7

F32 = jnp.float32
BF16 = jnp.bfloat16


def params(mib=16):
    return pltpu.CompilerParams(vmem_limit_bytes=int(mib * 1024 * 1024))


def cost(flops, moved):
    return pl.CostEstimate(flops=int(flops), bytes_accessed=int(moved), transcendentals=0)


def iota(shape, axis):
    return lax.broadcasted_iota(jnp.int32, shape, axis)


def dot(a, b, dims=((1,), (0,))):
    return lax.dot_general(a, b, (dims, ((), ())), preferred_element_type=F32)


def one_hot(wanted, columns):
    return (iota((wanted.shape[0], columns), 1) == wanted).astype(F32).astype(BF16)


def pick_rows(routes, keep, gates, expert, slot, valid):
    rows, tokens = expert.shape[0], routes.shape[1]
    chosen = jnp.zeros((rows, tokens), F32)
    gate = jnp.zeros((rows, tokens), F32)
    for k in range(routes.shape[0]):
        hit = (routes[k : k + 1, :] == expert) & (keep[k : k + 1, :] == 1)
        chosen = jnp.where(hit, 1.0, chosen)
        gate = jnp.where(hit, gates[k : k + 1, :], gate)
    upto = (iota((tokens, tokens), 0) <= iota((tokens, tokens), 1)).astype(F32).astype(BF16)
    rank = dot(chosen.astype(BF16), upto)
    hot = (chosen > 0.5) & (rank == (slot + 1).astype(F32)) & valid
    return hot, gate


def near(k, core):
    if isinstance(core, int):
        return 3 - k if core and k in (1, 2) else k
    return jnp.where((core == 1) & (k > 0) & (k < 3), 3 - k, k)


def gather_kernel(live, *refs):
    sources, outs, local, sems = refs[:5], refs[5:8], refs[8:13], refs[13]
    copies = [pltpu.make_async_copy(sources[i], local[i], sems.at[i]) for i in range(5)]
    for copy in copies:
        copy.start()
    routes_ref, keep_ref, gates_ref, x_ref, o_ref = local
    place, me = lax.axis_index("expert") // SPLIT, lax.axis_index("dp")
    half = x_ref.shape[1] // CORES
    for copy in copies[:3]:
        copy.wait()
    routes, keep, gates = routes_ref[...], keep_ref[...], gates_ref[...]

    row = iota((live * 8, 1), 0)
    expert, slot = place ^ (row // 8), lax.rem(row, 8)
    hot, _ = pick_rows(routes, keep, gates, expert, slot, slot < MOST)
    outs[2][...] = hot.astype(F32)

    row = iota((live * SIDES * MOST, 1), 0)
    expert = place ^ (row // (SIDES * MOST))
    side, slot = lax.rem(row // MOST, SIDES), lax.rem(row, MOST)
    hot, gate = pick_rows(routes, keep, gates, expert, slot, row >= 0)
    hot_x = (hot & (side == 0)).astype(F32).astype(BF16)
    hot_s = hot & (side == 1)
    scale = jnp.sum(jnp.where(hot_s, gate, 0.0), axis=1, keepdims=True)
    hot_s = hot_s.astype(F32).astype(BF16)
    for copy in copies[3:]:
        copy.wait()
    for q in range(CORES):
        columns = pl.ds(pl.multiple_of((me ^ q) * half, 128), half)
        rows = dot(hot_x, x_ref[:, columns]) + scale * dot(hot_s, o_ref[:, columns])
        outs[q][...] = rows.astype(BF16)


def chunk_kernel(live, mine_ref, other_ref, *outs):
    me = lax.axis_index("dp")
    rows, half = mine_ref.shape
    fold = half // FOLDS
    each = SIDES * MOST
    stacked = jnp.concatenate([mine_ref[...], other_ref[...]], axis=0)
    size = FOLDS * CORES * each
    row = iota((live * size, 1), 0)
    d, part, at = row // size, lax.rem(row // (CORES * each), FOLDS), lax.rem(row, CORES * each)
    wanted = (at // each ^ me) * rows + d * each + lax.rem(at, each)
    total = jnp.zeros((live * size, fold), F32)
    for f in range(FOLDS):
        pick = one_hot(jnp.where(part == f, wanted, -1), CORES * rows)
        total = total + dot(pick, stacked[:, f * fold : (f + 1) * fold])
    total = total.astype(BF16)
    for d in range(live):
        outs[d][...] = total[d * size : (d + 1) * size]


def merge_kernel(*refs):
    chunks, out_ref = refs[:-1], refs[-1]
    size, fold = chunks[0].shape
    stacked = jnp.concatenate([chunk[...] for chunk in chunks], axis=0)
    rows = len(chunks) * CORES * MOST
    out = iota((SIDES * rows, 1), 0)
    side, at = out // rows, lax.rem(out, rows)
    d, replica, slot = at // (CORES * MOST), lax.rem(at // MOST, CORES), lax.rem(at, MOST)
    for f in range(FOLDS):
        wanted = d * size + ((f * CORES + replica) * SIDES + side) * MOST + slot
        picked = dot(one_hot(wanted, len(chunks) * size), stacked)
        out_ref[:, f * fold : (f + 1) * fold] = picked.astype(BF16)


def partial_kernel(*refs):
    blocks, (gate_ref, up_ref, down_ref, out_ref), sided = refs[:SPLIT], refs[SPLIT:-2], refs[-2:]
    each, width = blocks[0].shape[0], gate_ref.shape[1]
    rows = each // SIDES
    stacked = jnp.concatenate([block[...] for block in blocks], axis=0)
    at = iota((SPLIT * rows, 1), 0)
    block = near(at // rows, lax.axis_index("dp"))
    for side in range(SIDES):
        wanted = block * each + side * rows + lax.rem(at, rows)
        sided[side][...] = dot(one_hot(wanted, SPLIT * each), stacked).astype(BF16)
    out_ref[:, :width] = dot(sided[0][...], gate_ref[...])
    out_ref[:, width : 2 * width] = dot(sided[0][...], up_ref[...])
    out_ref[:, 2 * width :] = dot(sided[1][...], down_ref[...])


def sides_kernel(*refs):
    sums, (gate_ref, up_ref), outs = refs[: 2 * GROUPS], refs[2 * GROUPS : 2 * GROUPS + 2], refs[2 * GROUPS + 2 :]
    parts, sides_ref = outs[:-1], outs[-1]
    width = gate_ref.shape[1]
    rows = parts[0].shape[0] * GROUPS
    total = [sums[i][...] + sums[GROUPS + i][...] for i in range(GROUPS)]
    total = jnp.concatenate(total, axis=0)
    pre_gate, pre_up = total[:, :width], total[:, width : 2 * width]
    hidden_grad = total[:, 2 * width :]
    sigma = jax.nn.sigmoid(pre_gate)
    activated = pre_gate * sigma
    slope = sigma * (1.0 + pre_gate * (1.0 - sigma))
    gate_side = (hidden_grad * pre_up * slope).astype(BF16)
    up_side = (hidden_grad * activated).astype(BF16)
    sides_ref[:, :width] = gate_side
    sides_ref[:, width : 2 * width] = up_side
    sides_ref[:, 2 * width :] = (activated * pre_up).astype(BF16)
    across = ((1,), (1,))
    at = iota((SPLIT * rows, 1), 0)
    k = near(at // rows, lax.axis_index("dp"))
    group, row = lax.rem(at, rows) // (rows // GROUPS), lax.rem(at, rows // GROUPS)
    order = one_hot(((GROUPS - 1 - group) * SPLIT + k) * (rows // GROUPS) + row, SPLIT * rows)
    gate_side, up_side = dot(order, gate_side).astype(BF16), dot(order, up_side).astype(BF16)
    part = dot(gate_side, gate_ref[...], across) + dot(up_side, up_ref[...], across)
    each = rows // GROUPS
    for k in range(SPLIT):
        for group in range(GROUPS):
            start = (k * GROUPS + group) * each
            parts[group * SPLIT + k][...] = part[start : start + each].astype(BF16)


def grads_kernel(*refs):
    xs, ss = refs[:GROUPS], refs[GROUPS : 2 * GROUPS]
    sides_ref, outs, token_ref = refs[2 * GROUPS], refs[2 * GROUPS + 1 : -5], refs[-5]
    held, sems = refs[-4:-1], refs[-1]
    half, width = held[0].shape
    block = half // CHUNKS
    first = ((0,), (0,))
    copies = []
    for c in range(CHUNKS):
        part = slice(c * block, (c + 1) * block)
        x = jnp.concatenate([ref[:, part] for ref in xs], axis=0)
        s = jnp.concatenate([ref[:, part] for ref in ss], axis=0)
        for i, rows in enumerate((x, x, s)):
            held[i][part, :] = dot(rows, sides_ref[:, i * width : (i + 1) * width], first).astype(BF16)
            copy = pltpu.make_async_copy(
                held[i].at[pl.ds(c * block, block)], outs[i].at[pl.ds(c * block, block)], sems.at[i, c]
            )
            copy.start()
            copies.append(copy)
    for copy in copies:
        copy.wait()
    token_ref[...] = jnp.zeros(token_ref.shape, F32)


def sum_kernel(count, *refs):
    parts, outs = refs[:SPLIT], refs[SPLIT:]
    total = parts[0][...].astype(F32)
    for part in parts[1:]:
        total = total + part[...].astype(F32)
    total = total.astype(BF16)
    rows, half = total.shape
    fold = half // FOLDS
    each = CORES * MOST
    size = FOLDS * each
    row = iota((count * size, 1), 0)
    d, part, at = row // size, lax.rem(row // each, FOLDS), lax.rem(row, each)
    moved = jnp.zeros((count * size, fold), F32)
    for f in range(FOLDS):
        pick = one_hot(jnp.where(part == f, d * each + at, -1), rows)
        moved = moved + dot(pick, total[:, f * fold : (f + 1) * fold])
    for d in range(count):
        outs[d][...] = moved[d * size : (d + 1) * size].astype(BF16)


def split_kernel(count, *refs):
    chunks, outs = refs[:count], refs[-CORES:]
    me = lax.axis_index("dp")
    size, fold = chunks[0].shape
    stacked = jnp.concatenate([chunk[...].astype(F32) for chunk in chunks], axis=0).astype(BF16)
    rows = len(chunks) * 8
    out = iota((CORES * rows, 1), 0)
    q, d, slot = out // rows, lax.rem(out, rows) // 8, lax.rem(out, 8)
    for f in range(FOLDS):
        wanted = d * size + (f * CORES + (q ^ me)) * MOST + slot
        pick = one_hot(jnp.where(slot < MOST, wanted, -1), len(chunks) * size)
        picked = dot(pick, stacked).astype(BF16)
        for core in range(CORES):
            outs[core][:, f * fold : (f + 1) * fold] = picked[core * rows : (core + 1) * rows]


def place_kernel(hot_ref, *refs):
    sources, out_ref = refs[:-1], refs[-1]
    me = lax.axis_index("dp")
    half = out_ref.shape[1] // CORES
    hot = hot_ref[...].astype(BF16)
    for q in range(CORES):
        rows = jnp.concatenate([ref[...] for ref in sources[q * GROUPS : (q + 1) * GROUPS]], axis=0)
        columns = pl.ds(pl.multiple_of((me ^ q) * half, 128), half)
        out_ref[:, columns] = dot(hot, rows, ((0,), (0,))).astype(BF16)


def like(shape, dtype):
    return jax.ShapeDtypeStruct(shape, dtype)


def body(
    layer_input, out_grad, routes, gate_values, keep_mask, gate_weight, up_weight, down_transposed
):
    devices = lax.axis_size("expert")
    live = devices // SPLIT
    tokens, model = layer_input.shape
    half, width = gate_weight.shape
    fold = half // FOLDS
    rows = CORES * live * MOST
    total = SPLIT * rows
    vmem, hbm = pl.BlockSpec(memory_space=pltpu.VMEM), pl.BlockSpec(memory_space=pltpu.HBM)

    def call(kernel, name, out_shape, operands, flops=0, moved=0):
        return pl.pallas_call(
            kernel,
            out_shape=out_shape,
            in_specs=[vmem] * len(operands),
            out_specs=jax.tree.map(lambda _: vmem, out_shape),
            compiler_params=params(),
            cost_estimate=cost(flops, moved) if flops else None,
            name=name,
        )(*operands)

    def swap_cores(array):
        return lax.ppermute(array, "dp", [(r, r ^ 1) for r in range(CORES)])

    def along_z(array, d):
        hop = [(i, (i // SPLIT ^ d) * SPLIT + i % SPLIT) for i in range(devices)]
        return lax.ppermute(array, "expert", hop)

    def in_plane(array, k):
        hop = []
        for i in range(devices):
            for r in range(CORES):
                hop.append((i * CORES + r, (i ^ near(k, r)) * CORES + r))
        return lax.ppermute(array, ("expert", "dp"), hop)

    gathered = like((live * SIDES * MOST, half), BF16)
    mine, other, hot = pl.pallas_call(
        lambda *refs: gather_kernel(live, *refs),
        out_shape=[gathered, gathered, like((live * 8, tokens), F32)],
        in_specs=[hbm] * 5,
        out_specs=[vmem] * 3,
        scratch_shapes=[
            pltpu.VMEM((TOP, tokens), jnp.int32),
            pltpu.VMEM((TOP, tokens), jnp.int32),
            pltpu.VMEM((TOP, tokens), F32),
            pltpu.VMEM((tokens, model), BF16),
            pltpu.VMEM((tokens, model), BF16),
            pltpu.SemaphoreType.DMA((5,)),
        ],
        compiler_params=params(FIRST_MIB),
        name="gather_rows",
    )(routes.T, keep_mask.T, gate_values.T, layer_input, out_grad)
    chunks = call(
        lambda *refs: chunk_kernel(live, *refs),
        "chunk_rows",
        [like((FOLDS * CORES * SIDES * MOST, fold), BF16)] * live,
        [mine, swap_cores(other)],
        1e10,
        2e7,
    )
    chunks = [chunks[0]] + [along_z(chunks[d], d) for d in range(1, live)]
    mines, others, xs, ss = [], [], [], []
    rows_in_group, planes = total // GROUPS, live // GROUPS
    for group in reversed(range(GROUPS)):
        rows_here = call(
            merge_kernel,
            "merge_rows",
            like((SIDES * rows // GROUPS, half), BF16),
            chunks[group * planes : (group + 1) * planes],
            1e8,
            1e6,
        )
        first, second = in_plane(rows_here, 1), in_plane(rows_here, 2)
        across = in_plane(first, 2)
        mine, x, s = call(
            partial_kernel,
            "partial_products",
            [like((rows_in_group, 3 * width), F32)] + [like((rows_in_group, half), BF16)] * SIDES,
            [rows_here, first, second, across, gate_weight, up_weight, down_transposed],
            6 * rows_in_group * half * width,
            6 * half * width,
        )
        mines.append(mine)
        others.append(swap_cores(mine))
        xs.append(x)
        ss.append(s)
    sided = call(
        sides_kernel,
        "sides_and_parts",
        [like((rows // GROUPS, half), BF16)] * (GROUPS * SPLIT) + [like((total, 3 * width), BF16)],
        [*mines, *others, gate_weight, up_weight],
        4 * total * half * width,
        4 * half * width,
    )
    parts, sides = [], sided[-1]
    for group in range(GROUPS):
        mine = sided[group * SPLIT : (group + 1) * SPLIT]
        parts.append([mine[0]] + [in_plane(mine[k], k) for k in reversed(range(1, SPLIT))])
    gate_grad, up_grad, down_grad, token = pl.pallas_call(
        grads_kernel,
        out_shape=[like((half, width), BF16)] * 3 + [like((8, 128), F32)],
        in_specs=[vmem] * (2 * GROUPS + 1),
        out_specs=[hbm] * 3 + [vmem],
        scratch_shapes=[pltpu.VMEM((half, width), BF16)] * 3 + [pltpu.SemaphoreType.DMA((3, CHUNKS))],
        compiler_params=params(),
        cost_estimate=cost(6 * total * half * width, 6 * half * width + 4 * total * half),
        name="weight_grads",
    )(*xs, *ss, sides)
    back, over = [], []
    for group in range(GROUPS):
        ordered = group == TOKEN_GROUP
        chunks = call(
            functools.partial(sum_kernel, planes),
            "sum_parts",
            [like((FOLDS * CORES * MOST, fold), BF16)] * planes,
            parts[group],
        )
        first = group * planes
        chunks = [along_z(chunks[d], first + d) if first + d else chunks[0] for d in range(planes)]
        mine, other = call(
            functools.partial(split_kernel, planes),
            "split_rows",
            [like((planes * 8, half), BF16)] * CORES,
            chunks + [token] * ordered,
            1e10 if group else 1e8,
            1e6,
        )
        back.append(mine)
        over.append(swap_cores(other))
    input_grad = call(place_kernel, "place_rows", like((tokens, model), BF16), [hot, *back, *over])
    return (input_grad, gate_grad, up_grad, down_grad)


def solution(mesh):
    return jax.shard_map(
        body,
        mesh=mesh,
        in_specs=(
            P(("expert", "dp"), None),
            P(("expert", "dp"), None),
            P(("expert", "dp"), None),
            P(("expert", "dp"), None),
            P(("expert", "dp"), None),
            P("dp", "expert"),
            P("dp", "expert"),
            P("dp", "expert"),
        ),
        out_specs=(
            P(("expert", "dp"), None),
            P("dp", "expert"),
            P("dp", "expert"),
            P("dp", "expert"),
        ),
        check_vma=False,
    )
```

profile of v0, /device:TPU:0, one launch (start us, length us, event | category | flops | bytes accessed | tf_op | source)
XLA Modules:
  0.0 56.8 jit_solution(14413132345300271868)
XLA Ops:
  0.6 2.6 %gather_rows.1 = (bf16[40,1792]{1,0:T(8,128)(2,1)}, bf16[40,1792]{1,0:T(8,128)(2,1)}, f32[32,128]{1,0:T(8,128)}) custom-call(s32[8,128]{1,0:T(8,128)} %bitcast.3, s32[8,128]{1,0:T(8,128)} %bitcast.4, f32[8,128]{1,0:T(8,128)} %bitcast.5, bf16[128,3584]{1,0:T(8,128)(2,1)} %refs_3_.1, bf16[128,3584]{1,0:T(8,128)(2,1)} %refs_4_.4), custom_call_target="tpu_custom_call" | custom-call | tf_op jit(solution)/shard_map/gather_rows/pallas_call | solution.py:290
  3.2 0.5 collective-permute-start
  3.8 1.2 %collective-permute-done.refs_1_ = bf16[40,1792]{1,0:T(8,128)(2,1)S(1)} collective-permute-done((bf16[40,1792]{1,0:T(8,128)(2,1)}, bf16[40,1792]{1,0:T(8,128)(2,1)S(1)}, u32[]{:S(2)}, u32[]{:S(2)}) %collective-permute-start) | collective-permute-done | bytes 143392 | tf_op jit(solution)/shard_map/ppermute | solution.py:276
  5.0 0.9 %copy-done.4 = bf16[40,1792]{1,0:T(8,128)(2,1)S(1)} copy-done((bf16[40,1792]{1,0:T(8,128)(2,1)S(1)}, bf16[40,1792]{1,0:T(8,128)(2,1)}, u32[]{:S(2)}) %copy-start.4) | copy-done | bytes 143384
  5.9 0.4 chunk_rows.1
  6.3 3.0 %collective-permute-start.6 = (bf16[40,896]{1,0:T(8,128)(2,1)S(1)}, bf16[40,896]{1,0:T(8,128)(2,1)S(1)}, u32[]{:S(2)}, u32[]{:S(2)}) collective-permute-start(bf16[40,896]{1,0:T(8,128)(2,1)S(1)} %get-tuple-element.45), channel_id=1, source_target_pairs={{0,8},{2,10},{4,12},{6,14},{8,0},{10,2},{12,4},{14,6},{16,24},{18,... | collective-permute-start | bytes 215048 | tf_op jit(solution)/shard_map/ppermute | solution.py:280
  9.3 2.6 %collective-permute-start.1 = (bf16[40,896]{1,0:T(8,128)(2,1)S(1)}, bf16[40,896]{1,0:T(8,128)(2,1)S(1)}, u32[]{:S(2)}, u32[]{:S(2)}) collective-permute-start(bf16[40,896]{1,0:T(8,128)(2,1)S(1)} %get-tuple-element.41), channel_id=1, source_target_pairs={{0,16},{2,18},{4,20},{6,22},{8,24},{10,26},{12,28},{14,30},{16,0},... | collective-permute-start | bytes 215048 | tf_op jit(solution)/shard_map/ppermute | solution.py:280
  11.9 0.0 collective-permute-start.2
  11.9 0.0 collective-permute-done.6.refs_1_
  11.9 0.2 merge_rows.3.refs_0_
  12.1 1.8 %collective-permute-start.7 = (bf16[40,1792]{1,0:T(8,128)(2,1)S(1)}, bf16[40,1792]{1,0:T(8,128)(2,1)S(1)}, u32[]{:S(2)}, u32[]{:S(2)}) collective-permute-start(bf16[40,1792]{1,0:T(8,128)(2,1)S(1)} %merge_rows.3.refs_0_), channel_id=1, source_target_pairs={{0,2},{1,5},{2,0},{3,7},{4,6},{5,1},{6,4},{7,3},{8,10},{9,13},{10,... | collective-permute-start | bytes 430088 | tf_op jit(solution)/shard_map/ppermute | solution.py:287
  13.9 3.3 %collective-permute-done.1.refs_0_ = bf16[40,896]{1,0:T(8,128)(2,1)S(1)} collective-permute-done((bf16[40,896]{1,0:T(8,128)(2,1)S(1)}, bf16[40,896]{1,0:T(8,128)(2,1)S(1)}, u32[]{:S(2)}, u32[]{:S(2)}) %collective-permute-start.1) | collective-permute-done | bytes 71712 | tf_op jit(solution)/shard_map/ppermute | solution.py:280
  17.2 0.9 %collective-permute-done.2.refs_1_ = bf16[40,896]{1,0:T(8,128)(2,1)S(1)} collective-permute-done((bf16[40,896]{1,0:T(8,128)(2,1)S(1)}, bf16[40,896]{1,0:T(8,128)(2,1)S(1)}, u32[]{:S(2)}, u32[]{:S(2)}) %collective-permute-start.2) | collective-permute-done | bytes 71712 | tf_op jit(solution)/shard_map/ppermute | solution.py:280
  18.1 0.2 merge_rows.2.refs_0_
  18.3 1.6 %collective-permute-start.3 = (bf16[40,1792]{1,0:T(8,128)(2,1)S(1)}, bf16[40,1792]{1,0:T(8,128)(2,1)S(1)}, u32[]{:S(2)}, u32[]{:S(2)}) collective-permute-start(bf16[40,1792]{1,0:T(8,128)(2,1)S(1)} %merge_rows.2.refs_0_), channel_id=1, source_target_pairs={{0,2},{1,5},{2,0},{3,7},{4,6},{5,1},{6,4},{7,3},{8,10},{9,13},{10,... | collective-permute-start | bytes 430088 | tf_op jit(solution)/shard_map/ppermute | solution.py:287
  19.9 1.5 %collective-permute-start.8 = (bf16[40,1792]{1,0:T(8,128)(2,1)S(1)}, bf16[40,1792]{1,0:T(8,128)(2,1)S(1)}, u32[]{:S(2)}, u32[]{:S(2)}) collective-permute-start(bf16[40,1792]{1,0:T(8,128)(2,1)S(1)} %merge_rows.3.refs_0_), channel_id=1, source_target_pairs={{0,4},{1,3},{2,6},{3,1},{4,0},{5,7},{6,2},{7,5},{8,12},{9,11},{10,... | collective-permute-start | bytes 430088 | tf_op jit(solution)/shard_map/ppermute | solution.py:287
  21.4 0.0 collective-permute-done.7.refs_1_
  21.4 0.5 collective-permute-start.9
  21.9 1.5 %collective-permute-start.4 = (bf16[40,1792]{1,0:T(8,128)(2,1)S(1)}, bf16[40,1792]{1,0:T(8,128)(2,1)S(1)}, u32[]{:S(2)}, u32[]{:S(2)}) collective-permute-start(bf16[40,1792]{1,0:T(8,128)(2,1)S(1)} %merge_rows.2.refs_0_), channel_id=1, source_target_pairs={{0,4},{1,3},{2,6},{3,1},{4,0},{5,7},{6,2},{7,5},{8,12},{9,11},{10,... | collective-permute-start | bytes 430088 | tf_op jit(solution)/shard_map/ppermute | solution.py:287
  23.4 1.6 %collective-permute-done.3.refs_1_ = bf16[40,1792]{1,0:T(8,128)(2,1)S(1)} collective-permute-done((bf16[40,1792]{1,0:T(8,128)(2,1)S(1)}, bf16[40,1792]{1,0:T(8,128)(2,1)S(1)}, u32[]{:S(2)}, u32[]{:S(2)}) %collective-permute-start.3) | collective-permute-done | bytes 143392 | tf_op jit(solution)/shard_map/ppermute | solution.py:287
  25.1 1.5 %collective-permute-start.5 = (bf16[40,1792]{1,0:T(8,128)(2,1)S(1)}, bf16[40,1792]{1,0:T(8,128)(2,1)S(1)}, u32[]{:S(2)}, u32[]{:S(2)}) collective-permute-start(bf16[40,1792]{1,0:T(8,128)(2,1)S(1)} %collective-permute-done.3.refs_1_), channel_id=1, source_target_pairs={{0,4},{1,3},{2,6},{3,1},{4,0},{5,7},{6,2},{7,5},{8,12},{9,11},{10,... | collective-permute-start | bytes 430088 | tf_op jit(solution)/shard_map/ppermute | solution.py:287
  26.6 0.0 collective-permute-done.8.refs_2_
  26.6 0.0 collective-permute-done.9.refs_3_
  26.6 0.0 copy-done
  26.6 0.0 copy-done.1
  26.6 0.0 copy-done.2
  26.6 1.0 %partial_products.3 = (f32[80,1152]{1,0:T(8,128)S(1)}, bf16[80,1792]{1,0:T(8,128)(2,1)S(1)}, bf16[80,1792]{1,0:T(8,128)(2,1)S(1)}) custom-call(bf16[40,1792]{1,0:T(8,128)(2,1)S(1)} %merge_rows.3.refs_0_, bf16[40,1792]{1,0:T(8,128)(2,1)S(1)} %collective-permute-done.7.refs_1_, bf16[40,1792]{1,0:T(8,128)(2,1)S(1)} %collective-permute-done.8.refs_2_, ...), custom_call_target="tpu_custom_call" | custom-call | flops 330301440 | bytes 4128768 | tf_op jit(solution)/shard_map/partial_products/pallas_call | solution.py:265
  27.6 0.1 collective-permute-start.11
  27.7 0.3 collective-permute-done.4.refs_2_
  28.0 2.1 %collective-permute-done.5.refs_3_ = bf16[40,1792]{1,0:T(8,128)(2,1)S(1)} collective-permute-done((bf16[40,1792]{1,0:T(8,128)(2,1)S(1)}, bf16[40,1792]{1,0:T(8,128)(2,1)S(1)}, u32[]{:S(2)}, u32[]{:S(2)}) %collective-permute-start.5) | collective-permute-done | bytes 143392 | tf_op jit(solution)/shard_map/ppermute | solution.py:287
  30.2 1.0 %partial_products.2 = (f32[80,1152]{1,0:T(8,128)S(1)}, bf16[80,1792]{1,0:T(8,128)(2,1)S(1)}, bf16[80,1792]{1,0:T(8,128)(2,1)S(1)}) custom-call(bf16[40,1792]{1,0:T(8,128)(2,1)S(1)} %merge_rows.2.refs_0_, bf16[40,1792]{1,0:T(8,128)(2,1)S(1)} %collective-permute-done.3.refs_1_, bf16[40,1792]{1,0:T(8,128)(2,1)S(1)} %collective-permute-done.4.refs_2_, ...), custom_call_target="tpu_custom_call" | custom-call | flops 330301440 | bytes 4128768 | tf_op jit(solution)/shard_map/partial_products/pallas_call | solution.py:265
  31.2 0.1 collective-permute-start.10
  31.3 0.0 collective-permute-done.11.refs_3_
  31.3 1.7 %collective-permute-done.10.refs_2_ = f32[80,1152]{1,0:T(8,128)S(1)} collective-permute-done((f32[80,1152]{1,0:T(8,128)S(1)}, f32[80,1152]{1,0:T(8,128)S(1)}, u32[]{:S(2)}, u32[]{:S(2)}) %collective-permute-start.10) | collective-permute-done | bytes 368672 | tf_op jit(solution)/shard_map/ppermute | solution.py:276
  32.9 1.4 %sides_and_parts.1 = (bf16[20,1792]{1,0:T(8,128)(2,1)S(1)}, bf16[20,1792]{1,0:T(8,128)(2,1)S(1)}, bf16[20,1792]{1,0:T(8,128)(2,1)S(1)}, bf16[20,1792]{1,0:T(8,12...) custom-call(f32[80,1152]{1,0:T(8,128)S(1)} %get-tuple-element.43.ref, ...), custom_call_target="tpu_custom_call" | custom-call | flops 440401920 | bytes 2752512 | tf_op jit(solution)/shard_map/sides_and_parts/pallas_call | solution.py:265
  34.4 2.5 %collective-permute-start.12 = (bf16[20,1792]{1,0:T(8,128)(2,1)S(1)}, bf16[20,1792]{1,0:T(8,128)(2,1)S(1)}, u32[]{:S(2)}, u32[]{:S(2)}) collective-permute-start(bf16[20,1792]{1,0:T(8,128)(2,1)S(1)} %get-tuple-element.48), channel_id=1, source_target_pairs={{0,6},{1,7},{2,4},{3,5},{4,2},{5,3},{6,0},{7,1},{8,14},{9,15},{10,... | collective-permute-start | bytes 215048 | tf_op jit(solution)/shard_map/ppermute | solution.py:287
  36.9 0.5 collective-permute-start.13
  37.4 0.5 collective-permute-start.14
  37.9 2.5 %collective-permute-start.16 = (bf16[20,1792]{1,0:T(8,128)(2,1)S(1)}, bf16[20,1792]{1,0:T(8,128)(2,1)S(1)}, u32[]{:S(2)}, u32[]{:S(2)}) collective-permute-start(bf16[20,1792]{1,0:T(8,128)(2,1)S(1)} %get-tuple-element.55), channel_id=1, source_target_pairs={{0,6},{1,7},{2,4},{3,5},{4,2},{5,3},{6,0},{7,1},{8,14},{9,15},{10,... | collective-permute-start | bytes 215048 | tf_op jit(solution)/shard_map/ppermute | solution.py:287
  40.4 0.5 collective-permute-start.17
  40.9 0.0 collective-permute-done.12.refs_1_
  40.9 1.3 %collective-permute-start.18 = (bf16[20,1792]{1,0:T(8,128)(2,1)S(1)}, bf16[20,1792]{1,0:T(8,128)(2,1)S(1)}, u32[]{:S(2)}, u32[]{:S(2)}) collective-permute-start(bf16[20,1792]{1,0:T(8,128)(2,1)S(1)} %get-tuple-element.57), channel_id=1, source_target_pairs={{0,2},{1,5},{2,0},{3,7},{4,6},{5,1},{6,4},{7,3},{8,10},{9,13},{10,... | collective-permute-start | bytes 215048 | tf_op jit(solution)/shard_map/ppermute | solution.py:287
  42.2 1.0 %collective-permute-done.13.refs_2_ = bf16[20,1792]{1,0:T(8,128)(2,1)S(1)} collective-permute-done((bf16[20,1792]{1,0:T(8,128)(2,1)S(1)}, bf16[20,1792]{1,0:T(8,128)(2,1)S(1)}, u32[]{:S(2)}, u32[]{:S(2)}) %collective-permute-start.13) | collective-permute-done | bytes 71712 | tf_op jit(solution)/shard_map/ppermute | solution.py:287
  43.2 0.0 collective-permute-done.14.refs_3_
  43.2 0.2 sum_parts.2
  43.5 1.3 %collective-permute-start.15 = (bf16[20,896]{1,0:T(8,128)(2,1)S(1)}, bf16[20,896]{1,0:T(8,128)(2,1)S(1)}, u32[]{:S(2)}, u32[]{:S(2)}) collective-permute-start(bf16[20,896]{1,0:T(8,128)(2,1)S(1)} %get-tuple-element.52), channel_id=1, source_target_pairs={{0,8},{2,10},{4,12},{6,14},{8,0},{10,2},{12,4},{14,6},{16,24},{18,... | collective-permute-start | bytes 107528 | tf_op jit(solution)/shard_map/ppermute | solution.py:280
  44.8 0.0 collective-permute-done.16.refs_1_
  44.8 0.8 %collective-permute-done.17.refs_2_ = bf16[20,1792]{1,0:T(8,128)(2,1)S(1)} collective-permute-done((bf16[20,1792]{1,0:T(8,128)(2,1)S(1)}, bf16[20,1792]{1,0:T(8,128)(2,1)S(1)}, u32[]{:S(2)}, u32[]{:S(2)}) %collective-permute-start.17) | collective-permute-done | bytes 71712 | tf_op jit(solution)/shard_map/ppermute | solution.py:287
  45.6 0.0 collective-permute-done.18.refs_3_
  45.6 0.2 sum_parts.3
  45.8 2.3 %collective-permute-start.19 = (bf16[20,896]{1,0:T(8,128)(2,1)S(1)}, bf16[20,896]{1,0:T(8,128)(2,1)S(1)}, u32[]{:S(2)}, u32[]{:S(2)}) collective-permute-start(bf16[20,896]{1,0:T(8,128)(2,1)S(1)} %get-tuple-element.58), channel_id=1, source_target_pairs={{0,16},{2,18},{4,20},{6,22},{8,24},{10,26},{12,28},{14,30},{16,0},... | collective-permute-start | bytes 107528 | tf_op jit(solution)/shard_map/ppermute | solution.py:280
  48.1 1.4 %collective-permute-start.20 = (bf16[20,896]{1,0:T(8,128)(2,1)S(1)}, bf16[20,896]{1,0:T(8,128)(2,1)S(1)}, u32[]{:S(2)}, u32[]{:S(2)}) collective-permute-start(bf16[20,896]{1,0:T(8,128)(2,1)S(1)} %get-tuple-element.59), channel_id=1, source_target_pairs={{0,24},{2,26},{4,28},{6,30},{8,16},{10,18},{12,20},{14,22},{16,8},... | collective-permute-start | bytes 107528 | tf_op jit(solution)/shard_map/ppermute | solution.py:280
  49.5 2.5 %weight_grads.1 = (bf16[1792,384]{1,0:T(8,128)(2,1)}, bf16[1792,384]{1,0:T(8,128)(2,1)}, bf16[1792,384]{1,0:T(8,128)(2,1)}, f32[8,128]{1,0:T(8,128)S(1)}) custom-call(bf16[80,1792]{1,0:T(8,128)(2,1)S(1)} %get-tuple-element.60.refs_0_, bf16[80,1792]{1,0:T(8,128)(2,1)S(1)} %get-tuple-element.61.refs_1_, bf16[80,1792]{1,0:T(8,128)(2,1)S(1)} %get-tuple-element.62.refs_2_, ...), custom_call_target="tpu_custom_call" | custom-call | flops 660602880 | bytes 5275648 | tf_op jit(solution)/shard_map/weight_grads/pallas_call | solution.py:352
  52.0 0.0 collective-permute-done.15.refs_1_
  52.1 0.2 split_rows.2
  52.2 0.1 collective-permute-start.21
  52.3 0.0 collective-permute-done.19.refs_0_
  52.3 1.6 %collective-permute-done.20.refs_1_ = bf16[20,896]{1,0:T(8,128)(2,1)S(1)} collective-permute-done((bf16[20,896]{1,0:T(8,128)(2,1)S(1)}, bf16[20,896]{1,0:T(8,128)(2,1)S(1)}, u32[]{:S(2)}, u32[]{:S(2)}) %collective-permute-start.20) | collective-permute-done | bytes 35872 | tf_op jit(solution)/shard_map/ppermute | solution.py:280
  53.9 0.2 split_rows.3
  54.1 0.1 collective-permute-start.22
  54.2 0.0 collective-permute-done.21.refs_2_
  54.2 1.2 %collective-permute-done.22.refs_3_ = bf16[16,1792]{1,0:T(8,128)(2,1)S(1)} collective-permute-done((bf16[16,1792]{1,0:T(8,128)(2,1)S(1)}, bf16[16,1792]{1,0:T(8,128)(2,1)S(1)}, u32[]{:S(2)}, u32[]{:S(2)}) %collective-permute-start.22) | collective-permute-done | bytes 57376 | tf_op jit(solution)/shard_map/ppermute | solution.py:276
  55.4 0.0 copy-done.3
  55.4 1.4 %place_rows.1 = bf16[128,3584]{1,0:T(8,128)(2,1)} custom-call(f32[32,128]{1,0:T(8,128)S(1)} %copy-done.3, bf16[16,1792]{1,0:T(8,128)(2,1)S(1)} %get-tuple-element.53.refs_0_, bf16[16,1792]{1,0:T(8,128)(2,1)S(1)} %get-tuple-element.66.refs_1_, bf16[16,1792]{1,0:T(8,128)(2,1)S(1)} %collective-permute-done.21.refs_2_, ...), custom_call_target="tpu_custom_call" | custom-call | tf_op jit(solution)/shard_map/place_rows/pallas_call | solution.py:265
  (5 shorter events, 0.0 us)
Async XLA Ops:
  3.2 1.7 %collective-permute-start = (bf16[40,1792]{1,0:T(8,128)(2,1)}, bf16[40,1792]{1,0:T(8,128)(2,1)S(1)}, u32[]{:S(2)}, u32[]{:S(2)}) collective-permute-start(bf16[40,1792]{1,0:T(8,128)(2,1)} %get-tuple-element.40), channel_id=1, source_target_pairs={{0,1},{1,0},{2,3},{3,2},{4,5},{5,4},{6,7},{7,6},{8,9},{9,8},{10,11... | collective-permute-start | bytes 430088 | tf_op jit(solution)/shard_map/ppermute | solution.py:276
  5.0 0.9 %copy-start.4 = (bf16[40,1792]{1,0:T(8,128)(2,1)S(1)}, bf16[40,1792]{1,0:T(8,128)(2,1)}, u32[]{:S(2)}) copy-start(bf16[40,1792]{1,0:T(8,128)(2,1)} %get-tuple-element.39.refs_0_) | copy-start | bytes 430084
  5.9 20.7 %copy-start = (bf16[1792,384]{1,0:T(8,128)(2,1)S(1)}, bf16[1792,384]{1,0:T(8,128)(2,1)}, u32[]{:S(2)}) copy-start(bf16[1792,384]{1,0:T(8,128)(2,1)} %refs_4_.7) | copy-start | bytes 4128772
  5.9 20.7 %copy-start.1 = (bf16[1792,384]{1,0:T(8,128)(2,1)S(1)}, bf16[1792,384]{1,0:T(8,128)(2,1)}, u32[]{:S(2)}) copy-start(bf16[1792,384]{1,0:T(8,128)(2,1)} %refs_5_.5) | copy-start | bytes 4128772
  5.9 20.7 %copy-start.2 = (bf16[1792,384]{1,0:T(8,128)(2,1)S(1)}, bf16[1792,384]{1,0:T(8,128)(2,1)}, u32[]{:S(2)}) copy-start(bf16[1792,384]{1,0:T(8,128)(2,1)} %refs_6_.3) | copy-start | bytes 4128772
  6.3 5.6 %collective-permute-start.6 = (bf16[40,896]{1,0:T(8,128)(2,1)S(1)}, bf16[40,896]{1,0:T(8,128)(2,1)S(1)}, u32[]{:S(2)}, u32[]{:S(2)}) collective-permute-start(bf16[40,896]{1,0:T(8,128)(2,1)S(1)} %get-tuple-element.45), channel_id=1, source_target_pairs={{0,8},{2,10},{4,12},{6,14},{8,0},{10,2},{12,4},{14,6},{16,24},{18,... | collective-permute-start | bytes 215048 | tf_op jit(solution)/shard_map/ppermute | solution.py:280
  9.3 7.9 %collective-permute-start.1 = (bf16[40,896]{1,0:T(8,128)(2,1)S(1)}, bf16[40,896]{1,0:T(8,128)(2,1)S(1)}, u32[]{:S(2)}, u32[]{:S(2)}) collective-permute-start(bf16[40,896]{1,0:T(8,128)(2,1)S(1)} %get-tuple-element.41), channel_id=1, source_target_pairs={{0,16},{2,18},{4,20},{6,22},{8,24},{10,26},{12,28},{14,30},{16,0},... | collective-permute-start | bytes 215048 | tf_op jit(solution)/shard_map/ppermute | solution.py:280
  11.9 6.2 %collective-permute-start.2 = (bf16[40,896]{1,0:T(8,128)(2,1)S(1)}, bf16[40,896]{1,0:T(8,128)(2,1)S(1)}, u32[]{:S(2)}, u32[]{:S(2)}) collective-permute-start(bf16[40,896]{1,0:T(8,128)(2,1)S(1)} %get-tuple-element.42), channel_id=1, source_target_pairs={{0,24},{2,26},{4,28},{6,30},{8,16},{10,18},{12,20},{14,22},{16,8},... | collective-permute-start | bytes 215048 | tf_op jit(solution)/shard_map/ppermute | solution.py:280
  12.1 9.3 %collective-permute-start.7 = (bf16[40,1792]{1,0:T(8,128)(2,1)S(1)}, bf16[40,1792]{1,0:T(8,128)(2,1)S(1)}, u32[]{:S(2)}, u32[]{:S(2)}) collective-permute-start(bf16[40,1792]{1,0:T(8,128)(2,1)S(1)} %merge_rows.3.refs_0_), channel_id=1, source_target_pairs={{0,2},{1,5},{2,0},{3,7},{4,6},{5,1},{6,4},{7,3},{8,10},{9,13},{10,... | collective-permute-start | bytes 430088 | tf_op jit(solution)/shard_map/ppermute | solution.py:287
  18.3 6.8 %collective-permute-start.3 = (bf16[40,1792]{1,0:T(8,128)(2,1)S(1)}, bf16[40,1792]{1,0:T(8,128)(2,1)S(1)}, u32[]{:S(2)}, u32[]{:S(2)}) collective-permute-start(bf16[40,1792]{1,0:T(8,128)(2,1)S(1)} %merge_rows.2.refs_0_), channel_id=1, source_target_pairs={{0,2},{1,5},{2,0},{3,7},{4,6},{5,1},{6,4},{7,3},{8,10},{9,13},{10,... | collective-permute-start | bytes 430088 | tf_op jit(solution)/shard_map/ppermute | solution.py:287
  19.9 6.7 %collective-permute-start.8 = (bf16[40,1792]{1,0:T(8,128)(2,1)S(1)}, bf16[40,1792]{1,0:T(8,128)(2,1)S(1)}, u32[]{:S(2)}, u32[]{:S(2)}) collective-permute-start(bf16[40,1792]{1,0:T(8,128)(2,1)S(1)} %merge_rows.3.refs_0_), channel_id=1, source_target_pairs={{0,4},{1,3},{2,6},{3,1},{4,0},{5,7},{6,2},{7,5},{8,12},{9,11},{10,... | collective-permute-start | bytes 430088 | tf_op jit(solution)/shard_map/ppermute | solution.py:287
  21.4 5.2 %collective-permute-start.9 = (bf16[40,1792]{1,0:T(8,128)(2,1)S(1)}, bf16[40,1792]{1,0:T(8,128)(2,1)S(1)}, u32[]{:S(2)}, u32[]{:S(2)}) collective-permute-start(bf16[40,1792]{1,0:T(8,128)(2,1)S(1)} %collective-permute-done.7.refs_1_), channel_id=1, source_target_pairs={{0,4},{1,3},{2,6},{3,1},{4,0},{5,7},{6,2},{7,5},{8,12},{9,11},{10,... | collective-permute-start | bytes 430088 | tf_op jit(solution)/shard_map/ppermute | solution.py:287
  21.9 6.1 %collective-permute-start.4 = (bf16[40,1792]{1,0:T(8,128)(2,1)S(1)}, bf16[40,1792]{1,0:T(8,128)(2,1)S(1)}, u32[]{:S(2)}, u32[]{:S(2)}) collective-permute-start(bf16[40,1792]{1,0:T(8,128)(2,1)S(1)} %merge_rows.2.refs_0_), channel_id=1, source_target_pairs={{0,4},{1,3},{2,6},{3,1},{4,0},{5,7},{6,2},{7,5},{8,12},{9,11},{10,... | collective-permute-start | bytes 430088 | tf_op jit(solution)/shard_map/ppermute | solution.py:287
  25.1 5.1 %collective-permute-start.5 = (bf16[40,1792]{1,0:T(8,128)(2,1)S(1)}, bf16[40,1792]{1,0:T(8,128)(2,1)S(1)}, u32[]{:S(2)}, u32[]{:S(2)}) collective-permute-start(bf16[40,1792]{1,0:T(8,128)(2,1)S(1)} %collective-permute-done.3.refs_1_), channel_id=1, source_target_pairs={{0,4},{1,3},{2,6},{3,1},{4,0},{5,7},{6,2},{7,5},{8,12},{9,11},{10,... | collective-permute-start | bytes 430088 | tf_op jit(solution)/shard_map/ppermute | solution.py:287
  27.6 3.6 %collective-permute-start.11 = (f32[80,1152]{1,0:T(8,128)S(1)}, f32[80,1152]{1,0:T(8,128)S(1)}, u32[]{:S(2)}, u32[]{:S(2)}) collective-permute-start(f32[80,1152]{1,0:T(8,128)S(1)} %get-tuple-element.46.refs_1_), channel_id=1, source_target_pairs={{0,1},{1,0},{2,3},{3,2},{4,5},{5,4},{6,7},{7,6},{8,9},{9,8},{10,11... | collective-permute-start | bytes 1105928 | tf_op jit(solution)/shard_map/ppermute | solution.py:276
  31.2 1.8 %collective-permute-start.10 = (f32[80,1152]{1,0:T(8,128)S(1)}, f32[80,1152]{1,0:T(8,128)S(1)}, u32[]{:S(2)}, u32[]{:S(2)}) collective-permute-start(f32[80,1152]{1,0:T(8,128)S(1)} %get-tuple-element.43.refs_0_), channel_id=1, source_target_pairs={{0,1},{1,0},{2,3},{3,2},{4,5},{5,4},{6,7},{7,6},{8,9},{9,8},{10,11... | collective-permute-start | bytes 1105928 | tf_op jit(solution)/shard_map/ppermute | solution.py:276
  34.4 6.5 %collective-permute-start.12 = (bf16[20,1792]{1,0:T(8,128)(2,1)S(1)}, bf16[20,1792]{1,0:T(8,128)(2,1)S(1)}, u32[]{:S(2)}, u32[]{:S(2)}) collective-permute-start(bf16[20,1792]{1,0:T(8,128)(2,1)S(1)} %get-tuple-element.48), channel_id=1, source_target_pairs={{0,6},{1,7},{2,4},{3,5},{4,2},{5,3},{6,0},{7,1},{8,14},{9,15},{10,... | collective-permute-start | bytes 215048 | tf_op jit(solution)/shard_map/ppermute | solution.py:287
  36.9 6.3 %collective-permute-start.13 = (bf16[20,1792]{1,0:T(8,128)(2,1)S(1)}, bf16[20,1792]{1,0:T(8,128)(2,1)S(1)}, u32[]{:S(2)}, u32[]{:S(2)}) collective-permute-start(bf16[20,1792]{1,0:T(8,128)(2,1)S(1)} %get-tuple-element.49), channel_id=1, source_target_pairs={{0,4},{1,3},{2,6},{3,1},{4,0},{5,7},{6,2},{7,5},{8,12},{9,11},{10,... | collective-permute-start | bytes 215048 | tf_op jit(solution)/shard_map/ppermute | solution.py:287
  37.4 5.9 %collective-permute-start.14 = (bf16[20,1792]{1,0:T(8,128)(2,1)S(1)}, bf16[20,1792]{1,0:T(8,128)(2,1)S(1)}, u32[]{:S(2)}, u32[]{:S(2)}) collective-permute-start(bf16[20,1792]{1,0:T(8,128)(2,1)S(1)} %get-tuple-element.50), channel_id=1, source_target_pairs={{0,2},{1,5},{2,0},{3,7},{4,6},{5,1},{6,4},{7,3},{8,10},{9,13},{10,... | collective-permute-start | bytes 215048 | tf_op jit(solution)/shard_map/ppermute | solution.py:287
  37.9 6.9 %collective-permute-start.16 = (bf16[20,1792]{1,0:T(8,128)(2,1)S(1)}, bf16[20,1792]{1,0:T(8,128)(2,1)S(1)}, u32[]{:S(2)}, u32[]{:S(2)}) collective-permute-start(bf16[20,1792]{1,0:T(8,128)(2,1)S(1)} %get-tuple-element.55), channel_id=1, source_target_pairs={{0,6},{1,7},{2,4},{3,5},{4,2},{5,3},{6,0},{7,1},{8,14},{9,15},{10,... | collective-permute-start | bytes 215048 | tf_op jit(solution)/shard_map/ppermute | solution.py:287
  40.4 5.2 %collective-permute-start.17 = (bf16[20,1792]{1,0:T(8,128)(2,1)S(1)}, bf16[20,1792]{1,0:T(8,128)(2,1)S(1)}, u32[]{:S(2)}, u32[]{:S(2)}) collective-permute-start(bf16[20,1792]{1,0:T(8,128)(2,1)S(1)} %get-tuple-element.56), channel_id=1, source_target_pairs={{0,4},{1,3},{2,6},{3,1},{4,0},{5,7},{6,2},{7,5},{8,12},{9,11},{10,... | collective-permute-start | bytes 215048 | tf_op jit(solution)/shard_map/ppermute | solution.py:287
  40.9 4.7 %collective-permute-start.18 = (bf16[20,1792]{1,0:T(8,128)(2,1)S(1)}, bf16[20,1792]{1,0:T(8,128)(2,1)S(1)}, u32[]{:S(2)}, u32[]{:S(2)}) collective-permute-start(bf16[20,1792]{1,0:T(8,128)(2,1)S(1)} %get-tuple-element.57), channel_id=1, source_target_pairs={{0,2},{1,5},{2,0},{3,7},{4,6},{5,1},{6,4},{7,3},{8,10},{9,13},{10,... | collective-permute-start | bytes 215048 | tf_op jit(solution)/shard_map/ppermute | solution.py:287
  43.5 8.6 %collective-permute-start.15 = (bf16[20,896]{1,0:T(8,128)(2,1)S(1)}, bf16[20,896]{1,0:T(8,128)(2,1)S(1)}, u32[]{:S(2)}, u32[]{:S(2)}) collective-permute-start(bf16[20,896]{1,0:T(8,128)(2,1)S(1)} %get-tuple-element.52), channel_id=1, source_target_pairs={{0,8},{2,10},{4,12},{6,14},{8,0},{10,2},{12,4},{14,6},{16,24},{18,... | collective-permute-start | bytes 107528 | tf_op jit(solution)/shard_map/ppermute | solution.py:280
  45.8 6.5 %collective-permute-start.19 = (bf16[20,896]{1,0:T(8,128)(2,1)S(1)}, bf16[20,896]{1,0:T(8,128)(2,1)S(1)}, u32[]{:S(2)}, u32[]{:S(2)}) collective-permute-start(bf16[20,896]{1,0:T(8,128)(2,1)S(1)} %get-tuple-element.58), channel_id=1, source_target_pairs={{0,16},{2,18},{4,20},{6,22},{8,24},{10,26},{12,28},{14,30},{16,0},... | collective-permute-start | bytes 107528 | tf_op jit(solution)/shard_map/ppermute | solution.py:280
  48.1 5.8 %collective-permute-start.20 = (bf16[20,896]{1,0:T(8,128)(2,1)S(1)}, bf16[20,896]{1,0:T(8,128)(2,1)S(1)}, u32[]{:S(2)}, u32[]{:S(2)}) collective-permute-start(bf16[20,896]{1,0:T(8,128)(2,1)S(1)} %get-tuple-element.59), channel_id=1, source_target_pairs={{0,24},{2,26},{4,28},{6,30},{8,16},{10,18},{12,20},{14,22},{16,8},... | collective-permute-start | bytes 107528 | tf_op jit(solution)/shard_map/ppermute | solution.py:280
  52.2 1.9 %collective-permute-start.21 = (bf16[16,1792]{1,0:T(8,128)(2,1)S(1)}, bf16[16,1792]{1,0:T(8,128)(2,1)S(1)}, u32[]{:S(2)}, u32[]{:S(2)}) collective-permute-start(bf16[16,1792]{1,0:T(8,128)(2,1)S(1)} %get-tuple-element.67), channel_id=1, source_target_pairs={{0,1},{1,0},{2,3},{3,2},{4,5},{5,4},{6,7},{7,6},{8,9},{9,8},{10,11... | collective-permute-start | bytes 172040 | tf_op jit(solution)/shard_map/ppermute | solution.py:276
  53.9 1.5 %copy-start.3 = (f32[32,128]{1,0:T(8,128)S(1)}, f32[32,128]{1,0:T(8,128)}, u32[]{:S(2)}) copy-start(f32[32,128]{1,0:T(8,128)} %get-tuple-element.38.hot_ref) | copy-start | bytes 49156
  54.1 1.3 %collective-permute-start.22 = (bf16[16,1792]{1,0:T(8,128)(2,1)S(1)}, bf16[16,1792]{1,0:T(8,128)(2,1)S(1)}, u32[]{:S(2)}, u32[]{:S(2)}) collective-permute-start(bf16[16,1792]{1,0:T(8,128)(2,1)S(1)} %get-tuple-element.68), channel_id=1, source_target_pairs={{0,1},{1,0},{2,3},{3,2},{4,5},{5,4},{6,7},{7,6},{8,9},{9,8},{10,11... | collective-permute-start | bytes 172040 | tf_op jit(solution)/shard_map/ppermute | solution.py:276
where the time goes:
time: 57 us; the launch traced here: 56.8 us
  starting transfers between devices  27.7 us (49%)
  waiting for transfers between devices  15.9 us (28%)
  Pallas kernels  11.5 us (20%)
  local copies, waits for them, and re-layouts  0.92 us (2%)
  between operations  0.8 us (1%)
    ppermute x12, starting transfers between devices, in_plane(): return lax.ppermute(array, ('expert', 'dp'), hop)  16.2 us
    ppermute x6, starting transfers between devices, along_z(): return lax.ppermute(array, 'expert', hop)  10.6 us
    pallas_call x11, Pallas kernels, call(): pl.pallas_call(kernel, out_shape=out_shape, in_specs=[vmem] * len(operand...  6.39 us
    ppermute x12, waiting for transfers between devices, in_plane(): return lax.ppermute(array, ('expert', 'dp'), hop)  5.97 us
    ppermute x6, waiting for transfers between devices, along_z(): return lax.ppermute(array, 'expert', hop)  5.83 us
    ppermute x5, waiting for transfers between devices, swap_cores(): return lax.ppermute(array, 'dp', [(r, r ^ 1) for r in range(CORES)])  4.1 us
    pallas_call x1, Pallas kernels, body(): pl.pallas_call(lambda *refs: gather_kernel(live, *refs), out_shape=[gathe...  2.6 us
    pallas_call x1, Pallas kernels, body(): pl.pallas_call(grads_kernel, out_shape=[like((half, width), BF16)] * 3 +...  2.51 us
  transfers between devices with their start and end apart: 23, of which 11 were waited for; matrix products, arithmetic and copies ran while one was open for 0% of the time, Pallas kernels for 10%

commit v1 on v0

--- a/solution.py
+++ b/solution.py
@@ -147,7 +147,7 @@
     sums, (gate_ref, up_ref), outs = refs[: 2 * GROUPS], refs[2 * GROUPS : 2 * GROUPS + 2], refs[2 * GROUPS + 2 :]
     parts, sides_ref = outs[:-1], outs[-1]
     width = gate_ref.shape[1]
-    rows = parts[0].shape[0] * GROUPS
+    rows = parts[0].shape[0] // FOLDS * GROUPS
     total = [sums[i][...] + sums[GROUPS + i][...] for i in range(GROUPS)]
     total = jnp.concatenate(total, axis=0)
     pre_gate, pre_up = total[:, :width], total[:, width : 2 * width]
@@ -167,11 +167,12 @@
     order = one_hot(((GROUPS - 1 - group) * SPLIT + k) * (rows // GROUPS) + row, SPLIT * rows)
     gate_side, up_side = dot(order, gate_side).astype(BF16), dot(order, up_side).astype(BF16)
     part = dot(gate_side, gate_ref[...], across) + dot(up_side, up_ref[...], across)
-    each = rows // GROUPS
+    each, fold = rows // GROUPS, parts[0].shape[1]
     for k in range(SPLIT):
         for group in range(GROUPS):
             start = (k * GROUPS + group) * each
-            parts[group * SPLIT + k][...] = part[start : start + each].astype(BF16)
+            folds = [part[start : start + each, f * fold : (f + 1) * fold] for f in range(FOLDS)]
+            parts[group * SPLIT + k][...] = jnp.concatenate(folds, axis=0).astype(BF16)
 
 
 def grads_kernel(*refs):
@@ -204,16 +205,18 @@
     for part in parts[1:]:
         total = total + part[...].astype(F32)
     total = total.astype(BF16)
-    rows, half = total.shape
-    fold = half // FOLDS
+    rows, fold = total.shape
+    blocks = fold // 128
     each = CORES * MOST
-    size = FOLDS * each
+    size = FOLDS * blocks * each
     row = iota((count * size, 1), 0)
-    d, part, at = row // size, lax.rem(row // each, FOLDS), lax.rem(row, each)
-    moved = jnp.zeros((count * size, fold), F32)
-    for f in range(FOLDS):
-        pick = one_hot(jnp.where(part == f, d * each + at, -1), rows)
-        moved = moved + dot(pick, total[:, f * fold : (f + 1) * fold])
+    d, part, at = row // size, lax.rem(row // (blocks * each), FOLDS), lax.rem(row, each)
+    block = lax.rem(row // each, blocks)
+    wanted = (part * count + d) * each + at
+    moved = jnp.zeros((count * size, 128), F32)
+    for c in range(blocks):
+        pick = one_hot(jnp.where(block == c, wanted, -1), rows)
+        moved = moved + dot(pick, total[:, c * 128 : (c + 1) * 128])
     for d in range(count):
         outs[d][...] = moved[d * size : (d + 1) * size].astype(BF16)
 
@@ -221,17 +224,16 @@
 def split_kernel(count, *refs):
     chunks, outs = refs[:count], refs[-CORES:]
     me = lax.axis_index("dp")
-    size, fold = chunks[0].shape
+    size = chunks[0].shape[0]
     stacked = jnp.concatenate([chunk[...].astype(F32) for chunk in chunks], axis=0).astype(BF16)
-    rows = len(chunks) * 8
+    rows = count * 8
     out = iota((CORES * rows, 1), 0)
     q, d, slot = out // rows, lax.rem(out, rows) // 8, lax.rem(out, 8)
-    for f in range(FOLDS):
-        wanted = d * size + (f * CORES + (q ^ me)) * MOST + slot
-        pick = one_hot(jnp.where(slot < MOST, wanted, -1), len(chunks) * size)
-        picked = dot(pick, stacked).astype(BF16)
+    first = jnp.where(slot < MOST, d * size + (q ^ me) * MOST + slot, -size)
+    for c in range(outs[0].shape[1] // 128):
+        picked = dot(one_hot(first + c * CORES * MOST, count * size), stacked).astype(BF16)
         for core in range(CORES):
-            outs[core][:, f * fold : (f + 1) * fold] = picked[core * rows : (core + 1) * rows]
+            outs[core][:, c * 128 : (c + 1) * 128] = picked[core * rows : (core + 1) * rows]
 
 
 def place_kernel(hot_ref, *refs):
@@ -340,7 +342,8 @@
     sided = call(
         sides_kernel,
         "sides_and_parts",
-        [like((rows // GROUPS, half), BF16)] * (GROUPS * SPLIT) + [like((total, 3 * width), BF16)],
+        [like((rows // GROUPS * FOLDS, fold), BF16)] * (GROUPS * SPLIT)
+        + [like((total, 3 * width), BF16)],
         [*mines, *others, gate_weight, up_weight],
         4 * total * half * width,
         4 * half * width,
@@ -365,7 +368,7 @@
         chunks = call(
             functools.partial(sum_kernel, planes),
             "sum_parts",
-            [like((FOLDS * CORES * MOST, fold), BF16)] * planes,
+            [like((half // 128 * CORES * MOST, 128), BF16)] * planes,
             parts[group],
         )
         first = group * planes

time: 57 us -> 56.8 us (level)
  Pallas kernels: 11.5 us -> 12.3 us
  waiting for transfers between devices: 15.9 us -> 15.2 us
    pallas_call x11, Pallas kernels: 6.39 us -> 7.17 us  [call(): pl.pallas_call(kernel, out_shape=out_shape, in_specs=[vmem] * len(operand...]
  transfers between devices with their start and end apart: 23 -> 23, of which waited for: 11 -> 13; matrix products, arithmetic and copies ran while one was open for 0% -> 0% of each run, Pallas kernels for 10% -> 12%
where the time goes in v1:
time: 56.8 us; the launch traced here: 56.7 us
  starting transfers between devices  27.4 us (48%)
  waiting for transfers between devices  15.2 us (27%)
  Pallas kernels  12.3 us (22%)
  local copies, waits for them, and re-layouts  0.92 us (2%)
  between operations  0.81 us (1%)
    ppermute x12, starting transfers between devices, in_plane(): return lax.ppermute(array, ('expert', 'dp'), hop)  16 us
    ppermute x6, starting transfers between devices, along_z(): return lax.ppermute(array, 'expert', hop)  10.6 us
    pallas_call x11, Pallas kernels, call(): pl.pallas_call(kernel, out_shape=out_shape, in_specs=[vmem] * len(operand...  7.17 us
    ppermute x6, waiting for transfers between devices, along_z(): return lax.ppermute(array, 'expert', hop)  5.62 us
    ppermute x12, waiting for transfers between devices, in_plane(): return lax.ppermute(array, ('expert', 'dp'), hop)  5.53 us
    ppermute x5, waiting for transfers between devices, swap_cores(): return lax.ppermute(array, 'dp', [(r, r ^ 1) for r in range(CORES)])  4.1 us
    pallas_call x1, Pallas kernels, body(): pl.pallas_call(lambda *refs: gather_kernel(live, *refs), out_shape=[gathe...  2.6 us
    pallas_call x1, Pallas kernels, body(): pl.pallas_call(grads_kernel, out_shape=[like((half, width), BF16)] * 3 +...  2.5 us
  transfers between devices with their start and end apart: 23, of which 13 were waited for; matrix products, arithmetic and copies ran while one was open for 0% of the time, Pallas kernels for 12%

profile of v1, /device:TPU:0, one launch (start us, length us, event | category | flops | bytes accessed | tf_op | source)
XLA Modules:
  0.0 56.7 jit_solution(14602299890807715546)
XLA Ops:
  0.6 2.6 %gather_rows.1 = (bf16[40,1792]{1,0:T(8,128)(2,1)}, bf16[40,1792]{1,0:T(8,128)(2,1)}, f32[32,128]{1,0:T(8,128)}) custom-call(s32[8,128]{1,0:T(8,128)} %bitcast.3, s32[8,128]{1,0:T(8,128)} %bitcast.4, f32[8,128]{1,0:T(8,128)} %bitcast.5, bf16[128,3584]{1,0:T(8,128)(2,1)} %refs_3_.1, bf16[128,3584]{1,0:T(8,128)(2,1)} %refs_4_.4), custom_call_target="tpu_custom_call" | custom-call | tf_op jit(solution)/shard_map/gather_rows/pallas_call | solution.py:292
  3.2 0.5 collective-permute-start
  3.8 1.2 %collective-permute-done.refs_1_ = bf16[40,1792]{1,0:T(8,128)(2,1)S(1)} collective-permute-done((bf16[40,1792]{1,0:T(8,128)(2,1)}, bf16[40,1792]{1,0:T(8,128)(2,1)S(1)}, u32[]{:S(2)}, u32[]{:S(2)}) %collective-permute-start) | collective-permute-done | bytes 143392 | tf_op jit(solution)/shard_map/ppermute | solution.py:278
  5.0 0.9 %copy-done.4 = bf16[40,1792]{1,0:T(8,128)(2,1)S(1)} copy-done((bf16[40,1792]{1,0:T(8,128)(2,1)S(1)}, bf16[40,1792]{1,0:T(8,128)(2,1)}, u32[]{:S(2)}) %copy-start.4) | copy-done | bytes 143384
  5.9 0.4 chunk_rows.1
  6.3 3.0 %collective-permute-start.6 = (bf16[40,896]{1,0:T(8,128)(2,1)S(1)}, bf16[40,896]{1,0:T(8,128)(2,1)S(1)}, u32[]{:S(2)}, u32[]{:S(2)}) collective-permute-start(bf16[40,896]{1,0:T(8,128)(2,1)S(1)} %get-tuple-element.45), channel_id=1, source_target_pairs={{0,8},{2,10},{4,12},{6,14},{8,0},{10,2},{12,4},{14,6},{16,24},{18,... | collective-permute-start | bytes 215048 | tf_op jit(solution)/shard_map/ppermute | solution.py:282
  9.3 2.6 %collective-permute-start.1 = (bf16[40,896]{1,0:T(8,128)(2,1)S(1)}, bf16[40,896]{1,0:T(8,128)(2,1)S(1)}, u32[]{:S(2)}, u32[]{:S(2)}) collective-permute-start(bf16[40,896]{1,0:T(8,128)(2,1)S(1)} %get-tuple-element.41), channel_id=1, source_target_pairs={{0,16},{2,18},{4,20},{6,22},{8,24},{10,26},{12,28},{14,30},{16,0},... | collective-permute-start | bytes 215048 | tf_op jit(solution)/shard_map/ppermute | solution.py:282
  11.9 0.0 collective-permute-start.2
  11.9 0.0 collective-permute-done.6.refs_1_
  11.9 0.2 merge_rows.3.refs_0_
  12.1 1.8 %collective-permute-start.7 = (bf16[40,1792]{1,0:T(8,128)(2,1)S(1)}, bf16[40,1792]{1,0:T(8,128)(2,1)S(1)}, u32[]{:S(2)}, u32[]{:S(2)}) collective-permute-start(bf16[40,1792]{1,0:T(8,128)(2,1)S(1)} %merge_rows.3.refs_0_), channel_id=1, source_target_pairs={{0,2},{1,5},{2,0},{3,7},{4,6},{5,1},{6,4},{7,3},{8,10},{9,13},{10,... | collective-permute-start | bytes 430088 | tf_op jit(solution)/shard_map/ppermute | solution.py:289
  13.9 3.3 %collective-permute-done.1.refs_0_ = bf16[40,896]{1,0:T(8,128)(2,1)S(1)} collective-permute-done((bf16[40,896]{1,0:T(8,128)(2,1)S(1)}, bf16[40,896]{1,0:T(8,128)(2,1)S(1)}, u32[]{:S(2)}, u32[]{:S(2)}) %collective-permute-start.1) | collective-permute-done | bytes 71712 | tf_op jit(solution)/shard_map/ppermute | solution.py:282
  17.2 0.9 %collective-permute-done.2.refs_1_ = bf16[40,896]{1,0:T(8,128)(2,1)S(1)} collective-permute-done((bf16[40,896]{1,0:T(8,128)(2,1)S(1)}, bf16[40,896]{1,0:T(8,128)(2,1)S(1)}, u32[]{:S(2)}, u32[]{:S(2)}) %collective-permute-start.2) | collective-permute-done | bytes 71712 | tf_op jit(solution)/shard_map/ppermute | solution.py:282
  18.1 0.2 merge_rows.2.refs_0_
  18.3 1.6 %collective-permute-start.3 = (bf16[40,1792]{1,0:T(8,128)(2,1)S(1)}, bf16[40,1792]{1,0:T(8,128)(2,1)S(1)}, u32[]{:S(2)}, u32[]{:S(2)}) collective-permute-start(bf16[40,1792]{1,0:T(8,128)(2,1)S(1)} %merge_rows.2.refs_0_), channel_id=1, source_target_pairs={{0,2},{1,5},{2,0},{3,7},{4,6},{5,1},{6,4},{7,3},{8,10},{9,13},{10,... | collective-permute-start | bytes 430088 | tf_op jit(solution)/shard_map/ppermute | solution.py:289
  19.9 1.5 %collective-permute-start.8 = (bf16[40,1792]{1,0:T(8,128)(2,1)S(1)}, bf16[40,1792]{1,0:T(8,128)(2,1)S(1)}, u32[]{:S(2)}, u32[]{:S(2)}) collective-permute-start(bf16[40,1792]{1,0:T(8,128)(2,1)S(1)} %merge_rows.3.refs_0_), channel_id=1, source_target_pairs={{0,4},{1,3},{2,6},{3,1},{4,0},{5,7},{6,2},{7,5},{8,12},{9,11},{10,... | collective-permute-start | bytes 430088 | tf_op jit(solution)/shard_map/ppermute | solution.py:289
  21.4 0.0 collective-permute-done.7.refs_1_
  21.4 0.5 collective-permute-start.9
  21.9 1.5 %collective-permute-start.4 = (bf16[40,1792]{1,0:T(8,128)(2,1)S(1)}, bf16[40,1792]{1,0:T(8,128)(2,1)S(1)}, u32[]{:S(2)}, u32[]{:S(2)}) collective-permute-start(bf16[40,1792]{1,0:T(8,128)(2,1)S(1)} %merge_rows.2.refs_0_), channel_id=1, source_target_pairs={{0,4},{1,3},{2,6},{3,1},{4,0},{5,7},{6,2},{7,5},{8,12},{9,11},{10,... | collective-permute-start | bytes 430088 | tf_op jit(solution)/shard_map/ppermute | solution.py:289
  23.4 1.6 %collective-permute-done.3.refs_1_ = bf16[40,1792]{1,0:T(8,128)(2,1)S(1)} collective-permute-done((bf16[40,1792]{1,0:T(8,128)(2,1)S(1)}, bf16[40,1792]{1,0:T(8,128)(2,1)S(1)}, u32[]{:S(2)}, u32[]{:S(2)}) %collective-permute-start.3) | collective-permute-done | bytes 143392 | tf_op jit(solution)/shard_map/ppermute | solution.py:289
  25.1 1.5 %collective-permute-start.5 = (bf16[40,1792]{1,0:T(8,128)(2,1)S(1)}, bf16[40,1792]{1,0:T(8,128)(2,1)S(1)}, u32[]{:S(2)}, u32[]{:S(2)}) collective-permute-start(bf16[40,1792]{1,0:T(8,128)(2,1)S(1)} %collective-permute-done.3.refs_1_), channel_id=1, source_target_pairs={{0,4},{1,3},{2,6},{3,1},{4,0},{5,7},{6,2},{7,5},{8,12},{9,11},{10,... | collective-permute-start | bytes 430088 | tf_op jit(solution)/shard_map/ppermute | solution.py:289
  26.6 0.0 collective-permute-done.8.refs_2_
  26.6 0.0 collective-permute-done.9.refs_3_
  26.6 0.0 copy-done
  26.6 0.0 copy-done.1
  26.6 0.0 copy-done.2
  26.6 1.0 %partial_products.3 = (f32[80,1152]{1,0:T(8,128)S(1)}, bf16[80,1792]{1,0:T(8,128)(2,1)S(1)}, bf16[80,1792]{1,0:T(8,128)(2,1)S(1)}) custom-call(bf16[40,1792]{1,0:T(8,128)(2,1)S(1)} %merge_rows.3.refs_0_, bf16[40,1792]{1,0:T(8,128)(2,1)S(1)} %collective-permute-done.7.refs_1_, bf16[40,1792]{1,0:T(8,128)(2,1)S(1)} %collective-permute-done.8.refs_2_, ...), custom_call_target="tpu_custom_call" | custom-call | flops 330301440 | bytes 4128768 | tf_op jit(solution)/shard_map/partial_products/pallas_call | solution.py:267
  27.6 0.1 collective-permute-start.11
  27.7 0.3 collective-permute-done.4.refs_2_
  28.0 2.1 %collective-permute-done.5.refs_3_ = bf16[40,1792]{1,0:T(8,128)(2,1)S(1)} collective-permute-done((bf16[40,1792]{1,0:T(8,128)(2,1)S(1)}, bf16[40,1792]{1,0:T(8,128)(2,1)S(1)}, u32[]{:S(2)}, u32[]{:S(2)}) %collective-permute-start.5) | collective-permute-done | bytes 143392 | tf_op jit(solution)/shard_map/ppermute | solution.py:289
  30.2 1.0 %partial_products.2 = (f32[80,1152]{1,0:T(8,128)S(1)}, bf16[80,1792]{1,0:T(8,128)(2,1)S(1)}, bf16[80,1792]{1,0:T(8,128)(2,1)S(1)}) custom-call(bf16[40,1792]{1,0:T(8,128)(2,1)S(1)} %merge_rows.2.refs_0_, bf16[40,1792]{1,0:T(8,128)(2,1)S(1)} %collective-permute-done.3.refs_1_, bf16[40,1792]{1,0:T(8,128)(2,1)S(1)} %collective-permute-done.4.refs_2_, ...), custom_call_target="tpu_custom_call" | custom-call | flops 330301440 | bytes 4128768 | tf_op jit(solution)/shard_map/partial_products/pallas_call | solution.py:267
  31.2 0.1 collective-permute-start.10
  31.3 0.0 collective-permute-done.11.refs_3_
  31.3 1.7 %collective-permute-done.10.refs_2_ = f32[80,1152]{1,0:T(8,128)S(1)} collective-permute-done((f32[80,1152]{1,0:T(8,128)S(1)}, f32[80,1152]{1,0:T(8,128)S(1)}, u32[]{:S(2)}, u32[]{:S(2)}) %collective-permute-start.10) | collective-permute-done | bytes 368672 | tf_op jit(solution)/shard_map/ppermute | solution.py:278
  32.9 1.4 %sides_and_parts.1 = (bf16[40,896]{1,0:T(8,128)(2,1)S(1)}, bf16[40,896]{1,0:T(8,128)(2,1)S(1)}, bf16[40,896]{1,0:T(8,128)(2,1)S(1)}, bf16[40,896]{1,0:T(8,128)(2...) custom-call(f32[80,1152]{1,0:T(8,128)S(1)} %get-tuple-element.43.ref, ...), custom_call_target="tpu_custom_call" | custom-call | flops 440401920 | bytes 2752512 | tf_op jit(solution)/shard_map/sides_and_parts/pallas_call | solution.py:267
  34.4 2.5 %collective-permute-start.12 = (bf16[40,896]{1,0:T(8,128)(2,1)S(1)}, bf16[40,896]{1,0:T(8,128)(2,1)S(1)}, u32[]{:S(2)}, u32[]{:S(2)}) collective-permute-start(bf16[40,896]{1,0:T(8,128)(2,1)S(1)} %get-tuple-element.48), channel_id=1, source_target_pairs={{0,6},{1,7},{2,4},{3,5},{4,2},{5,3},{6,0},{7,1},{8,14},{9,15},{10,... | collective-permute-start | bytes 215048 | tf_op jit(solution)/shard_map/ppermute | solution.py:289
  36.9 0.5 collective-permute-start.13
  37.4 0.5 collective-permute-start.14
  37.9 2.5 %collective-permute-start.16 = (bf16[40,896]{1,0:T(8,128)(2,1)S(1)}, bf16[40,896]{1,0:T(8,128)(2,1)S(1)}, u32[]{:S(2)}, u32[]{:S(2)}) collective-permute-start(bf16[40,896]{1,0:T(8,128)(2,1)S(1)} %get-tuple-element.55), channel_id=1, source_target_pairs={{0,6},{1,7},{2,4},{3,5},{4,2},{5,3},{6,0},{7,1},{8,14},{9,15},{10,... | collective-permute-start | bytes 215048 | tf_op jit(solution)/shard_map/ppermute | solution.py:289
  40.4 0.5 collective-permute-start.17
  40.9 0.0 collective-permute-done.12.refs_1_
  40.9 1.1 %collective-permute-start.18 = (bf16[40,896]{1,0:T(8,128)(2,1)S(1)}, bf16[40,896]{1,0:T(8,128)(2,1)S(1)}, u32[]{:S(2)}, u32[]{:S(2)}) collective-permute-start(bf16[40,896]{1,0:T(8,128)(2,1)S(1)} %get-tuple-element.57), channel_id=1, source_target_pairs={{0,2},{1,5},{2,0},{3,7},{4,6},{5,1},{6,4},{7,3},{8,10},{9,13},{10,... | collective-permute-start | bytes 215048 | tf_op jit(solution)/shard_map/ppermute | solution.py:289
  41.9 0.2 collective-permute-done.13.refs_2_
  42.2 0.3 collective-permute-done.14.refs_3_
  42.5 0.5 sum_parts.2
  43.0 1.3 %collective-permute-start.15 = (bf16[140,128]{1,0:T(8,128)(2,1)S(1)}, bf16[140,128]{1,0:T(8,128)(2,1)S(1)}, u32[]{:S(2)}, u32[]{:S(2)}) collective-permute-start(bf16[140,128]{1,0:T(8,128)(2,1)S(1)} %get-tuple-element.52), channel_id=1, source_target_pairs={{0,8},{2,10},{4,12},{6,14},{8,0},{10,2},{12,4},{14,6},{16,24},{18,... | collective-permute-start | bytes 107528 | tf_op jit(solution)/shard_map/ppermute | solution.py:282
  44.3 0.0 collective-permute-done.16.refs_1_
  44.3 0.7 %collective-permute-done.17.refs_2_ = bf16[40,896]{1,0:T(8,128)(2,1)S(1)} collective-permute-done((bf16[40,896]{1,0:T(8,128)(2,1)S(1)}, bf16[40,896]{1,0:T(8,128)(2,1)S(1)}, u32[]{:S(2)}, u32[]{:S(2)}) %collective-permute-start.17) | collective-permute-done | bytes 71712 | tf_op jit(solution)/shard_map/ppermute | solution.py:289
  45.0 0.2 collective-permute-done.18.refs_3_
  45.2 0.5 sum_parts.3
  45.7 2.2 %collective-permute-start.19 = (bf16[140,128]{1,0:T(8,128)(2,1)S(1)}, bf16[140,128]{1,0:T(8,128)(2,1)S(1)}, u32[]{:S(2)}, u32[]{:S(2)}) collective-permute-start(bf16[140,128]{1,0:T(8,128)(2,1)S(1)} %get-tuple-element.58), channel_id=1, source_target_pairs={{0,16},{2,18},{4,20},{6,22},{8,24},{10,26},{12,28},{14,30},{16,0},... | collective-permute-start | bytes 107528 | tf_op jit(solution)/shard_map/ppermute | solution.py:282
  47.9 1.5 %collective-permute-start.20 = (bf16[140,128]{1,0:T(8,128)(2,1)S(1)}, bf16[140,128]{1,0:T(8,128)(2,1)S(1)}, u32[]{:S(2)}, u32[]{:S(2)}) collective-permute-start(bf16[140,128]{1,0:T(8,128)(2,1)S(1)} %get-tuple-element.59), channel_id=1, source_target_pairs={{0,24},{2,26},{4,28},{6,30},{8,16},{10,18},{12,20},{14,22},{16,8},... | collective-permute-start | bytes 107528 | tf_op jit(solution)/shard_map/ppermute | solution.py:282
  49.4 2.5 %weight_grads.1 = (bf16[1792,384]{1,0:T(8,128)(2,1)}, bf16[1792,384]{1,0:T(8,128)(2,1)}, bf16[1792,384]{1,0:T(8,128)(2,1)}, f32[8,128]{1,0:T(8,128)S(1)}) custom-call(bf16[80,1792]{1,0:T(8,128)(2,1)S(1)} %get-tuple-element.60.refs_0_, bf16[80,1792]{1,0:T(8,128)(2,1)S(1)} %get-tuple-element.61.refs_1_, bf16[80,1792]{1,0:T(8,128)(2,1)S(1)} %get-tuple-element.62.refs_2_, ...), custom_call_target="tpu_custom_call" | custom-call | flops 660602880 | bytes 5275648 | tf_op jit(solution)/shard_map/weight_grads/pallas_call | solution.py:355
  51.9 0.0 collective-permute-done.15.refs_1_
  51.9 0.3 split_rows.2
  52.2 0.1 collective-permute-start.21
  52.3 0.0 collective-permute-done.19.refs_0_
  52.3 1.4 %collective-permute-done.20.refs_1_ = bf16[140,128]{1,0:T(8,128)(2,1)S(1)} collective-permute-done((bf16[140,128]{1,0:T(8,128)(2,1)S(1)}, bf16[140,128]{1,0:T(8,128)(2,1)S(1)}, u32[]{:S(2)}, u32[]{:S(2)}) %collective-permute-start.20) | collective-permute-done | bytes 35872 | tf_op jit(solution)/shard_map/ppermute | solution.py:282
  53.7 0.3 split_rows.3
  54.0 0.1 collective-permute-start.22
  54.1 0.0 collective-permute-done.21.refs_2_
  54.1 1.2 %collective-permute-done.22.refs_3_ = bf16[16,1792]{1,0:T(8,128)(2,1)S(1)} collective-permute-done((bf16[16,1792]{1,0:T(8,128)(2,1)S(1)}, bf16[16,1792]{1,0:T(8,128)(2,1)S(1)}, u32[]{:S(2)}, u32[]{:S(2)}) %collective-permute-start.22) | collective-permute-done | bytes 57376 | tf_op jit(solution)/shard_map/ppermute | solution.py:278
  55.3 0.0 copy-done.3
  55.3 1.3 %place_rows.1 = bf16[128,3584]{1,0:T(8,128)(2,1)} custom-call(f32[32,128]{1,0:T(8,128)S(1)} %copy-done.3, bf16[16,1792]{1,0:T(8,128)(2,1)S(1)} %get-tuple-element.53.refs_0_, bf16[16,1792]{1,0:T(8,128)(2,1)S(1)} %get-tuple-element.66.refs_1_, bf16[16,1792]{1,0:T(8,128)(2,1)S(1)} %collective-permute-done.21.refs_2_, ...), custom_call_target="tpu_custom_call" | custom-call | tf_op jit(solution)/shard_map/place_rows/pallas_call | solution.py:267
  (5 shorter events, 0.0 us)
Async XLA Ops:
  3.2 1.7 %collective-permute-start = (bf16[40,1792]{1,0:T(8,128)(2,1)}, bf16[40,1792]{1,0:T(8,128)(2,1)S(1)}, u32[]{:S(2)}, u32[]{:S(2)}) collective-permute-start(bf16[40,1792]{1,0:T(8,128)(2,1)} %get-tuple-element.40), channel_id=1, source_target_pairs={{0,1},{1,0},{2,3},{3,2},{4,5},{5,4},{6,7},{7,6},{8,9},{9,8},{10,11... | collective-permute-start | bytes 430088 | tf_op jit(solution)/shard_map/ppermute | solution.py:278
  5.0 0.9 %copy-start.4 = (bf16[40,1792]{1,0:T(8,128)(2,1)S(1)}, bf16[40,1792]{1,0:T(8,128)(2,1)}, u32[]{:S(2)}) copy-start(bf16[40,1792]{1,0:T(8,128)(2,1)} %get-tuple-element.39.refs_0_) | copy-start | bytes 430084
  5.9 20.7 %copy-start = (bf16[1792,384]{1,0:T(8,128)(2,1)S(1)}, bf16[1792,384]{1,0:T(8,128)(2,1)}, u32[]{:S(2)}) copy-start(bf16[1792,384]{1,0:T(8,128)(2,1)} %refs_4_.7) | copy-start | bytes 4128772
  5.9 20.7 %copy-start.1 = (bf16[1792,384]{1,0:T(8,128)(2,1)S(1)}, bf16[1792,384]{1,0:T(8,128)(2,1)}, u32[]{:S(2)}) copy-start(bf16[1792,384]{1,0:T(8,128)(2,1)} %refs_5_.5) | copy-start | bytes 4128772
  5.9 20.7 %copy-start.2 = (bf16[1792,384]{1,0:T(8,128)(2,1)S(1)}, bf16[1792,384]{1,0:T(8,128)(2,1)}, u32[]{:S(2)}) copy-start(bf16[1792,384]{1,0:T(8,128)(2,1)} %refs_6_.3) | copy-start | bytes 4128772
  6.3 5.6 %collective-permute-start.6 = (bf16[40,896]{1,0:T(8,128)(2,1)S(1)}, bf16[40,896]{1,0:T(8,128)(2,1)S(1)}, u32[]{:S(2)}, u32[]{:S(2)}) collective-permute-start(bf16[40,896]{1,0:T(8,128)(2,1)S(1)} %get-tuple-element.45), channel_id=1, source_target_pairs={{0,8},{2,10},{4,12},{6,14},{8,0},{10,2},{12,4},{14,6},{16,24},{18,... | collective-permute-start | bytes 215048 | tf_op jit(solution)/shard_map/ppermute | solution.py:282
  9.3 7.9 %collective-permute-start.1 = (bf16[40,896]{1,0:T(8,128)(2,1)S(1)}, bf16[40,896]{1,0:T(8,128)(2,1)S(1)}, u32[]{:S(2)}, u32[]{:S(2)}) collective-permute-start(bf16[40,896]{1,0:T(8,128)(2,1)S(1)} %get-tuple-element.41), channel_id=1, source_target_pairs={{0,16},{2,18},{4,20},{6,22},{8,24},{10,26},{12,28},{14,30},{16,0},... | collective-permute-start | bytes 215048 | tf_op jit(solution)/shard_map/ppermute | solution.py:282
  11.9 6.2 %collective-permute-start.2 = (bf16[40,896]{1,0:T(8,128)(2,1)S(1)}, bf16[40,896]{1,0:T(8,128)(2,1)S(1)}, u32[]{:S(2)}, u32[]{:S(2)}) collective-permute-start(bf16[40,896]{1,0:T(8,128)(2,1)S(1)} %get-tuple-element.42), channel_id=1, source_target_pairs={{0,24},{2,26},{4,28},{6,30},{8,16},{10,18},{12,20},{14,22},{16,8},... | collective-permute-start | bytes 215048 | tf_op jit(solution)/shard_map/ppermute | solution.py:282
  12.1 9.3 %collective-permute-start.7 = (bf16[40,1792]{1,0:T(8,128)(2,1)S(1)}, bf16[40,1792]{1,0:T(8,128)(2,1)S(1)}, u32[]{:S(2)}, u32[]{:S(2)}) collective-permute-start(bf16[40,1792]{1,0:T(8,128)(2,1)S(1)} %merge_rows.3.refs_0_), channel_id=1, source_target_pairs={{0,2},{1,5},{2,0},{3,7},{4,6},{5,1},{6,4},{7,3},{8,10},{9,13},{10,... | collective-permute-start | bytes 430088 | tf_op jit(solution)/shard_map/ppermute | solution.py:289
  18.3 6.8 %collective-permute-start.3 = (bf16[40,1792]{1,0:T(8,128)(2,1)S(1)}, bf16[40,1792]{1,0:T(8,128)(2,1)S(1)}, u32[]{:S(2)}, u32[]{:S(2)}) collective-permute-start(bf16[40,1792]{1,0:T(8,128)(2,1)S(1)} %merge_rows.2.refs_0_), channel_id=1, source_target_pairs={{0,2},{1,5},{2,0},{3,7},{4,6},{5,1},{6,4},{7,3},{8,10},{9,13},{10,... | collective-permute-start | bytes 430088 | tf_op jit(solution)/shard_map/ppermute | solution.py:289
  19.9 6.7 %collective-permute-start.8 = (bf16[40,1792]{1,0:T(8,128)(2,1)S(1)}, bf16[40,1792]{1,0:T(8,128)(2,1)S(1)}, u32[]{:S(2)}, u32[]{:S(2)}) collective-permute-start(bf16[40,1792]{1,0:T(8,128)(2,1)S(1)} %merge_rows.3.refs_0_), channel_id=1, source_target_pairs={{0,4},{1,3},{2,6},{3,1},{4,0},{5,7},{6,2},{7,5},{8,12},{9,11},{10,... | collective-permute-start | bytes 430088 | tf_op jit(solution)/shard_map/ppermute | solution.py:289
  21.4 5.2 %collective-permute-start.9 = (bf16[40,1792]{1,0:T(8,128)(2,1)S(1)}, bf16[40,1792]{1,0:T(8,128)(2,1)S(1)}, u32[]{:S(2)}, u32[]{:S(2)}) collective-permute-start(bf16[40,1792]{1,0:T(8,128)(2,1)S(1)} %collective-permute-done.7.refs_1_), channel_id=1, source_target_pairs={{0,4},{1,3},{2,6},{3,1},{4,0},{5,7},{6,2},{7,5},{8,12},{9,11},{10,... | collective-permute-start | bytes 430088 | tf_op jit(solution)/shard_map/ppermute | solution.py:289
  21.9 6.1 %collective-permute-start.4 = (bf16[40,1792]{1,0:T(8,128)(2,1)S(1)}, bf16[40,1792]{1,0:T(8,128)(2,1)S(1)}, u32[]{:S(2)}, u32[]{:S(2)}) collective-permute-start(bf16[40,1792]{1,0:T(8,128)(2,1)S(1)} %merge_rows.2.refs_0_), channel_id=1, source_target_pairs={{0,4},{1,3},{2,6},{3,1},{4,0},{5,7},{6,2},{7,5},{8,12},{9,11},{10,... | collective-permute-start | bytes 430088 | tf_op jit(solution)/shard_map/ppermute | solution.py:289
  25.1 5.1 %collective-permute-start.5 = (bf16[40,1792]{1,0:T(8,128)(2,1)S(1)}, bf16[40,1792]{1,0:T(8,128)(2,1)S(1)}, u32[]{:S(2)}, u32[]{:S(2)}) collective-permute-start(bf16[40,1792]{1,0:T(8,128)(2,1)S(1)} %collective-permute-done.3.refs_1_), channel_id=1, source_target_pairs={{0,4},{1,3},{2,6},{3,1},{4,0},{5,7},{6,2},{7,5},{8,12},{9,11},{10,... | collective-permute-start | bytes 430088 | tf_op jit(solution)/shard_map/ppermute | solution.py:289
  27.6 3.6 %collective-permute-start.11 = (f32[80,1152]{1,0:T(8,128)S(1)}, f32[80,1152]{1,0:T(8,128)S(1)}, u32[]{:S(2)}, u32[]{:S(2)}) collective-permute-start(f32[80,1152]{1,0:T(8,128)S(1)} %get-tuple-element.46.refs_1_), channel_id=1, source_target_pairs={{0,1},{1,0},{2,3},{3,2},{4,5},{5,4},{6,7},{7,6},{8,9},{9,8},{10,11... | collective-permute-start | bytes 1105928 | tf_op jit(solution)/shard_map/ppermute | solution.py:278
  31.2 1.8 %collective-permute-start.10 = (f32[80,1152]{1,0:T(8,128)S(1)}, f32[80,1152]{1,0:T(8,128)S(1)}, u32[]{:S(2)}, u32[]{:S(2)}) collective-permute-start(f32[80,1152]{1,0:T(8,128)S(1)} %get-tuple-element.43.refs_0_), channel_id=1, source_target_pairs={{0,1},{1,0},{2,3},{3,2},{4,5},{5,4},{6,7},{7,6},{8,9},{9,8},{10,11... | collective-permute-start | bytes 1105928 | tf_op jit(solution)/shard_map/ppermute | solution.py:278
  34.4 6.5 %collective-permute-start.12 = (bf16[40,896]{1,0:T(8,128)(2,1)S(1)}, bf16[40,896]{1,0:T(8,128)(2,1)S(1)}, u32[]{:S(2)}, u32[]{:S(2)}) collective-permute-start(bf16[40,896]{1,0:T(8,128)(2,1)S(1)} %get-tuple-element.48), channel_id=1, source_target_pairs={{0,6},{1,7},{2,4},{3,5},{4,2},{5,3},{6,0},{7,1},{8,14},{9,15},{10,... | collective-permute-start | bytes 215048 | tf_op jit(solution)/shard_map/ppermute | solution.py:289
  36.9 5.3 %collective-permute-start.13 = (bf16[40,896]{1,0:T(8,128)(2,1)S(1)}, bf16[40,896]{1,0:T(8,128)(2,1)S(1)}, u32[]{:S(2)}, u32[]{:S(2)}) collective-permute-start(bf16[40,896]{1,0:T(8,128)(2,1)S(1)} %get-tuple-element.49), channel_id=1, source_target_pairs={{0,4},{1,3},{2,6},{3,1},{4,0},{5,7},{6,2},{7,5},{8,12},{9,11},{10,... | collective-permute-start | bytes 215048 | tf_op jit(solution)/shard_map/ppermute | solution.py:289
  37.4 5.1 %collective-permute-start.14 = (bf16[40,896]{1,0:T(8,128)(2,1)S(1)}, bf16[40,896]{1,0:T(8,128)(2,1)S(1)}, u32[]{:S(2)}, u32[]{:S(2)}) collective-permute-start(bf16[40,896]{1,0:T(8,128)(2,1)S(1)} %get-tuple-element.50), channel_id=1, source_target_pairs={{0,2},{1,5},{2,0},{3,7},{4,6},{5,1},{6,4},{7,3},{8,10},{9,13},{10,... | collective-permute-start | bytes 215048 | tf_op jit(solution)/shard_map/ppermute | solution.py:289
  37.9 6.4 %collective-permute-start.16 = (bf16[40,896]{1,0:T(8,128)(2,1)S(1)}, bf16[40,896]{1,0:T(8,128)(2,1)S(1)}, u32[]{:S(2)}, u32[]{:S(2)}) collective-permute-start(bf16[40,896]{1,0:T(8,128)(2,1)S(1)} %get-tuple-element.55), channel_id=1, source_target_pairs={{0,6},{1,7},{2,4},{3,5},{4,2},{5,3},{6,0},{7,1},{8,14},{9,15},{10,... | collective-permute-start | bytes 215048 | tf_op jit(solution)/shard_map/ppermute | solution.py:289
  40.4 4.6 %collective-permute-start.17 = (bf16[40,896]{1,0:T(8,128)(2,1)S(1)}, bf16[40,896]{1,0:T(8,128)(2,1)S(1)}, u32[]{:S(2)}, u32[]{:S(2)}) collective-permute-start(bf16[40,896]{1,0:T(8,128)(2,1)S(1)} %get-tuple-element.56), channel_id=1, source_target_pairs={{0,4},{1,3},{2,6},{3,1},{4,0},{5,7},{6,2},{7,5},{8,12},{9,11},{10,... | collective-permute-start | bytes 215048 | tf_op jit(solution)/shard_map/ppermute | solution.py:289
  40.9 4.3 %collective-permute-start.18 = (bf16[40,896]{1,0:T(8,128)(2,1)S(1)}, bf16[40,896]{1,0:T(8,128)(2,1)S(1)}, u32[]{:S(2)}, u32[]{:S(2)}) collective-permute-start(bf16[40,896]{1,0:T(8,128)(2,1)S(1)} %get-tuple-element.57), channel_id=1, source_target_pairs={{0,2},{1,5},{2,0},{3,7},{4,6},{5,1},{6,4},{7,3},{8,10},{9,13},{10,... | collective-permute-start | bytes 215048 | tf_op jit(solution)/shard_map/ppermute | solution.py:289
  43.0 8.9 %collective-permute-start.15 = (bf16[140,128]{1,0:T(8,128)(2,1)S(1)}, bf16[140,128]{1,0:T(8,128)(2,1)S(1)}, u32[]{:S(2)}, u32[]{:S(2)}) collective-permute-start(bf16[140,128]{1,0:T(8,128)(2,1)S(1)} %get-tuple-element.52), channel_id=1, source_target_pairs={{0,8},{2,10},{4,12},{6,14},{8,0},{10,2},{12,4},{14,6},{16,24},{18,... | collective-permute-start | bytes 107528 | tf_op jit(solution)/shard_map/ppermute | solution.py:282
  45.7 6.6 %collective-permute-start.19 = (bf16[140,128]{1,0:T(8,128)(2,1)S(1)}, bf16[140,128]{1,0:T(8,128)(2,1)S(1)}, u32[]{:S(2)}, u32[]{:S(2)}) collective-permute-start(bf16[140,128]{1,0:T(8,128)(2,1)S(1)} %get-tuple-element.58), channel_id=1, source_target_pairs={{0,16},{2,18},{4,20},{6,22},{8,24},{10,26},{12,28},{14,30},{16,0},... | collective-permute-start | bytes 107528 | tf_op jit(solution)/shard_map/ppermute | solution.py:282
  47.9 5.8 %collective-permute-start.20 = (bf16[140,128]{1,0:T(8,128)(2,1)S(1)}, bf16[140,128]{1,0:T(8,128)(2,1)S(1)}, u32[]{:S(2)}, u32[]{:S(2)}) collective-permute-start(bf16[140,128]{1,0:T(8,128)(2,1)S(1)} %get-tuple-element.59), channel_id=1, source_target_pairs={{0,24},{2,26},{4,28},{6,30},{8,16},{10,18},{12,20},{14,22},{16,8},... | collective-permute-start | bytes 107528 | tf_op jit(solution)/shard_map/ppermute | solution.py:282
  52.2 1.9 %collective-permute-start.21 = (bf16[16,1792]{1,0:T(8,128)(2,1)S(1)}, bf16[16,1792]{1,0:T(8,128)(2,1)S(1)}, u32[]{:S(2)}, u32[]{:S(2)}) collective-permute-start(bf16[16,1792]{1,0:T(8,128)(2,1)S(1)} %get-tuple-element.67), channel_id=1, source_target_pairs={{0,1},{1,0},{2,3},{3,2},{4,5},{5,4},{6,7},{7,6},{8,9},{9,8},{10,11... | collective-permute-start | bytes 172040 | tf_op jit(solution)/shard_map/ppermute | solution.py:278
  53.7 1.6 %copy-start.3 = (f32[32,128]{1,0:T(8,128)S(1)}, f32[32,128]{1,0:T(8,128)}, u32[]{:S(2)}) copy-start(f32[32,128]{1,0:T(8,128)} %get-tuple-element.38.hot_ref) | copy-start | bytes 49156
  54.0 1.3 %collective-permute-start.22 = (bf16[16,1792]{1,0:T(8,128)(2,1)S(1)}, bf16[16,1792]{1,0:T(8,128)(2,1)S(1)}, u32[]{:S(2)}, u32[]{:S(2)}) collective-permute-start(bf16[16,1792]{1,0:T(8,128)(2,1)S(1)} %get-tuple-element.68), channel_id=1, source_target_pairs={{0,1},{1,0},{2,3},{3,2},{4,5},{5,4},{6,7},{7,6},{8,9},{9,8},{10,11... | collective-permute-start | bytes 172040 | tf_op jit(solution)/shard_map/ppermute | solution.py:278

commit v2 on v1

--- a/solution.py
+++ b/solution.py
@@ -63,7 +63,7 @@
 
 
 def gather_kernel(live, *refs):
-    sources, outs, local, sems = refs[:5], refs[5:8], refs[8:13], refs[13]
+    sources, outs, local, sems = refs[:5], refs[5:-6], refs[-6:-1], refs[-1]
     copies = [pltpu.make_async_copy(sources[i], local[i], sems.at[i]) for i in range(5)]
     for copy in copies:
         copy.start()
@@ -77,7 +77,7 @@
     row = iota((live * 8, 1), 0)
     expert, slot = place ^ (row // 8), lax.rem(row, 8)
     hot, _ = pick_rows(routes, keep, gates, expert, slot, slot < MOST)
-    outs[2][...] = hot.astype(F32)
+    outs[-1][...] = hot.astype(F32)
 
     row = iota((live * SIDES * MOST, 1), 0)
     expert = place ^ (row // (SIDES * MOST))
@@ -89,32 +89,42 @@
     hot_s = hot_s.astype(F32).astype(BF16)
     for copy in copies[3:]:
         copy.wait()
+    fold = half // FOLDS
+    each = SIDES * MOST
+    folds = []
+    for f in range(CORES * FOLDS):
+        start = (me ^ (f // FOLDS)) * half + f % FOLDS * fold
+        columns = pl.ds(pl.multiple_of(start, 128), fold)
+        folds.append(dot(hot_x, x_ref[:, columns]) + scale * dot(hot_s, o_ref[:, columns]))
+    count = live // GROUPS * each
     for q in range(CORES):
-        columns = pl.ds(pl.multiple_of((me ^ q) * half, 128), half)
-        rows = dot(hot_x, x_ref[:, columns]) + scale * dot(hot_s, o_ref[:, columns])
-        outs[q][...] = rows.astype(BF16)
-
-
-def chunk_kernel(live, mine_ref, other_ref, *outs):
+        for f in range(FOLDS):
+            outs[q][:, f * fold : (f + 1) * fold] = folds[q * FOLDS + f][:count].astype(BF16)
+    for d in range(live // GROUPS, live):
+        chunk = [rows[d * each : (d + 1) * each] for rows in folds]
+        outs[CORES + d - live // GROUPS][...] = jnp.concatenate(chunk, axis=0).astype(BF16)
+
+
+def chunk_kernel(planes, mine_ref, other_ref, *outs):
     me = lax.axis_index("dp")
     rows, half = mine_ref.shape
     fold = half // FOLDS
     each = SIDES * MOST
     stacked = jnp.concatenate([mine_ref[...], other_ref[...]], axis=0)
     size = FOLDS * CORES * each
-    row = iota((live * size, 1), 0)
+    row = iota((planes * size, 1), 0)
     d, part, at = row // size, lax.rem(row // (CORES * each), FOLDS), lax.rem(row, CORES * each)
     wanted = (at // each ^ me) * rows + d * each + lax.rem(at, each)
-    total = jnp.zeros((live * size, fold), F32)
+    total = jnp.zeros((planes * size, fold), F32)
     for f in range(FOLDS):
         pick = one_hot(jnp.where(part == f, wanted, -1), CORES * rows)
         total = total + dot(pick, stacked[:, f * fold : (f + 1) * fold])
     total = total.astype(BF16)
-    for d in range(live):
+    for d in range(planes):
         outs[d][...] = total[d * size : (d + 1) * size]
 
 
-def merge_kernel(*refs):
+def merge_near_kernel(*refs):
     chunks, out_ref = refs[:-1], refs[-1]
     size, fold = chunks[0].shape
     stacked = jnp.concatenate([chunk[...] for chunk in chunks], axis=0)
@@ -125,6 +135,22 @@
     for f in range(FOLDS):
         wanted = d * size + ((f * CORES + replica) * SIDES + side) * MOST + slot
         picked = dot(one_hot(wanted, len(chunks) * size), stacked)
+        out_ref[:, f * fold : (f + 1) * fold] = picked.astype(BF16)
+
+
+def merge_far_kernel(*refs):
+    chunks, out_ref = refs[:-1], refs[-1]
+    me = lax.axis_index("dp")
+    planes, (size, fold) = len(chunks) // CORES, chunks[0].shape
+    stacked = jnp.concatenate([chunk[...] for chunk in chunks], axis=0)
+    rows = planes * CORES * MOST
+    out = iota((SIDES * rows, 1), 0)
+    side, at = out // rows, lax.rem(out, rows)
+    d, replica, slot = at // (CORES * MOST), lax.rem(at // MOST, CORES), lax.rem(at, MOST)
+    q = replica ^ me
+    first = (q * planes + d) * size + (q * FOLDS * SIDES + side) * MOST + slot
+    for f in range(FOLDS):
+        picked = dot(one_hot(first + f * SIDES * MOST, len(chunks) * size), stacked)
         out_ref[:, f * fold : (f + 1) * fold] = picked.astype(BF16)
 
 
@@ -261,6 +287,7 @@
     fold = half // FOLDS
     rows = CORES * live * MOST
     total = SPLIT * rows
+    planes = live // GROUPS
     vmem, hbm = pl.BlockSpec(memory_space=pltpu.VMEM), pl.BlockSpec(memory_space=pltpu.HBM)
 
     def call(kernel, name, out_shape, operands, flops=0, moved=0):
@@ -288,12 +315,15 @@
                 hop.append((i * CORES + r, (i ^ near(k, r)) * CORES + r))
         return lax.ppermute(array, ("expert", "dp"), hop)
 
-    gathered = like((live * SIDES * MOST, half), BF16)
-    mine, other, hot = pl.pallas_call(
-        lambda *refs: gather_kernel(live, *refs),
-        out_shape=[gathered, gathered, like((live * 8, tokens), F32)],
+    size = FOLDS * CORES * SIDES * MOST
+    near_rows = like((planes * SIDES * MOST, half), BF16)
+    mine, other, *far, hot = pl.pallas_call(
+        functools.partial(gather_kernel, live),
+        out_shape=[near_rows] * CORES
+        + [like((size, fold), BF16)] * (live - planes)
+        + [like((live * 8, tokens), F32)],
         in_specs=[hbm] * 5,
-        out_specs=[vmem] * 3,
+        out_specs=[vmem] * (CORES + live - planes + 1),
         scratch_shapes=[
             pltpu.VMEM((TOP, tokens), jnp.int32),
             pltpu.VMEM((TOP, tokens), jnp.int32),
@@ -305,23 +335,25 @@
         compiler_params=params(FIRST_MIB),
         name="gather_rows",
     )(routes.T, keep_mask.T, gate_values.T, layer_input, out_grad)
-    chunks = call(
-        lambda *refs: chunk_kernel(live, *refs),
+    far = [along_z(chunk, planes + d) for d, chunk in enumerate(far)]
+    near_chunks = call(
+        functools.partial(chunk_kernel, planes),
         "chunk_rows",
-        [like((FOLDS * CORES * SIDES * MOST, fold), BF16)] * live,
+        [like((size, fold), BF16)] * planes,
         [mine, swap_cores(other)],
         1e10,
         2e7,
     )
-    chunks = [chunks[0]] + [along_z(chunks[d], d) for d in range(1, live)]
+    near_chunks = [near_chunks[0]] + [along_z(near_chunks[d], d) for d in range(1, planes)]
     mines, others, xs, ss = [], [], [], []
-    rows_in_group, planes = total // GROUPS, live // GROUPS
+    rows_in_group = total // GROUPS
     for group in reversed(range(GROUPS)):
+        here = far + [swap_cores(chunk) for chunk in far] if group else near_chunks
         rows_here = call(
-            merge_kernel,
+            merge_far_kernel if group else merge_near_kernel,
             "merge_rows",
             like((SIDES * rows // GROUPS, half), BF16),
-            chunks[group * planes : (group + 1) * planes],
+            here,
             1e8,
             1e6,
         )

time: 56.8 us -> 56.2 us (0.989)
  starting transfers between devices: 27.4 us -> 24.6 us
  waiting for transfers between devices: 15.2 us -> 17.5 us
    ppermute x12, waiting for transfers between devices: 5.53 us -> 7.97 us  [in_plane(): return lax.ppermute(array, ('expert', 'dp'), hop)]
    ppermute x6, starting transfers between devices: 10.6 us -> 8.74 us  [along_z(): return lax.ppermute(array, 'expert', hop)]
    ppermute x5 -> x7, waiting for transfers between devices: 4.1 us -> 2.9 us  [swap_cores(): return lax.ppermute(array, 'dp', [(r, r ^ 1) for r in range(CORES)])]
    ppermute x6, waiting for transfers between devices: 5.62 us -> 6.59 us  [along_z(): return lax.ppermute(array, 'expert', hop)]
    ppermute x12, starting transfers between devices: 16 us -> 15 us  [in_plane(): return lax.ppermute(array, ('expert', 'dp'), hop)]
  transfers between devices with their start and end apart: 23 -> 25, of which waited for: 13 -> 16; matrix products, arithmetic and copies ran while one was open for 0% -> 0% of each run, Pallas kernels for 12% -> 12%
where the time goes in v2:
time: 56.2 us; the launch traced here: 56 us
  starting transfers between devices  24.6 us (44%)
  waiting for transfers between devices  17.5 us (31%)
  Pallas kernels  12.3 us (22%)
  local copies, waits for them, and re-layouts  0.9 us (2%)
  between operations  0.8 us (1%)
    ppermute x12, starting transfers between devices, in_plane(): return lax.ppermute(array, ('expert', 'dp'), hop)  15 us
    ppermute x6, starting transfers between devices, along_z(): return lax.ppermute(array, 'expert', hop)  8.74 us
    ppermute x12, waiting for transfers between devices, in_plane(): return lax.ppermute(array, ('expert', 'dp'), hop)  7.97 us
    pallas_call x11, Pallas kernels, call(): pl.pallas_call(kernel, out_shape=out_shape, in_specs=[vmem] * len(operand...  7.14 us
    ppermute x6, waiting for transfers between devices, along_z(): return lax.ppermute(array, 'expert', hop)  6.59 us
    ppermute x7, waiting for transfers between devices, swap_cores(): return lax.ppermute(array, 'dp', [(r, r ^ 1) for r in range(CORES)])  2.9 us
    pallas_call x1, Pallas kernels, body(): pl.pallas_call(functools.partial(gather_kernel, live), out_shape=[near_ro...  2.65 us
    pallas_call x1, Pallas kernels, body(): pl.pallas_call(grads_kernel, out_shape=[like((half, width), BF16)] * 3 +...  2.5 us
  transfers between devices with their start and end apart: 25, of which 16 were waited for; matrix products, arithmetic and copies ran while one was open for 0% of the time, Pallas kernels for 12%

profile of v2, /device:TPU:0, one launch (start us, length us, event | category | flops | bytes accessed | tf_op | source)
XLA Modules:
  0.0 56.0 jit_solution(5715977410493370838)
XLA Ops:
  0.6 2.6 %gather_rows.1 = (bf16[20,1792]{1,0:T(8,128)(2,1)}, bf16[20,1792]{1,0:T(8,128)(2,1)}, bf16[40,896]{1,0:T(8,128)(2,1)}, bf16[40,896]{1,0:T(8,128)(2,1)}, f32[32,128]{1,0:T(8,128)}) custom-call(s32[8,128]{1,0:T(8,128)} %bitcast.3, s32[8,128]{1,0:T(8,128)} %bitcast.4, f32[8,128]{1,0:T(8,128)} %bitcast.5, bf16[128,3584]{1,0:T(8,128)(2,1)} %refs_3_.1, ...), custom_call_target="tpu_custom_call" | custom-call | tf_op jit(solution)/shard_map/gather_rows/pallas_call | solution.py:320
  3.3 0.5 collective-permute-start.7
  3.8 3.7 %collective-permute-start = (bf16[40,896]{1,0:T(8,128)(2,1)}, bf16[40,896]{1,0:T(8,128)(2,1)S(1)}, u32[]{:S(2)}, u32[]{:S(2)}) collective-permute-start(bf16[40,896]{1,0:T(8,128)(2,1)} %get-tuple-element.39), channel_id=1, source_target_pairs={{0,16},{2,18},{4,20},{6,22},{8,24},{10,26},{12,28},{14,30},{16,0},... | collective-permute-start | bytes 215048 | tf_op jit(solution)/shard_map/ppermute | solution.py:309
  7.5 1.3 %collective-permute-start.1 = (bf16[40,896]{1,0:T(8,128)(2,1)}, bf16[40,896]{1,0:T(8,128)(2,1)S(1)}, u32[]{:S(2)}, u32[]{:S(2)}) collective-permute-start(bf16[40,896]{1,0:T(8,128)(2,1)} %get-tuple-element.40), channel_id=1, source_target_pairs={{0,24},{2,26},{4,28},{6,30},{8,16},{10,18},{12,20},{14,22},{16,8},... | collective-permute-start | bytes 215048 | tf_op jit(solution)/shard_map/ppermute | solution.py:309
  8.8 0.0 collective-permute-done.7.other_ref
  8.8 0.9 %copy-done.4 = bf16[20,1792]{1,0:T(8,128)(2,1)S(1)} copy-done((bf16[20,1792]{1,0:T(8,128)(2,1)S(1)}, bf16[20,1792]{1,0:T(8,128)(2,1)}, u32[]{:S(2)}) %copy-start.4) | copy-done | bytes 71704
  9.7 0.3 chunk_rows.1
  10.0 0.3 collective-permute-start.8
  10.3 2.0 %collective-permute-done.refs_0_ = bf16[40,896]{1,0:T(8,128)(2,1)S(1)} collective-permute-done((bf16[40,896]{1,0:T(8,128)(2,1)}, bf16[40,896]{1,0:T(8,128)(2,1)S(1)}, u32[]{:S(2)}, u32[]{:S(2)}) %collective-permute-start) | collective-permute-done | bytes 71712 | tf_op jit(solution)/shard_map/ppermute | solution.py:309
  12.3 0.0 collective-permute-start.2
  12.3 1.7 %collective-permute-done.1.refs_1_ = bf16[40,896]{1,0:T(8,128)(2,1)S(1)} collective-permute-done((bf16[40,896]{1,0:T(8,128)(2,1)}, bf16[40,896]{1,0:T(8,128)(2,1)S(1)}, u32[]{:S(2)}, u32[]{:S(2)}) %collective-permute-start.1) | collective-permute-done | bytes 71712 | tf_op jit(solution)/shard_map/ppermute | solution.py:309
  14.0 0.0 collective-permute-start.3
  14.0 1.4 %collective-permute-done.8.refs_1_ = bf16[40,896]{1,0:T(8,128)(2,1)S(1)} collective-permute-done((bf16[40,896]{1,0:T(8,128)(2,1)S(1)}, bf16[40,896]{1,0:T(8,128)(2,1)S(1)}, u32[]{:S(2)}, u32[]{:S(2)}) %collective-permute-start.8) | collective-permute-done | bytes 71712 | tf_op jit(solution)/shard_map/ppermute | solution.py:309
  15.4 0.2 merge_rows.3.refs_0_
  15.6 1.6 %collective-permute-start.9 = (bf16[40,1792]{1,0:T(8,128)(2,1)S(1)}, bf16[40,1792]{1,0:T(8,128)(2,1)S(1)}, u32[]{:S(2)}, u32[]{:S(2)}) collective-permute-start(bf16[40,1792]{1,0:T(8,128)(2,1)S(1)} %merge_rows.3.refs_0_), channel_id=1, source_target_pairs={{0,2},{1,5},{2,0},{3,7},{4,6},{5,1},{6,4},{7,3},{8,10},{9,13},{10,... | collective-permute-start | bytes 430088 | tf_op jit(solution)/shard_map/ppermute | solution.py:316
  17.3 0.0 collective-permute-done.2.refs_2_
  17.3 0.0 collective-permute-done.3.refs_3_
  17.3 0.2 merge_rows.2.refs_0_
  17.5 0.5 collective-permute-start.4
  18.1 1.6 %collective-permute-start.10 = (bf16[40,1792]{1,0:T(8,128)(2,1)S(1)}, bf16[40,1792]{1,0:T(8,128)(2,1)S(1)}, u32[]{:S(2)}, u32[]{:S(2)}) collective-permute-start(bf16[40,1792]{1,0:T(8,128)(2,1)S(1)} %merge_rows.3.refs_0_), channel_id=1, source_target_pairs={{0,4},{1,3},{2,6},{3,1},{4,0},{5,7},{6,2},{7,5},{8,12},{9,11},{10,... | collective-permute-start | bytes 430088 | tf_op jit(solution)/shard_map/ppermute | solution.py:316
  19.7 1.9 %collective-permute-done.9.refs_1_ = bf16[40,1792]{1,0:T(8,128)(2,1)S(1)} collective-permute-done((bf16[40,1792]{1,0:T(8,128)(2,1)S(1)}, bf16[40,1792]{1,0:T(8,128)(2,1)S(1)}, u32[]{:S(2)}, u32[]{:S(2)}) %collective-permute-start.9) | collective-permute-done | bytes 143392 | tf_op jit(solution)/shard_map/ppermute | solution.py:316
  21.5 1.6 %collective-permute-start.11 = (bf16[40,1792]{1,0:T(8,128)(2,1)S(1)}, bf16[40,1792]{1,0:T(8,128)(2,1)S(1)}, u32[]{:S(2)}, u32[]{:S(2)}) collective-permute-start(bf16[40,1792]{1,0:T(8,128)(2,1)S(1)} %collective-permute-done.9.refs_1_), channel_id=1, source_target_pairs={{0,4},{1,3},{2,6},{3,1},{4,0},{5,7},{6,2},{7,5},{8,12},{9,11},{10,... | collective-permute-start | bytes 430088 | tf_op jit(solution)/shard_map/ppermute | solution.py:316
  23.1 0.4 collective-permute-start.5
  23.6 1.0 %collective-permute-done.4.refs_1_ = bf16[40,1792]{1,0:T(8,128)(2,1)S(1)} collective-permute-done((bf16[40,1792]{1,0:T(8,128)(2,1)S(1)}, bf16[40,1792]{1,0:T(8,128)(2,1)S(1)}, u32[]{:S(2)}, u32[]{:S(2)}) %collective-permute-start.4) | collective-permute-done | bytes 143392 | tf_op jit(solution)/shard_map/ppermute | solution.py:316
  24.6 1.6 %collective-permute-start.6 = (bf16[40,1792]{1,0:T(8,128)(2,1)S(1)}, bf16[40,1792]{1,0:T(8,128)(2,1)S(1)}, u32[]{:S(2)}, u32[]{:S(2)}) collective-permute-start(bf16[40,1792]{1,0:T(8,128)(2,1)S(1)} %collective-permute-done.4.refs_1_), channel_id=1, source_target_pairs={{0,4},{1,3},{2,6},{3,1},{4,0},{5,7},{6,2},{7,5},{8,12},{9,11},{10,... | collective-permute-start | bytes 430088 | tf_op jit(solution)/shard_map/ppermute | solution.py:316
  26.2 0.0 collective-permute-done.10.refs_2_
  26.2 0.4 collective-permute-done.11.refs_3_
  26.6 1.0 %partial_products.3 = (f32[80,1152]{1,0:T(8,128)S(1)}, bf16[80,1792]{1,0:T(8,128)(2,1)S(1)}, bf16[80,1792]{1,0:T(8,128)(2,1)S(1)}) custom-call(bf16[40,1792]{1,0:T(8,128)(2,1)S(1)} %merge_rows.3.refs_0_, bf16[40,1792]{1,0:T(8,128)(2,1)S(1)} %collective-permute-done.9.refs_1_, bf16[40,1792]{1,0:T(8,128)(2,1)S(1)} %collective-permute-done.10.refs_2_, ...), custom_call_target="tpu_custom_call" | custom-call | flops 330301440 | bytes 4128768 | tf_op jit(solution)/shard_map/partial_products/pallas_call | solution.py:294
  27.7 0.1 collective-permute-start.13
  27.8 0.5 collective-permute-done.5.refs_2_
  28.2 1.5 %collective-permute-done.6.refs_3_ = bf16[40,1792]{1,0:T(8,128)(2,1)S(1)} collective-permute-done((bf16[40,1792]{1,0:T(8,128)(2,1)S(1)}, bf16[40,1792]{1,0:T(8,128)(2,1)S(1)}, u32[]{:S(2)}, u32[]{:S(2)}) %collective-permute-start.6) | collective-permute-done | bytes 143392 | tf_op jit(solution)/shard_map/ppermute | solution.py:316
  29.8 1.0 %partial_products.2 = (f32[80,1152]{1,0:T(8,128)S(1)}, bf16[80,1792]{1,0:T(8,128)(2,1)S(1)}, bf16[80,1792]{1,0:T(8,128)(2,1)S(1)}) custom-call(bf16[40,1792]{1,0:T(8,128)(2,1)S(1)} %merge_rows.2.refs_0_, bf16[40,1792]{1,0:T(8,128)(2,1)S(1)} %collective-permute-done.4.refs_1_, bf16[40,1792]{1,0:T(8,128)(2,1)S(1)} %collective-permute-done.5.refs_2_, ...), custom_call_target="tpu_custom_call" | custom-call | flops 330301440 | bytes 4128768 | tf_op jit(solution)/shard_map/partial_products/pallas_call | solution.py:294
  30.8 0.1 collective-permute-start.12
  30.9 0.0 collective-permute-done.13.refs_3_
  30.9 1.7 %collective-permute-done.12.refs_2_ = f32[80,1152]{1,0:T(8,128)S(1)} collective-permute-done((f32[80,1152]{1,0:T(8,128)S(1)}, f32[80,1152]{1,0:T(8,128)S(1)}, u32[]{:S(2)}, u32[]{:S(2)}) %collective-permute-start.12) | collective-permute-done | bytes 368672 | tf_op jit(solution)/shard_map/ppermute | solution.py:305
  32.6 1.4 %sides_and_parts.1 = (bf16[40,896]{1,0:T(8,128)(2,1)S(1)}, bf16[40,896]{1,0:T(8,128)(2,1)S(1)}, bf16[40,896]{1,0:T(8,128)(2,1)S(1)}, bf16[40,896]{1,0:T(8,128)(2...) custom-call(f32[80,1152]{1,0:T(8,128)S(1)} %get-tuple-element.41.ref, ...), custom_call_target="tpu_custom_call" | custom-call | flops 440401920 | bytes 2752512 | tf_op jit(solution)/shard_map/sides_and_parts/pallas_call | solution.py:294
  34.0 2.5 %collective-permute-start.14 = (bf16[40,896]{1,0:T(8,128)(2,1)S(1)}, bf16[40,896]{1,0:T(8,128)(2,1)S(1)}, u32[]{:S(2)}, u32[]{:S(2)}) collective-permute-start(bf16[40,896]{1,0:T(8,128)(2,1)S(1)} %get-tuple-element.48), channel_id=1, source_target_pairs={{0,6},{1,7},{2,4},{3,5},{4,2},{5,3},{6,0},{7,1},{8,14},{9,15},{10,... | collective-permute-start | bytes 215048 | tf_op jit(solution)/shard_map/ppermute | solution.py:316
  36.5 0.5 collective-permute-start.15
  37.0 0.5 collective-permute-start.16
  37.5 2.5 %collective-permute-start.18 = (bf16[40,896]{1,0:T(8,128)(2,1)S(1)}, bf16[40,896]{1,0:T(8,128)(2,1)S(1)}, u32[]{:S(2)}, u32[]{:S(2)}) collective-permute-start(bf16[40,896]{1,0:T(8,128)(2,1)S(1)} %get-tuple-element.55), channel_id=1, source_target_pairs={{0,6},{1,7},{2,4},{3,5},{4,2},{5,3},{6,0},{7,1},{8,14},{9,15},{10,... | collective-permute-start | bytes 215048 | tf_op jit(solution)/shard_map/ppermute | solution.py:316
  40.0 0.5 collective-permute-start.19
  40.5 0.0 collective-permute-done.14.refs_1_
  40.5 1.1 %collective-permute-start.20 = (bf16[40,896]{1,0:T(8,128)(2,1)S(1)}, bf16[40,896]{1,0:T(8,128)(2,1)S(1)}, u32[]{:S(2)}, u32[]{:S(2)}) collective-permute-start(bf16[40,896]{1,0:T(8,128)(2,1)S(1)} %get-tuple-element.57), channel_id=1, source_target_pairs={{0,2},{1,5},{2,0},{3,7},{4,6},{5,1},{6,4},{7,3},{8,10},{9,13},{10,... | collective-permute-start | bytes 215048 | tf_op jit(solution)/shard_map/ppermute | solution.py:316
  41.6 0.2 collective-permute-done.15.refs_2_
  41.8 0.3 collective-permute-done.16.refs_3_
  42.1 0.5 sum_parts.2
  42.6 0.1 collective-permute-start.17
  42.7 1.1 %collective-permute-done.18.refs_1_ = bf16[40,896]{1,0:T(8,128)(2,1)S(1)} collective-permute-done((bf16[40,896]{1,0:T(8,128)(2,1)S(1)}, bf16[40,896]{1,0:T(8,128)(2,1)S(1)}, u32[]{:S(2)}, u32[]{:S(2)}) %collective-permute-start.18) | collective-permute-done | bytes 71712 | tf_op jit(solution)/shard_map/ppermute | solution.py:316
  43.9 0.7 %collective-permute-done.19.refs_2_ = bf16[40,896]{1,0:T(8,128)(2,1)S(1)} collective-permute-done((bf16[40,896]{1,0:T(8,128)(2,1)S(1)}, bf16[40,896]{1,0:T(8,128)(2,1)S(1)}, u32[]{:S(2)}, u32[]{:S(2)}) %collective-permute-start.19) | collective-permute-done | bytes 71712 | tf_op jit(solution)/shard_map/ppermute | solution.py:316
  44.6 0.2 collective-permute-done.20.refs_3_
  44.8 0.5 sum_parts.3
  45.3 1.9 %collective-permute-start.21 = (bf16[140,128]{1,0:T(8,128)(2,1)S(1)}, bf16[140,128]{1,0:T(8,128)(2,1)S(1)}, u32[]{:S(2)}, u32[]{:S(2)}) collective-permute-start(bf16[140,128]{1,0:T(8,128)(2,1)S(1)} %get-tuple-element.58), channel_id=1, source_target_pairs={{0,16},{2,18},{4,20},{6,22},{8,24},{10,26},{12,28},{14,30},{16,0},... | collective-permute-start | bytes 107528 | tf_op jit(solution)/shard_map/ppermute | solution.py:309
  47.3 1.4 %collective-permute-start.22 = (bf16[140,128]{1,0:T(8,128)(2,1)S(1)}, bf16[140,128]{1,0:T(8,128)(2,1)S(1)}, u32[]{:S(2)}, u32[]{:S(2)}) collective-permute-start(bf16[140,128]{1,0:T(8,128)(2,1)S(1)} %get-tuple-element.59), channel_id=1, source_target_pairs={{0,24},{2,26},{4,28},{6,30},{8,16},{10,18},{12,20},{14,22},{16,8},... | collective-permute-start | bytes 107528 | tf_op jit(solution)/shard_map/ppermute | solution.py:309
  48.6 2.5 %weight_grads.1 = (bf16[1792,384]{1,0:T(8,128)(2,1)}, bf16[1792,384]{1,0:T(8,128)(2,1)}, bf16[1792,384]{1,0:T(8,128)(2,1)}, f32[8,128]{1,0:T(8,128)S(1)}) custom-call(bf16[80,1792]{1,0:T(8,128)(2,1)S(1)} %get-tuple-element.60.refs_0_, bf16[80,1792]{1,0:T(8,128)(2,1)S(1)} %get-tuple-element.61.refs_1_, bf16[80,1792]{1,0:T(8,128)(2,1)S(1)} %get-tuple-element.62.refs_2_, ...), custom_call_target="tpu_custom_call" | custom-call | flops 660602880 | bytes 5275648 | tf_op jit(solution)/shard_map/weight_grads/pallas_call | solution.py:387
  51.2 0.0 collective-permute-done.17.refs_1_
  51.2 0.3 split_rows.2
  51.5 0.1 collective-permute-start.23
  51.6 0.0 collective-permute-done.21.refs_0_
  51.6 1.5 %collective-permute-done.22.refs_1_ = bf16[140,128]{1,0:T(8,128)(2,1)S(1)} collective-permute-done((bf16[140,128]{1,0:T(8,128)(2,1)S(1)}, bf16[140,128]{1,0:T(8,128)(2,1)S(1)}, u32[]{:S(2)}, u32[]{:S(2)}) %collective-permute-start.22) | collective-permute-done | bytes 35872 | tf_op jit(solution)/shard_map/ppermute | solution.py:309
  53.0 0.3 split_rows.3
  53.3 0.1 collective-permute-start.24
  53.4 0.0 collective-permute-done.23.refs_2_
  53.4 1.2 %collective-permute-done.24.refs_3_ = bf16[16,1792]{1,0:T(8,128)(2,1)S(1)} collective-permute-done((bf16[16,1792]{1,0:T(8,128)(2,1)S(1)}, bf16[16,1792]{1,0:T(8,128)(2,1)S(1)}, u32[]{:S(2)}, u32[]{:S(2)}) %collective-permute-start.24) | collective-permute-done | bytes 57376 | tf_op jit(solution)/shard_map/ppermute | solution.py:305
  54.7 1.3 %place_rows.1 = bf16[128,3584]{1,0:T(8,128)(2,1)} custom-call(f32[32,128]{1,0:T(8,128)S(1)} %copy-done.3, bf16[16,1792]{1,0:T(8,128)(2,1)S(1)} %get-tuple-element.53.refs_0_, bf16[16,1792]{1,0:T(8,128)(2,1)S(1)} %get-tuple-element.66.refs_1_, bf16[16,1792]{1,0:T(8,128)(2,1)S(1)} %collective-permute-done.23.refs_2_, ...), custom_call_target="tpu_custom_call" | custom-call | tf_op jit(solution)/shard_map/place_rows/pallas_call | solution.py:294
  (9 shorter events, 0.0 us)
Async XLA Ops:
  3.3 5.5 %collective-permute-start.7 = (bf16[20,1792]{1,0:T(8,128)(2,1)}, bf16[20,1792]{1,0:T(8,128)(2,1)S(1)}, u32[]{:S(2)}, u32[]{:S(2)}) collective-permute-start(bf16[20,1792]{1,0:T(8,128)(2,1)} %get-tuple-element.43), channel_id=1, source_target_pairs={{0,1},{1,0},{2,3},{3,2},{4,5},{5,4},{6,7},{7,6},{8,9},{9,8},{10,11... | collective-permute-start | bytes 215048 | tf_op jit(solution)/shard_map/ppermute | solution.py:305
  3.8 8.5 %collective-permute-start = (bf16[40,896]{1,0:T(8,128)(2,1)}, bf16[40,896]{1,0:T(8,128)(2,1)S(1)}, u32[]{:S(2)}, u32[]{:S(2)}) collective-permute-start(bf16[40,896]{1,0:T(8,128)(2,1)} %get-tuple-element.39), channel_id=1, source_target_pairs={{0,16},{2,18},{4,20},{6,22},{8,24},{10,26},{12,28},{14,30},{16,0},... | collective-permute-start | bytes 215048 | tf_op jit(solution)/shard_map/ppermute | solution.py:309
  7.5 6.6 %collective-permute-start.1 = (bf16[40,896]{1,0:T(8,128)(2,1)}, bf16[40,896]{1,0:T(8,128)(2,1)S(1)}, u32[]{:S(2)}, u32[]{:S(2)}) collective-permute-start(bf16[40,896]{1,0:T(8,128)(2,1)} %get-tuple-element.40), channel_id=1, source_target_pairs={{0,24},{2,26},{4,28},{6,30},{8,16},{10,18},{12,20},{14,22},{16,8},... | collective-permute-start | bytes 215048 | tf_op jit(solution)/shard_map/ppermute | solution.py:309
  8.8 0.9 %copy-start.4 = (bf16[20,1792]{1,0:T(8,128)(2,1)S(1)}, bf16[20,1792]{1,0:T(8,128)(2,1)}, u32[]{:S(2)}) copy-start(bf16[20,1792]{1,0:T(8,128)(2,1)} %get-tuple-element.42.mine_ref) | copy-start | bytes 215044
  9.7 16.9 %copy-start = (bf16[1792,384]{1,0:T(8,128)(2,1)S(1)}, bf16[1792,384]{1,0:T(8,128)(2,1)}, u32[]{:S(2)}) copy-start(bf16[1792,384]{1,0:T(8,128)(2,1)} %refs_4_.7) | copy-start | bytes 4128772
  9.7 16.9 %copy-start.1 = (bf16[1792,384]{1,0:T(8,128)(2,1)S(1)}, bf16[1792,384]{1,0:T(8,128)(2,1)}, u32[]{:S(2)}) copy-start(bf16[1792,384]{1,0:T(8,128)(2,1)} %refs_5_.5) | copy-start | bytes 4128772
  9.7 16.9 %copy-start.2 = (bf16[1792,384]{1,0:T(8,128)(2,1)S(1)}, bf16[1792,384]{1,0:T(8,128)(2,1)}, u32[]{:S(2)}) copy-start(bf16[1792,384]{1,0:T(8,128)(2,1)} %refs_6_.3) | copy-start | bytes 4128772
  10.0 5.4 %collective-permute-start.8 = (bf16[40,896]{1,0:T(8,128)(2,1)S(1)}, bf16[40,896]{1,0:T(8,128)(2,1)S(1)}, u32[]{:S(2)}, u32[]{:S(2)}) collective-permute-start(bf16[40,896]{1,0:T(8,128)(2,1)S(1)} %get-tuple-element.45), channel_id=1, source_target_pairs={{0,8},{2,10},{4,12},{6,14},{8,0},{10,2},{12,4},{14,6},{16,24},{18,... | collective-permute-start | bytes 215048 | tf_op jit(solution)/shard_map/ppermute | solution.py:309
  12.3 5.0 %collective-permute-start.2 = (bf16[40,896]{1,0:T(8,128)(2,1)S(1)}, bf16[40,896]{1,0:T(8,128)(2,1)S(1)}, u32[]{:S(2)}, u32[]{:S(2)}) collective-permute-start(bf16[40,896]{1,0:T(8,128)(2,1)S(1)} %collective-permute-done.refs_0_), channel_id=1, source_target_pairs={{0,1},{1,0},{2,3},{3,2},{4,5},{5,4},{6,7},{7,6},{8,9},{9,8},{10,11... | collective-permute-start | bytes 215048 | tf_op jit(solution)/shard_map/ppermute | solution.py:305
  14.0 3.2 %collective-permute-start.3 = (bf16[40,896]{1,0:T(8,128)(2,1)S(1)}, bf16[40,896]{1,0:T(8,128)(2,1)S(1)}, u32[]{:S(2)}, u32[]{:S(2)}) collective-permute-start(bf16[40,896]{1,0:T(8,128)(2,1)S(1)} %collective-permute-done.1.refs_1_), channel_id=1, source_target_pairs={{0,1},{1,0},{2,3},{3,2},{4,5},{5,4},{6,7},{7,6},{8,9},{9,8},{10,11... | collective-permute-start | bytes 215048 | tf_op jit(solution)/shard_map/ppermute | solution.py:305
  15.6 5.9 %collective-permute-start.9 = (bf16[40,1792]{1,0:T(8,128)(2,1)S(1)}, bf16[40,1792]{1,0:T(8,128)(2,1)S(1)}, u32[]{:S(2)}, u32[]{:S(2)}) collective-permute-start(bf16[40,1792]{1,0:T(8,128)(2,1)S(1)} %merge_rows.3.refs_0_), channel_id=1, source_target_pairs={{0,2},{1,5},{2,0},{3,7},{4,6},{5,1},{6,4},{7,3},{8,10},{9,13},{10,... | collective-permute-start | bytes 430088 | tf_op jit(solution)/shard_map/ppermute | solution.py:316
  17.5 7.1 %collective-permute-start.4 = (bf16[40,1792]{1,0:T(8,128)(2,1)S(1)}, bf16[40,1792]{1,0:T(8,128)(2,1)S(1)}, u32[]{:S(2)}, u32[]{:S(2)}) collective-permute-start(bf16[40,1792]{1,0:T(8,128)(2,1)S(1)} %merge_rows.2.refs_0_), channel_id=1, source_target_pairs={{0,2},{1,5},{2,0},{3,7},{4,6},{5,1},{6,4},{7,3},{8,10},{9,13},{10,... | collective-permute-start | bytes 430088 | tf_op jit(solution)/shard_map/ppermute | solution.py:316
  18.1 8.2 %collective-permute-start.10 = (bf16[40,1792]{1,0:T(8,128)(2,1)S(1)}, bf16[40,1792]{1,0:T(8,128)(2,1)S(1)}, u32[]{:S(2)}, u32[]{:S(2)}) collective-permute-start(bf16[40,1792]{1,0:T(8,128)(2,1)S(1)} %merge_rows.3.refs_0_), channel_id=1, source_target_pairs={{0,4},{1,3},{2,6},{3,1},{4,0},{5,7},{6,2},{7,5},{8,12},{9,11},{10,... | collective-permute-start | bytes 430088 | tf_op jit(solution)/shard_map/ppermute | solution.py:316
  21.5 5.1 %collective-permute-start.11 = (bf16[40,1792]{1,0:T(8,128)(2,1)S(1)}, bf16[40,1792]{1,0:T(8,128)(2,1)S(1)}, u32[]{:S(2)}, u32[]{:S(2)}) collective-permute-start(bf16[40,1792]{1,0:T(8,128)(2,1)S(1)} %collective-permute-done.9.refs_1_), channel_id=1, source_target_pairs={{0,4},{1,3},{2,6},{3,1},{4,0},{5,7},{6,2},{7,5},{8,12},{9,11},{10,... | collective-permute-start | bytes 430088 | tf_op jit(solution)/shard_map/ppermute | solution.py:316
  23.1 5.1 %collective-permute-start.5 = (bf16[40,1792]{1,0:T(8,128)(2,1)S(1)}, bf16[40,1792]{1,0:T(8,128)(2,1)S(1)}, u32[]{:S(2)}, u32[]{:S(2)}) collective-permute-start(bf16[40,1792]{1,0:T(8,128)(2,1)S(1)} %merge_rows.2.refs_0_), channel_id=1, source_target_pairs={{0,4},{1,3},{2,6},{3,1},{4,0},{5,7},{6,2},{7,5},{8,12},{9,11},{10,... | collective-permute-start | bytes 430088 | tf_op jit(solution)/shard_map/ppermute | solution.py:316
  24.6 5.2 %collective-permute-start.6 = (bf16[40,1792]{1,0:T(8,128)(2,1)S(1)}, bf16[40,1792]{1,0:T(8,128)(2,1)S(1)}, u32[]{:S(2)}, u32[]{:S(2)}) collective-permute-start(bf16[40,1792]{1,0:T(8,128)(2,1)S(1)} %collective-permute-done.4.refs_1_), channel_id=1, source_target_pairs={{0,4},{1,3},{2,6},{3,1},{4,0},{5,7},{6,2},{7,5},{8,12},{9,11},{10,... | collective-permute-start | bytes 430088 | tf_op jit(solution)/shard_map/ppermute | solution.py:316
  27.7 3.2 %collective-permute-start.13 = (f32[80,1152]{1,0:T(8,128)S(1)}, f32[80,1152]{1,0:T(8,128)S(1)}, u32[]{:S(2)}, u32[]{:S(2)}) collective-permute-start(f32[80,1152]{1,0:T(8,128)S(1)} %get-tuple-element.46.refs_1_), channel_id=1, source_target_pairs={{0,1},{1,0},{2,3},{3,2},{4,5},{5,4},{6,7},{7,6},{8,9},{9,8},{10,11... | collective-permute-start | bytes 1105928 | tf_op jit(solution)/shard_map/ppermute | solution.py:305
  30.8 1.8 %collective-permute-start.12 = (f32[80,1152]{1,0:T(8,128)S(1)}, f32[80,1152]{1,0:T(8,128)S(1)}, u32[]{:S(2)}, u32[]{:S(2)}) collective-permute-start(f32[80,1152]{1,0:T(8,128)S(1)} %get-tuple-element.41.refs_0_), channel_id=1, source_target_pairs={{0,1},{1,0},{2,3},{3,2},{4,5},{5,4},{6,7},{7,6},{8,9},{9,8},{10,11... | collective-permute-start | bytes 1105928 | tf_op jit(solution)/shard_map/ppermute | solution.py:305
  34.0 6.5 %collective-permute-start.14 = (bf16[40,896]{1,0:T(8,128)(2,1)S(1)}, bf16[40,896]{1,0:T(8,128)(2,1)S(1)}, u32[]{:S(2)}, u32[]{:S(2)}) collective-permute-start(bf16[40,896]{1,0:T(8,128)(2,1)S(1)} %get-tuple-element.48), channel_id=1, source_target_pairs={{0,6},{1,7},{2,4},{3,5},{4,2},{5,3},{6,0},{7,1},{8,14},{9,15},{10,... | collective-permute-start | bytes 215048 | tf_op jit(solution)/shard_map/ppermute | solution.py:316
  36.5 5.3 %collective-permute-start.15 = (bf16[40,896]{1,0:T(8,128)(2,1)S(1)}, bf16[40,896]{1,0:T(8,128)(2,1)S(1)}, u32[]{:S(2)}, u32[]{:S(2)}) collective-permute-start(bf16[40,896]{1,0:T(8,128)(2,1)S(1)} %get-tuple-element.49), channel_id=1, source_target_pairs={{0,4},{1,3},{2,6},{3,1},{4,0},{5,7},{6,2},{7,5},{8,12},{9,11},{10,... | collective-permute-start | bytes 215048 | tf_op jit(solution)/shard_map/ppermute | solution.py:316
  37.0 5.1 %collective-permute-start.16 = (bf16[40,896]{1,0:T(8,128)(2,1)S(1)}, bf16[40,896]{1,0:T(8,128)(2,1)S(1)}, u32[]{:S(2)}, u32[]{:S(2)}) collective-permute-start(bf16[40,896]{1,0:T(8,128)(2,1)S(1)} %get-tuple-element.50), channel_id=1, source_target_pairs={{0,2},{1,5},{2,0},{3,7},{4,6},{5,1},{6,4},{7,3},{8,10},{9,13},{10,... | collective-permute-start | bytes 215048 | tf_op jit(solution)/shard_map/ppermute | solution.py:316
  37.5 6.3 %collective-permute-start.18 = (bf16[40,896]{1,0:T(8,128)(2,1)S(1)}, bf16[40,896]{1,0:T(8,128)(2,1)S(1)}, u32[]{:S(2)}, u32[]{:S(2)}) collective-permute-start(bf16[40,896]{1,0:T(8,128)(2,1)S(1)} %get-tuple-element.55), channel_id=1, source_target_pairs={{0,6},{1,7},{2,4},{3,5},{4,2},{5,3},{6,0},{7,1},{8,14},{9,15},{10,... | collective-permute-start | bytes 215048 | tf_op jit(solution)/shard_map/ppermute | solution.py:316
  40.0 4.6 %collective-permute-start.19 = (bf16[40,896]{1,0:T(8,128)(2,1)S(1)}, bf16[40,896]{1,0:T(8,128)(2,1)S(1)}, u32[]{:S(2)}, u32[]{:S(2)}) collective-permute-start(bf16[40,896]{1,0:T(8,128)(2,1)S(1)} %get-tuple-element.56), channel_id=1, source_target_pairs={{0,4},{1,3},{2,6},{3,1},{4,0},{5,7},{6,2},{7,5},{8,12},{9,11},{10,... | collective-permute-start | bytes 215048 | tf_op jit(solution)/shard_map/ppermute | solution.py:316
  40.5 4.3 %collective-permute-start.20 = (bf16[40,896]{1,0:T(8,128)(2,1)S(1)}, bf16[40,896]{1,0:T(8,128)(2,1)S(1)}, u32[]{:S(2)}, u32[]{:S(2)}) collective-permute-start(bf16[40,896]{1,0:T(8,128)(2,1)S(1)} %get-tuple-element.57), channel_id=1, source_target_pairs={{0,2},{1,5},{2,0},{3,7},{4,6},{5,1},{6,4},{7,3},{8,10},{9,13},{10,... | collective-permute-start | bytes 215048 | tf_op jit(solution)/shard_map/ppermute | solution.py:316
  42.6 8.6 %collective-permute-start.17 = (bf16[140,128]{1,0:T(8,128)(2,1)S(1)}, bf16[140,128]{1,0:T(8,128)(2,1)S(1)}, u32[]{:S(2)}, u32[]{:S(2)}) collective-permute-start(bf16[140,128]{1,0:T(8,128)(2,1)S(1)} %get-tuple-element.52), channel_id=1, source_target_pairs={{0,8},{2,10},{4,12},{6,14},{8,0},{10,2},{12,4},{14,6},{16,24},{18,... | collective-permute-start | bytes 107528 | tf_op jit(solution)/shard_map/ppermute | solution.py:309
  45.3 6.2 %collective-permute-start.21 = (bf16[140,128]{1,0:T(8,128)(2,1)S(1)}, bf16[140,128]{1,0:T(8,128)(2,1)S(1)}, u32[]{:S(2)}, u32[]{:S(2)}) collective-permute-start(bf16[140,128]{1,0:T(8,128)(2,1)S(1)} %get-tuple-element.58), channel_id=1, source_target_pairs={{0,16},{2,18},{4,20},{6,22},{8,24},{10,26},{12,28},{14,30},{16,0},... | collective-permute-start | bytes 107528 | tf_op jit(solution)/shard_map/ppermute | solution.py:309
  47.3 5.8 %collective-permute-start.22 = (bf16[140,128]{1,0:T(8,128)(2,1)S(1)}, bf16[140,128]{1,0:T(8,128)(2,1)S(1)}, u32[]{:S(2)}, u32[]{:S(2)}) collective-permute-start(bf16[140,128]{1,0:T(8,128)(2,1)S(1)} %get-tuple-element.59), channel_id=1, source_target_pairs={{0,24},{2,26},{4,28},{6,30},{8,16},{10,18},{12,20},{14,22},{16,8},... | collective-permute-start | bytes 107528 | tf_op jit(solution)/shard_map/ppermute | solution.py:309
  51.5 2.0 %collective-permute-start.23 = (bf16[16,1792]{1,0:T(8,128)(2,1)S(1)}, bf16[16,1792]{1,0:T(8,128)(2,1)S(1)}, u32[]{:S(2)}, u32[]{:S(2)}) collective-permute-start(bf16[16,1792]{1,0:T(8,128)(2,1)S(1)} %get-tuple-element.67), channel_id=1, source_target_pairs={{0,1},{1,0},{2,3},{3,2},{4,5},{5,4},{6,7},{7,6},{8,9},{9,8},{10,11... | collective-permute-start | bytes 172040 | tf_op jit(solution)/shard_map/ppermute | solution.py:305
  53.0 1.6 %copy-start.3 = (f32[32,128]{1,0:T(8,128)S(1)}, f32[32,128]{1,0:T(8,128)}, u32[]{:S(2)}) copy-start(f32[32,128]{1,0:T(8,128)} %get-tuple-element.38.hot_ref) | copy-start | bytes 49156
  53.3 1.3 %collective-permute-start.24 = (bf16[16,1792]{1,0:T(8,128)(2,1)S(1)}, bf16[16,1792]{1,0:T(8,128)(2,1)S(1)}, u32[]{:S(2)}, u32[]{:S(2)}) collective-permute-start(bf16[16,1792]{1,0:T(8,128)(2,1)S(1)} %get-tuple-element.68), channel_id=1, source_target_pairs={{0,1},{1,0},{2,3},{3,2},{4,5},{5,4},{6,7},{7,6},{8,9},{9,8},{10,11... | collective-permute-start | bytes 172040 | tf_op jit(solution)/shard_map/ppermute | solution.py:305

commit v3 on v2

--- a/solution.py
+++ b/solution.py
@@ -13,6 +13,7 @@
 SIDES = 2
 CORES = 2
 TOKEN_GROUP = 1
+OWN_COST = 1e10
 GROUPS = 2
 FOLDS = 2
 FIRST_MIB = 60
@@ -96,74 +97,58 @@
         start = (me ^ (f // FOLDS)) * half + f % FOLDS * fold
         columns = pl.ds(pl.multiple_of(start, 128), fold)
         folds.append(dot(hot_x, x_ref[:, columns]) + scale * dot(hot_s, o_ref[:, columns]))
-    count = live // GROUPS * each
     for q in range(CORES):
         for f in range(FOLDS):
-            outs[q][:, f * fold : (f + 1) * fold] = folds[q * FOLDS + f][:count].astype(BF16)
-    for d in range(live // GROUPS, live):
+            outs[q][:, f * fold : (f + 1) * fold] = folds[q * FOLDS + f][:each].astype(BF16)
+    for d in range(1, live):
         chunk = [rows[d * each : (d + 1) * each] for rows in folds]
-        outs[CORES + d - live // GROUPS][...] = jnp.concatenate(chunk, axis=0).astype(BF16)
-
-
-def chunk_kernel(planes, mine_ref, other_ref, *outs):
+        outs[CORES + d - 1][...] = jnp.concatenate(chunk, axis=0).astype(BF16)
+
+
+def own_kernel(mine_ref, other_ref, out_ref):
     me = lax.axis_index("dp")
     rows, half = mine_ref.shape
     fold = half // FOLDS
-    each = SIDES * MOST
-    stacked = jnp.concatenate([mine_ref[...], other_ref[...]], axis=0)
-    size = FOLDS * CORES * each
-    row = iota((planes * size, 1), 0)
-    d, part, at = row // size, lax.rem(row // (CORES * each), FOLDS), lax.rem(row, CORES * each)
-    wanted = (at // each ^ me) * rows + d * each + lax.rem(at, each)
-    total = jnp.zeros((planes * size, fold), F32)
-    for f in range(FOLDS):
-        pick = one_hot(jnp.where(part == f, wanted, -1), CORES * rows)
-        total = total + dot(pick, stacked[:, f * fold : (f + 1) * fold])
-    total = total.astype(BF16)
-    for d in range(planes):
-        outs[d][...] = total[d * size : (d + 1) * size]
-
-
-def merge_near_kernel(*refs):
-    chunks, out_ref = refs[:-1], refs[-1]
-    size, fold = chunks[0].shape
-    stacked = jnp.concatenate([chunk[...] for chunk in chunks], axis=0)
-    rows = len(chunks) * CORES * MOST
-    out = iota((SIDES * rows, 1), 0)
-    side, at = out // rows, lax.rem(out, rows)
-    d, replica, slot = at // (CORES * MOST), lax.rem(at // MOST, CORES), lax.rem(at, MOST)
-    for f in range(FOLDS):
-        wanted = d * size + ((f * CORES + replica) * SIDES + side) * MOST + slot
-        picked = dot(one_hot(wanted, len(chunks) * size), stacked)
-        out_ref[:, f * fold : (f + 1) * fold] = picked.astype(BF16)
-
-
-def merge_far_kernel(*refs):
+    stacked = jnp.concatenate([mine_ref[...].astype(F32), other_ref[...].astype(F32)], axis=0).astype(BF16)
+    out = iota((CORES * rows, 1), 0)
+    side, replica, slot = out // (CORES * MOST), lax.rem(out // MOST, CORES), lax.rem(out, MOST)
+    picked = dot(one_hot((replica ^ me) * rows + side * MOST + slot, CORES * rows), stacked)
+    folds = [picked[:, f * fold : (f + 1) * fold] for f in range(FOLDS)]
+    out_ref[...] = jnp.concatenate(folds, axis=0).astype(BF16)
+
+
+def merge_kernel(*refs):
     chunks, out_ref = refs[:-1], refs[-1]
     me = lax.axis_index("dp")
-    planes, (size, fold) = len(chunks) // CORES, chunks[0].shape
+    planes, size = len(chunks) // CORES, chunks[0].shape[0]
     stacked = jnp.concatenate([chunk[...] for chunk in chunks], axis=0)
     rows = planes * CORES * MOST
-    out = iota((SIDES * rows, 1), 0)
-    side, at = out // rows, lax.rem(out, rows)
+    out = iota((out_ref.shape[0], 1), 0)
+    f, side, at = out // (SIDES * rows), lax.rem(out // rows, SIDES), lax.rem(out, rows)
     d, replica, slot = at // (CORES * MOST), lax.rem(at // MOST, CORES), lax.rem(at, MOST)
     q = replica ^ me
-    first = (q * planes + d) * size + (q * FOLDS * SIDES + side) * MOST + slot
-    for f in range(FOLDS):
-        picked = dot(one_hot(first + f * SIDES * MOST, len(chunks) * size), stacked)
-        out_ref[:, f * fold : (f + 1) * fold] = picked.astype(BF16)
+    wanted = (q * planes + d) * size + ((q * FOLDS + f) * SIDES + side) * MOST + slot
+    out_ref[...] = dot(one_hot(wanted, len(chunks) * size), stacked).astype(BF16)
 
 
 def partial_kernel(*refs):
     blocks, (gate_ref, up_ref, down_ref, out_ref), sided = refs[:SPLIT], refs[SPLIT:-2], refs[-2:]
-    each, width = blocks[0].shape[0], gate_ref.shape[1]
-    rows = each // SIDES
+    (each, fold), width = blocks[0].shape, gate_ref.shape[1]
+    rows = each // (FOLDS * SIDES)
     stacked = jnp.concatenate([block[...] for block in blocks], axis=0)
     at = iota((SPLIT * rows, 1), 0)
     block = near(at // rows, lax.axis_index("dp"))
     for side in range(SIDES):
-        wanted = block * each + side * rows + lax.rem(at, rows)
-        sided[side][...] = dot(one_hot(wanted, SPLIT * each), stacked).astype(BF16)
+        for f in range(FOLDS):
+            wanted = (f * SIDES + side) * rows + lax.rem(at, rows)
+            if SPLIT * each <= 1024:
+                picked = dot(one_hot(block * each + wanted, SPLIT * each), stacked)
+            else:
+                picked = jnp.zeros((SPLIT * rows, fold), F32)
+                for b in range(SPLIT):
+                    here = jnp.where(block == b, wanted, -1)
+                    picked = picked + dot(one_hot(here, each), blocks[b][...])
+            sided[side][:, f * fold : (f + 1) * fold] = picked.astype(BF16)
     out_ref[:, :width] = dot(sided[0][...], gate_ref[...])
     out_ref[:, width : 2 * width] = dot(sided[0][...], up_ref[...])
     out_ref[:, 2 * width :] = dot(sided[1][...], down_ref[...])
@@ -189,8 +174,10 @@
     across = ((1,), (1,))
     at = iota((SPLIT * rows, 1), 0)
     k = near(at // rows, lax.axis_index("dp"))
-    group, row = lax.rem(at, rows) // (rows // GROUPS), lax.rem(at, rows // GROUPS)
-    order = one_hot(((GROUPS - 1 - group) * SPLIT + k) * (rows // GROUPS) + row, SPLIT * rows)
+    each, row = CORES * MOST, lax.rem(at, rows)
+    others = rows - each
+    source = jnp.where(row < each, SPLIT * others + k * each + row, k * others + row - each)
+    order = one_hot(source, SPLIT * rows)
     gate_side, up_side = dot(order, gate_side).astype(BF16), dot(order, up_side).astype(BF16)
     part = dot(gate_side, gate_ref[...], across) + dot(up_side, up_ref[...], across)
     each, fold = rows // GROUPS, parts[0].shape[1]
@@ -296,7 +283,7 @@
             out_shape=out_shape,
             in_specs=[vmem] * len(operands),
             out_specs=jax.tree.map(lambda _: vmem, out_shape),
-            compiler_params=params(),
+            compiler_params=params(min(60, 4 * live)),
             cost_estimate=cost(flops, moved) if flops else None,
             name=name,
         )(*operands)
@@ -316,14 +303,14 @@
         return lax.ppermute(array, ("expert", "dp"), hop)
 
     size = FOLDS * CORES * SIDES * MOST
-    near_rows = like((planes * SIDES * MOST, half), BF16)
+    own_rows = like((SIDES * MOST, half), BF16)
     mine, other, *far, hot = pl.pallas_call(
         functools.partial(gather_kernel, live),
-        out_shape=[near_rows] * CORES
-        + [like((size, fold), BF16)] * (live - planes)
+        out_shape=[own_rows] * CORES
+        + [like((size, fold), BF16)] * (live - 1)
         + [like((live * 8, tokens), F32)],
         in_specs=[hbm] * 5,
-        out_specs=[vmem] * (CORES + live - planes + 1),
+        out_specs=[vmem] * (CORES + live),
         scratch_shapes=[
             pltpu.VMEM((TOP, tokens), jnp.int32),
             pltpu.VMEM((TOP, tokens), jnp.int32),
@@ -335,31 +322,27 @@
         compiler_params=params(FIRST_MIB),
         name="gather_rows",
     )(routes.T, keep_mask.T, gate_values.T, layer_input, out_grad)
-    far = [along_z(chunk, planes + d) for d, chunk in enumerate(far)]
-    near_chunks = call(
-        functools.partial(chunk_kernel, planes),
-        "chunk_rows",
-        [like((size, fold), BF16)] * planes,
-        [mine, swap_cores(other)],
-        1e10,
-        2e7,
-    )
-    near_chunks = [near_chunks[0]] + [along_z(near_chunks[d], d) for d in range(1, planes)]
+    moved = {d: along_z(far[d - 1], d) for d in [*range(2, live), 1]}
+    far = [moved[d] for d in range(1, live)]
     mines, others, xs, ss = [], [], [], []
-    rows_in_group = total // GROUPS
-    for group in reversed(range(GROUPS)):
-        here = far + [swap_cores(chunk) for chunk in far] if group else near_chunks
+    first = second = across = rows_here = None
+    for group in range(GROUPS):
+        count = live - 1 if group else 1
+        rows_in_group = SPLIT * CORES * MOST * count
+        rows_in = far + [swap_cores(chunk) for chunk in far] if group else [mine, swap_cores(other)]
+        if group:
+            rows_in = lax.optimization_barrier((rows_in, (second, across)))[0]
         rows_here = call(
-            merge_far_kernel if group else merge_near_kernel,
+            merge_kernel if group else own_kernel,
             "merge_rows",
-            like((SIDES * rows // GROUPS, half), BF16),
-            here,
-            1e8,
+            like((size * count, fold), BF16),
+            rows_in,
+            1e8 if group else OWN_COST,
             1e6,
         )
         first, second = in_plane(rows_here, 1), in_plane(rows_here, 2)
         across = in_plane(first, 2)
-        mine, x, s = call(
+        product, x, s = call(
             partial_kernel,
             "partial_products",
             [like((rows_in_group, 3 * width), F32)] + [like((rows_in_group, half), BF16)] * SIDES,
@@ -367,10 +350,11 @@
             6 * rows_in_group * half * width,
             6 * half * width,
         )
-        mines.append(mine)
-        others.append(swap_cores(mine))
+        mines.append(product)
+        others.append(swap_cores(product))
         xs.append(x)
         ss.append(s)
+    mines, others, xs, ss = mines[::-1], others[::-1], xs[::-1], ss[::-1]
     sided = call(
         sides_kernel,
         "sides_and_parts",

time: 56.2 us -> 62.7 us (1.12)
  waiting for transfers between devices: 17.5 us -> 21.3 us
  starting transfers between devices: 24.6 us -> 27.2 us
    ppermute x12, waiting for transfers between devices: 7.97 us -> 15.5 us  [in_plane(): return lax.ppermute(array, ('expert', 'dp'), hop)]
    ppermute x6, waiting for transfers between devices: 6.59 us -> 3.54 us  [along_z(): return lax.ppermute(array, 'expert', hop)]
    ppermute x6, starting transfers between devices: 8.74 us -> 9.9 us  [along_z(): return lax.ppermute(array, 'expert', hop)]
    ppermute x7 -> x8, starting transfers between devices: 0.81 us -> 1.82 us  [swap_cores(): return lax.ppermute(array, 'dp', [(r, r ^ 1) for r in range(CORES)])]
    ppermute x7 -> x8, waiting for transfers between devices: 2.9 us -> 2.29 us  [swap_cores(): return lax.ppermute(array, 'dp', [(r, r ^ 1) for r in range(CORES)])]
    pallas_call x11 -> x10, Pallas kernels: 7.14 us -> 7.17 us  [call(): pl.pallas_call(kernel, out_shape=out_shape, in_specs=[vmem] * len(operand...]
  transfers between devices with their start and end apart: 25 -> 26, of which waited for: 16 -> 10; matrix products, arithmetic and copies ran while one was open for 0% -> 0% of each run, Pallas kernels for 12% -> 8%
where the time goes in v3:
time: 62.7 us; the launch traced here: 62.5 us
  starting transfers between devices  27.2 us (43%)
  waiting for transfers between devices  21.3 us (34%)
  Pallas kernels  12.3 us (20%)
  local copies, waits for them, and re-layouts  0.83 us (1%)
  between operations  0.8 us (1%)
    ppermute x12, waiting for transfers between devices, in_plane(): return lax.ppermute(array, ('expert', 'dp'), hop)  15.5 us
    ppermute x12, starting transfers between devices, in_plane(): return lax.ppermute(array, ('expert', 'dp'), hop)  15.4 us
    ppermute x6, starting transfers between devices, along_z(): return lax.ppermute(array, 'expert', hop)  9.9 us
    pallas_call x10, Pallas kernels, call(): pl.pallas_call(kernel, out_shape=out_shape, in_specs=[vmem] * len(operand...  7.17 us
    ppermute x6, waiting for transfers between devices, along_z(): return lax.ppermute(array, 'expert', hop)  3.54 us
    pallas_call x1, Pallas kernels, body(): pl.pallas_call(functools.partial(gather_kernel, live), out_shape=[own_row...  2.66 us
    pallas_call x1, Pallas kernels, body(): pl.pallas_call(grads_kernel, out_shape=[like((half, width), BF16)] * 3 +...  2.5 us
    ppermute x8, waiting for transfers between devices, swap_cores(): return lax.ppermute(array, 'dp', [(r, r ^ 1) for r in range(CORES)])  2.29 us
  transfers between devices with their start and end apart: 26, of which 10 were waited for; matrix products, arithmetic and copies ran while one was open for 0% of the time, Pallas kernels for 8%

profile of v3, /device:TPU:0, one launch (start us, length us, event | category | flops | bytes accessed | tf_op | source)
XLA Modules:
  0.0 62.5 jit_solution(6167210177734672343)
XLA Ops:
  0.6 2.7 %gather_rows.1 = (bf16[10,1792]{1,0:T(8,128)(2,1)}, bf16[10,1792]{1,0:T(8,128)(2,1)}, bf16[40,896]{1,0:T(8,128)(2,1)}, bf16[40,896]{1,0:T(8,128)(2,1)}, bf16[40,896]{1,0:T(8,128)(2,1)}, /*index=5*/f32[32,128]{1,0:T(8,128)}) custom-call(s32[8,128]{1,0:T(8,128)} %bitcast.3, s32[8,128]{1,0:T(8,128)} %bitcast.4, f32[8,128]{1,0:T(8,128)} %bitcast.5, ...), custom_call_target="tpu_custom_call" | custom-call | tf_op jit(solution)/shard_map/gather_rows/pallas_call | solution.py:307
  3.3 0.5 collective-permute-start.6
  3.8 2.6 %collective-permute-start = (bf16[40,896]{1,0:T(8,128)(2,1)}, bf16[40,896]{1,0:T(8,128)(2,1)S(1)}, u32[]{:S(2)}, u32[]{:S(2)}) collective-permute-start(bf16[40,896]{1,0:T(8,128)(2,1)} %get-tuple-element.44), channel_id=1, source_target_pairs={{0,8},{2,10},{4,12},{6,14},{8,0},{10,2},{12,4},{14,6},{16,24},{18,... | collective-permute-start | bytes 215048 | tf_op jit(solution)/shard_map/ppermute | solution.py:296
  6.5 2.6 %collective-permute-start.1 = (bf16[40,896]{1,0:T(8,128)(2,1)}, bf16[40,896]{1,0:T(8,128)(2,1)S(1)}, u32[]{:S(2)}, u32[]{:S(2)}) collective-permute-start(bf16[40,896]{1,0:T(8,128)(2,1)} %get-tuple-element.45), channel_id=1, source_target_pairs={{0,16},{2,18},{4,20},{6,22},{8,24},{10,26},{12,28},{14,30},{16,0},... | collective-permute-start | bytes 215048 | tf_op jit(solution)/shard_map/ppermute | solution.py:296
  9.1 0.0 collective-permute-start.2
  9.1 0.0 collective-permute-done.6.other_ref
  9.1 0.8 %copy-done.4 = bf16[10,1792]{1,0:T(8,128)(2,1)S(1)} copy-done((bf16[10,1792]{1,0:T(8,128)(2,1)S(1)}, bf16[10,1792]{1,0:T(8,128)(2,1)}, u32[]{:S(2)}) %copy-start.4) | copy-done | bytes 35864
  9.9 0.2 merge_rows.2.refs_0_
  10.1 1.8 %collective-permute-start.8 = (bf16[40,896]{1,0:T(8,128)(2,1)S(1)}, bf16[40,896]{1,0:T(8,128)(2,1)S(1)}, u32[]{:S(2)}, u32[]{:S(2)}) collective-permute-start(bf16[40,896]{1,0:T(8,128)(2,1)S(1)} %merge_rows.2.refs_0_), channel_id=1, source_target_pairs={{0,2},{1,5},{2,0},{3,7},{4,6},{5,1},{6,4},{7,3},{8,10},{9,13},{10,... | collective-permute-start | bytes 215048 | tf_op jit(solution)/shard_map/ppermute | solution.py:303
  11.9 1.5 %collective-permute-start.7 = (bf16[40,896]{1,0:T(8,128)(2,1)S(1)}, bf16[40,896]{1,0:T(8,128)(2,1)S(1)}, u32[]{:S(2)}, u32[]{:S(2)}) collective-permute-start(bf16[40,896]{1,0:T(8,128)(2,1)S(1)} %merge_rows.2.refs_0_), channel_id=1, source_target_pairs={{0,4},{1,3},{2,6},{3,1},{4,0},{5,7},{6,2},{7,5},{8,12},{9,11},{10,... | collective-permute-start | bytes 215048 | tf_op jit(solution)/shard_map/ppermute | solution.py:303
  13.4 0.0 collective-permute-done.refs_0_
  13.4 0.0 collective-permute-start.3
  13.4 2.1 %collective-permute-done.1.refs_1_ = bf16[40,896]{1,0:T(8,128)(2,1)S(1)} collective-permute-done((bf16[40,896]{1,0:T(8,128)(2,1)}, bf16[40,896]{1,0:T(8,128)(2,1)S(1)}, u32[]{:S(2)}, u32[]{:S(2)}) %collective-permute-start.1) | collective-permute-done | bytes 71712 | tf_op jit(solution)/shard_map/ppermute | solution.py:296
  15.4 0.0 collective-permute-start.4
  15.5 0.0 collective-permute-done.2.refs_2_
  15.5 0.5 collective-permute-start.5
  16.0 0.0 collective-permute-done.8.refs_1_
  16.0 1.5 %collective-permute-start.9 = (bf16[40,896]{1,0:T(8,128)(2,1)S(1)}, bf16[40,896]{1,0:T(8,128)(2,1)S(1)}, u32[]{:S(2)}, u32[]{:S(2)}) collective-permute-start(bf16[40,896]{1,0:T(8,128)(2,1)S(1)} %collective-permute-done.8.refs_1_), channel_id=1, source_target_pairs={{0,4},{1,3},{2,6},{3,1},{4,0},{5,7},{6,2},{7,5},{8,12},{9,11},{10,... | collective-permute-start | bytes 215048 | tf_op jit(solution)/shard_map/ppermute | solution.py:303
  17.5 0.0 collective-permute-done.7.refs_2_
  17.5 0.0 collective-permute-done.3.refs_3_
  17.5 0.0 collective-permute-done.4.refs_4_
  17.5 0.0 collective-permute-done.5.refs_5_
  17.5 2.8 %collective-permute-done.9.refs_3_ = bf16[40,896]{1,0:T(8,128)(2,1)S(1)} collective-permute-done((bf16[40,896]{1,0:T(8,128)(2,1)S(1)}, bf16[40,896]{1,0:T(8,128)(2,1)S(1)}, u32[]{:S(2)}, u32[]{:S(2)}) %collective-permute-start.9) | collective-permute-done | bytes 71712 | tf_op jit(solution)/shard_map/ppermute | solution.py:303
  20.3 0.3 merge_rows.3.refs_0_
  20.6 1.6 %collective-permute-start.10 = (bf16[120,896]{1,0:T(8,128)(2,1)S(1)}, bf16[120,896]{1,0:T(8,128)(2,1)S(1)}, u32[]{:S(2)}, u32[]{:S(2)}) collective-permute-start(bf16[120,896]{1,0:T(8,128)(2,1)S(1)} %merge_rows.3.refs_0_), channel_id=1, source_target_pairs={{0,2},{1,5},{2,0},{3,7},{4,6},{5,1},{6,4},{7,3},{8,10},{9,13},{10,... | collective-permute-start | bytes 645128 | tf_op jit(solution)/shard_map/ppermute | solution.py:303
  22.2 1.5 %collective-permute-start.11 = (bf16[120,896]{1,0:T(8,128)(2,1)S(1)}, bf16[120,896]{1,0:T(8,128)(2,1)S(1)}, u32[]{:S(2)}, u32[]{:S(2)}) collective-permute-start(bf16[120,896]{1,0:T(8,128)(2,1)S(1)} %merge_rows.3.refs_0_), channel_id=1, source_target_pairs={{0,4},{1,3},{2,6},{3,1},{4,0},{5,7},{6,2},{7,5},{8,12},{9,11},{10,... | collective-permute-start | bytes 645128 | tf_op jit(solution)/shard_map/ppermute | solution.py:303
  23.7 5.1 %collective-permute-done.10.refs_1_ = bf16[120,896]{1,0:T(8,128)(2,1)S(1)} collective-permute-done((bf16[120,896]{1,0:T(8,128)(2,1)S(1)}, bf16[120,896]{1,0:T(8,128)(2,1)S(1)}, u32[]{:S(2)}, u32[]{:S(2)}) %collective-permute-start.10) | collective-permute-done | bytes 215072 | tf_op jit(solution)/shard_map/ppermute | solution.py:303
  28.8 0.0 collective-permute-start.12
  28.8 0.0 collective-permute-done.11.refs_2_
  28.8 5.9 %collective-permute-done.12.refs_3_ = bf16[120,896]{1,0:T(8,128)(2,1)S(1)} collective-permute-done((bf16[120,896]{1,0:T(8,128)(2,1)S(1)}, bf16[120,896]{1,0:T(8,128)(2,1)S(1)}, u32[]{:S(2)}, u32[]{:S(2)}) %collective-permute-start.12) | collective-permute-done | bytes 215072 | tf_op jit(solution)/shard_map/ppermute | solution.py:303
  34.7 1.4 %partial_products.2 = (f32[120,1152]{1,0:T(8,128)S(1)}, bf16[120,1792]{1,0:T(8,128)(2,1)S(1)}, bf16[120,1792]{1,0:T(8,128)(2,1)S(1)}) custom-call(bf16[120,896]{1,0:T(8,128)(2,1)S(1)} %merge_rows.3.refs_0_, bf16[120,896]{1,0:T(8,128)(2,1)S(1)} %collective-permute-done.10.refs_1_, bf16[120,896]{1,0:T(8,128)(2,1)S(1)} %collective-permute-done.11.refs_2_, ...), custom_call_target="tpu_custom_call" | custom-call | flops 495452160 | bytes 4128768 | tf_op jit(solution)/shard_map/partial_products/pallas_call | solution.py:281
  36.2 0.1 collective-permute-start.13
  36.2 0.9 %partial_products.3 = (f32[40,1152]{1,0:T(8,128)S(1)}, bf16[40,1792]{1,0:T(8,128)(2,1)S(1)}, bf16[40,1792]{1,0:T(8,128)(2,1)S(1)}) custom-call(bf16[40,896]{1,0:T(8,128)(2,1)S(1)} %merge_rows.2.refs_0_, bf16[40,896]{1,0:T(8,128)(2,1)S(1)} %collective-permute-done.8.refs_1_, bf16[40,896]{1,0:T(8,128)(2,1)S(1)} %collective-permute-done.7.refs_2_, ...), custom_call_target="tpu_custom_call" | custom-call | flops 165150720 | bytes 4128768 | tf_op jit(solution)/shard_map/partial_products/pallas_call | solution.py:281
  37.2 0.6 collective-permute-start.14
  37.8 1.1 %collective-permute-done.14.refs_3_ = f32[40,1152]{1,0:T(8,128)S(1)} collective-permute-done((f32[40,1152]{1,0:T(8,128)S(1)}, f32[40,1152]{1,0:T(8,128)S(1)}, u32[]{:S(2)}, u32[]{:S(2)}) %collective-permute-start.14) | collective-permute-done | bytes 184352 | tf_op jit(solution)/shard_map/ppermute | solution.py:292
  38.8 0.0 collective-permute-done.13.refs_2_
  38.8 1.4 %sides_and_parts.1 = (bf16[40,896]{1,0:T(8,128)(2,1)S(1)}, bf16[40,896]{1,0:T(8,128)(2,1)S(1)}, bf16[40,896]{1,0:T(8,128)(2,1)S(1)}, bf16[40,896]{1,0:T(8,128)(2...) custom-call(f32[120,1152]{1,0:T(8,128)S(1)} %get-tuple-element.55.re, ...), custom_call_target="tpu_custom_call" | custom-call | flops 440401920 | bytes 2752512 | tf_op jit(solution)/shard_map/sides_and_parts/pallas_call | solution.py:281
  40.2 1.0 %collective-permute-start.15 = (bf16[40,896]{1,0:T(8,128)(2,1)S(1)}, bf16[40,896]{1,0:T(8,128)(2,1)S(1)}, u32[]{:S(2)}, u32[]{:S(2)}) collective-permute-start(bf16[40,896]{1,0:T(8,128)(2,1)S(1)} %get-tuple-element.58), channel_id=1, source_target_pairs={{0,6},{1,7},{2,4},{3,5},{4,2},{5,3},{6,0},{7,1},{8,14},{9,15},{10,... | collective-permute-start | bytes 215048 | tf_op jit(solution)/shard_map/ppermute | solution.py:303
  41.2 2.0 %collective-permute-start.16 = (bf16[40,896]{1,0:T(8,128)(2,1)S(1)}, bf16[40,896]{1,0:T(8,128)(2,1)S(1)}, u32[]{:S(2)}, u32[]{:S(2)}) collective-permute-start(bf16[40,896]{1,0:T(8,128)(2,1)S(1)} %get-tuple-element.59), channel_id=1, source_target_pairs={{0,4},{1,3},{2,6},{3,1},{4,0},{5,7},{6,2},{7,5},{8,12},{9,11},{10,... | collective-permute-start | bytes 215048 | tf_op jit(solution)/shard_map/ppermute | solution.py:303
  43.2 0.5 collective-permute-start.17
  43.8 0.9 %collective-permute-start.19 = (bf16[40,896]{1,0:T(8,128)(2,1)S(1)}, bf16[40,896]{1,0:T(8,128)(2,1)S(1)}, u32[]{:S(2)}, u32[]{:S(2)}) collective-permute-start(bf16[40,896]{1,0:T(8,128)(2,1)S(1)} %get-tuple-element.65), channel_id=1, source_target_pairs={{0,6},{1,7},{2,4},{3,5},{4,2},{5,3},{6,0},{7,1},{8,14},{9,15},{10,... | collective-permute-start | bytes 215048 | tf_op jit(solution)/shard_map/ppermute | solution.py:303
  44.7 2.0 %collective-permute-start.20 = (bf16[40,896]{1,0:T(8,128)(2,1)S(1)}, bf16[40,896]{1,0:T(8,128)(2,1)S(1)}, u32[]{:S(2)}, u32[]{:S(2)}) collective-permute-start(bf16[40,896]{1,0:T(8,128)(2,1)S(1)} %get-tuple-element.66), channel_id=1, source_target_pairs={{0,4},{1,3},{2,6},{3,1},{4,0},{5,7},{6,2},{7,5},{8,12},{9,11},{10,... | collective-permute-start | bytes 215048 | tf_op jit(solution)/shard_map/ppermute | solution.py:303
  46.7 0.0 collective-permute-done.15.refs_1_
  46.7 1.0 %collective-permute-start.21 = (bf16[40,896]{1,0:T(8,128)(2,1)S(1)}, bf16[40,896]{1,0:T(8,128)(2,1)S(1)}, u32[]{:S(2)}, u32[]{:S(2)}) collective-permute-start(bf16[40,896]{1,0:T(8,128)(2,1)S(1)} %get-tuple-element.67), channel_id=1, source_target_pairs={{0,2},{1,5},{2,0},{3,7},{4,6},{5,1},{6,4},{7,3},{8,10},{9,13},{10,... | collective-permute-start | bytes 215048 | tf_op jit(solution)/shard_map/ppermute | solution.py:303
  47.8 0.0 collective-permute-done.16.refs_2_
  47.8 0.6 collective-permute-done.17.refs_3_
  48.3 0.5 sum_parts.2
  48.8 1.1 %collective-permute-start.18 = (bf16[140,128]{1,0:T(8,128)(2,1)S(1)}, bf16[140,128]{1,0:T(8,128)(2,1)S(1)}, u32[]{:S(2)}, u32[]{:S(2)}) collective-permute-start(bf16[140,128]{1,0:T(8,128)(2,1)S(1)} %get-tuple-element.62), channel_id=1, source_target_pairs={{0,8},{2,10},{4,12},{6,14},{8,0},{10,2},{12,4},{14,6},{16,24},{18,... | collective-permute-start | bytes 107528 | tf_op jit(solution)/shard_map/ppermute | solution.py:296
  49.9 0.0 collective-permute-done.19.refs_1_
  49.9 0.4 collective-permute-done.20.refs_2_
  50.3 0.8 %collective-permute-done.21.refs_3_ = bf16[40,896]{1,0:T(8,128)(2,1)S(1)} collective-permute-done((bf16[40,896]{1,0:T(8,128)(2,1)S(1)}, bf16[40,896]{1,0:T(8,128)(2,1)S(1)}, u32[]{:S(2)}, u32[]{:S(2)}) %collective-permute-start.21) | collective-permute-done | bytes 71712 | tf_op jit(solution)/shard_map/ppermute | solution.py:303
  51.1 0.5 sum_parts.3
  51.5 2.2 %collective-permute-start.22 = (bf16[140,128]{1,0:T(8,128)(2,1)S(1)}, bf16[140,128]{1,0:T(8,128)(2,1)S(1)}, u32[]{:S(2)}, u32[]{:S(2)}) collective-permute-start(bf16[140,128]{1,0:T(8,128)(2,1)S(1)} %get-tuple-element.68), channel_id=1, source_target_pairs={{0,16},{2,18},{4,20},{6,22},{8,24},{10,26},{12,28},{14,30},{16,0},... | collective-permute-start | bytes 107528 | tf_op jit(solution)/shard_map/ppermute | solution.py:296
  53.7 1.4 %collective-permute-start.23 = (bf16[140,128]{1,0:T(8,128)(2,1)S(1)}, bf16[140,128]{1,0:T(8,128)(2,1)S(1)}, u32[]{:S(2)}, u32[]{:S(2)}) collective-permute-start(bf16[140,128]{1,0:T(8,128)(2,1)S(1)} %get-tuple-element.69), channel_id=1, source_target_pairs={{0,24},{2,26},{4,28},{6,30},{8,16},{10,18},{12,20},{14,22},{16,8},... | collective-permute-start | bytes 107528 | tf_op jit(solution)/shard_map/ppermute | solution.py:296
  55.1 2.5 %weight_grads.1 = (bf16[1792,384]{1,0:T(8,128)(2,1)}, bf16[1792,384]{1,0:T(8,128)(2,1)}, bf16[1792,384]{1,0:T(8,128)(2,1)}, f32[8,128]{1,0:T(8,128)S(1)}) custom-call(bf16[120,1792]{1,0:T(8,128)(2,1)S(1)} %get-tuple-element.70.refs_0_, bf16[40,1792]{1,0:T(8,128)(2,1)S(1)} %get-tuple-element.71.refs_1_, bf16[120,1792]{1,0:T(8,128)(2,1)S(1)} %get-tuple-element.72.refs_2_, ...), custom_call_target="tpu_custom_call" | custom-call | flops 660602880 | bytes 5275648 | tf_op jit(solution)/shard_map/weight_grads/pallas_call | solution.py:371
  57.6 0.0 collective-permute-done.18.refs_1_
  57.6 0.3 split_rows.2
  58.0 0.1 collective-permute-start.24
  58.0 1.5 %collective-permute-done.23.refs_1_ = bf16[140,128]{1,0:T(8,128)(2,1)S(1)} collective-permute-done((bf16[140,128]{1,0:T(8,128)(2,1)S(1)}, bf16[140,128]{1,0:T(8,128)(2,1)S(1)}, u32[]{:S(2)}, u32[]{:S(2)}) %collective-permute-start.23) | collective-permute-done | bytes 35872 | tf_op jit(solution)/shard_map/ppermute | solution.py:296
  59.5 0.3 split_rows.3
  59.8 0.1 collective-permute-start.25
  59.9 0.0 collective-permute-done.24.refs_2_
  59.9 1.2 %collective-permute-done.25.refs_3_ = bf16[16,1792]{1,0:T(8,128)(2,1)S(1)} collective-permute-done((bf16[16,1792]{1,0:T(8,128)(2,1)S(1)}, bf16[16,1792]{1,0:T(8,128)(2,1)S(1)}, u32[]{:S(2)}, u32[]{:S(2)}) %collective-permute-start.25) | collective-permute-done | bytes 57376 | tf_op jit(solution)/shard_map/ppermute | solution.py:292
  61.1 1.3 %place_rows.1 = bf16[128,3584]{1,0:T(8,128)(2,1)} custom-call(f32[32,128]{1,0:T(8,128)S(1)} %copy-done.3, bf16[16,1792]{1,0:T(8,128)(2,1)S(1)} %get-tuple-element.63.refs_0_, bf16[16,1792]{1,0:T(8,128)(2,1)S(1)} %get-tuple-element.76.refs_1_, bf16[16,1792]{1,0:T(8,128)(2,1)S(1)} %collective-permute-done.24.refs_2_, ...), custom_call_target="tpu_custom_call" | custom-call | tf_op jit(solution)/shard_map/place_rows/pallas_call | solution.py:281
  (10 shorter events, 0.0 us)
Async XLA Ops:
  3.3 5.8 %collective-permute-start.6 = (bf16[10,1792]{1,0:T(8,128)(2,1)}, bf16[10,1792]{1,0:T(8,128)(2,1)S(1)}, u32[]{:S(2)}, u32[]{:S(2)}) collective-permute-start(bf16[10,1792]{1,0:T(8,128)(2,1)} %get-tuple-element.48), channel_id=1, source_target_pairs={{0,1},{1,0},{2,3},{3,2},{4,5},{5,4},{6,7},{7,6},{8,9},{9,8},{10,11... | collective-permute-start | bytes 107528 | tf_op jit(solution)/shard_map/ppermute | solution.py:292
  3.8 9.6 %collective-permute-start = (bf16[40,896]{1,0:T(8,128)(2,1)}, bf16[40,896]{1,0:T(8,128)(2,1)S(1)}, u32[]{:S(2)}, u32[]{:S(2)}) collective-permute-start(bf16[40,896]{1,0:T(8,128)(2,1)} %get-tuple-element.44), channel_id=1, source_target_pairs={{0,8},{2,10},{4,12},{6,14},{8,0},{10,2},{12,4},{14,6},{16,24},{18,... | collective-permute-start | bytes 215048 | tf_op jit(solution)/shard_map/ppermute | solution.py:296
  6.5 9.0 %collective-permute-start.1 = (bf16[40,896]{1,0:T(8,128)(2,1)}, bf16[40,896]{1,0:T(8,128)(2,1)S(1)}, u32[]{:S(2)}, u32[]{:S(2)}) collective-permute-start(bf16[40,896]{1,0:T(8,128)(2,1)} %get-tuple-element.45), channel_id=1, source_target_pairs={{0,16},{2,18},{4,20},{6,22},{8,24},{10,26},{12,28},{14,30},{16,0},... | collective-permute-start | bytes 215048 | tf_op jit(solution)/shard_map/ppermute | solution.py:296
  9.1 6.4 %collective-permute-start.2 = (bf16[40,896]{1,0:T(8,128)(2,1)}, bf16[40,896]{1,0:T(8,128)(2,1)S(1)}, u32[]{:S(2)}, u32[]{:S(2)}) collective-permute-start(bf16[40,896]{1,0:T(8,128)(2,1)} %get-tuple-element.46), channel_id=1, source_target_pairs={{0,24},{2,26},{4,28},{6,30},{8,16},{10,18},{12,20},{14,22},{16,8},... | collective-permute-start | bytes 215048 | tf_op jit(solution)/shard_map/ppermute | solution.py:296
  9.1 0.8 %copy-start.4 = (bf16[10,1792]{1,0:T(8,128)(2,1)S(1)}, bf16[10,1792]{1,0:T(8,128)(2,1)}, u32[]{:S(2)}) copy-start(bf16[10,1792]{1,0:T(8,128)(2,1)} %get-tuple-element.47.mine_ref) | copy-start | bytes 107524
  9.9 24.8 %copy-start = (bf16[1792,384]{1,0:T(8,128)(2,1)S(1)}, bf16[1792,384]{1,0:T(8,128)(2,1)}, u32[]{:S(2)}) copy-start(bf16[1792,384]{1,0:T(8,128)(2,1)} %refs_4_.7) | copy-start | bytes 4128772
  9.9 24.8 %copy-start.1 = (bf16[1792,384]{1,0:T(8,128)(2,1)S(1)}, bf16[1792,384]{1,0:T(8,128)(2,1)}, u32[]{:S(2)}) copy-start(bf16[1792,384]{1,0:T(8,128)(2,1)} %refs_5_.5) | copy-start | bytes 4128772
  9.9 24.8 %copy-start.2 = (bf16[1792,384]{1,0:T(8,128)(2,1)S(1)}, bf16[1792,384]{1,0:T(8,128)(2,1)}, u32[]{:S(2)}) copy-start(bf16[1792,384]{1,0:T(8,128)(2,1)} %refs_6_.3) | copy-start | bytes 4128772
  10.1 5.9 %collective-permute-start.8 = (bf16[40,896]{1,0:T(8,128)(2,1)S(1)}, bf16[40,896]{1,0:T(8,128)(2,1)S(1)}, u32[]{:S(2)}, u32[]{:S(2)}) collective-permute-start(bf16[40,896]{1,0:T(8,128)(2,1)S(1)} %merge_rows.2.refs_0_), channel_id=1, source_target_pairs={{0,2},{1,5},{2,0},{3,7},{4,6},{5,1},{6,4},{7,3},{8,10},{9,13},{10,... | collective-permute-start | bytes 215048 | tf_op jit(solution)/shard_map/ppermute | solution.py:303
  11.9 5.6 %collective-permute-start.7 = (bf16[40,896]{1,0:T(8,128)(2,1)S(1)}, bf16[40,896]{1,0:T(8,128)(2,1)S(1)}, u32[]{:S(2)}, u32[]{:S(2)}) collective-permute-start(bf16[40,896]{1,0:T(8,128)(2,1)S(1)} %merge_rows.2.refs_0_), channel_id=1, source_target_pairs={{0,4},{1,3},{2,6},{3,1},{4,0},{5,7},{6,2},{7,5},{8,12},{9,11},{10,... | collective-permute-start | bytes 215048 | tf_op jit(solution)/shard_map/ppermute | solution.py:303
  13.4 4.1 %collective-permute-start.3 = (bf16[40,896]{1,0:T(8,128)(2,1)S(1)}, bf16[40,896]{1,0:T(8,128)(2,1)S(1)}, u32[]{:S(2)}, u32[]{:S(2)}) collective-permute-start(bf16[40,896]{1,0:T(8,128)(2,1)S(1)} %collective-permute-done.refs_0_), channel_id=1, source_target_pairs={{0,1},{1,0},{2,3},{3,2},{4,5},{5,4},{6,7},{7,6},{8,9},{9,8},{10,11... | collective-permute-start | bytes 215048 | tf_op jit(solution)/shard_map/ppermute | solution.py:292
  15.4 2.0 %collective-permute-start.4 = (bf16[40,896]{1,0:T(8,128)(2,1)S(1)}, bf16[40,896]{1,0:T(8,128)(2,1)S(1)}, u32[]{:S(2)}, u32[]{:S(2)}) collective-permute-start(bf16[40,896]{1,0:T(8,128)(2,1)S(1)} %collective-permute-done.1.refs_1_), channel_id=1, source_target_pairs={{0,1},{1,0},{2,3},{3,2},{4,5},{5,4},{6,7},{7,6},{8,9},{9,8},{10,11... | collective-permute-start | bytes 215048 | tf_op jit(solution)/shard_map/ppermute | solution.py:292
  15.5 2.0 %collective-permute-start.5 = (bf16[40,896]{1,0:T(8,128)(2,1)S(1)}, bf16[40,896]{1,0:T(8,128)(2,1)S(1)}, u32[]{:S(2)}, u32[]{:S(2)}) collective-permute-start(bf16[40,896]{1,0:T(8,128)(2,1)S(1)} %collective-permute-done.2.refs_2_), channel_id=1, source_target_pairs={{0,1},{1,0},{2,3},{3,2},{4,5},{5,4},{6,7},{7,6},{8,9},{9,8},{10,11... | collective-permute-start | bytes 215048 | tf_op jit(solution)/shard_map/ppermute | solution.py:292
  16.0 4.3 %collective-permute-start.9 = (bf16[40,896]{1,0:T(8,128)(2,1)S(1)}, bf16[40,896]{1,0:T(8,128)(2,1)S(1)}, u32[]{:S(2)}, u32[]{:S(2)}) collective-permute-start(bf16[40,896]{1,0:T(8,128)(2,1)S(1)} %collective-permute-done.8.refs_1_), channel_id=1, source_target_pairs={{0,4},{1,3},{2,6},{3,1},{4,0},{5,7},{6,2},{7,5},{8,12},{9,11},{10,... | collective-permute-start | bytes 215048 | tf_op jit(solution)/shard_map/ppermute | solution.py:303
  20.6 8.2 %collective-permute-start.10 = (bf16[120,896]{1,0:T(8,128)(2,1)S(1)}, bf16[120,896]{1,0:T(8,128)(2,1)S(1)}, u32[]{:S(2)}, u32[]{:S(2)}) collective-permute-start(bf16[120,896]{1,0:T(8,128)(2,1)S(1)} %merge_rows.3.refs_0_), channel_id=1, source_target_pairs={{0,2},{1,5},{2,0},{3,7},{4,6},{5,1},{6,4},{7,3},{8,10},{9,13},{10,... | collective-permute-start | bytes 645128 | tf_op jit(solution)/shard_map/ppermute | solution.py:303
  22.2 6.7 %collective-permute-start.11 = (bf16[120,896]{1,0:T(8,128)(2,1)S(1)}, bf16[120,896]{1,0:T(8,128)(2,1)S(1)}, u32[]{:S(2)}, u32[]{:S(2)}) collective-permute-start(bf16[120,896]{1,0:T(8,128)(2,1)S(1)} %merge_rows.3.refs_0_), channel_id=1, source_target_pairs={{0,4},{1,3},{2,6},{3,1},{4,0},{5,7},{6,2},{7,5},{8,12},{9,11},{10,... | collective-permute-start | bytes 645128 | tf_op jit(solution)/shard_map/ppermute | solution.py:303
  28.8 5.9 %collective-permute-start.12 = (bf16[120,896]{1,0:T(8,128)(2,1)S(1)}, bf16[120,896]{1,0:T(8,128)(2,1)S(1)}, u32[]{:S(2)}, u32[]{:S(2)}) collective-permute-start(bf16[120,896]{1,0:T(8,128)(2,1)S(1)} %collective-permute-done.10.refs_1_), channel_id=1, source_target_pairs={{0,4},{1,3},{2,6},{3,1},{4,0},{5,7},{6,2},{7,5},{8,12},{9,11},{10,... | collective-permute-start | bytes 645128 | tf_op jit(solution)/shard_map/ppermute | solution.py:303
  36.2 2.7 %collective-permute-start.13 = (f32[120,1152]{1,0:T(8,128)S(1)}, f32[120,1152]{1,0:T(8,128)S(1)}, u32[]{:S(2)}, u32[]{:S(2)}) collective-permute-start(f32[120,1152]{1,0:T(8,128)S(1)} %get-tuple-element.55.refs_0_), channel_id=1, source_target_pairs={{0,1},{1,0},{2,3},{3,2},{4,5},{5,4},{6,7},{7,6},{8,9},{9,8},{10,11... | collective-permute-start | bytes 1658888 | tf_op jit(solution)/shard_map/ppermute | solution.py:292
  37.2 1.6 %collective-permute-start.14 = (f32[40,1152]{1,0:T(8,128)S(1)}, f32[40,1152]{1,0:T(8,128)S(1)}, u32[]{:S(2)}, u32[]{:S(2)}) collective-permute-start(f32[40,1152]{1,0:T(8,128)S(1)} %get-tuple-element.56.refs_1_), channel_id=1, source_target_pairs={{0,1},{1,0},{2,3},{3,2},{4,5},{5,4},{6,7},{7,6},{8,9},{9,8},{10,11... | collective-permute-start | bytes 552968 | tf_op jit(solution)/shard_map/ppermute | solution.py:292
  40.2 6.5 %collective-permute-start.15 = (bf16[40,896]{1,0:T(8,128)(2,1)S(1)}, bf16[40,896]{1,0:T(8,128)(2,1)S(1)}, u32[]{:S(2)}, u32[]{:S(2)}) collective-permute-start(bf16[40,896]{1,0:T(8,128)(2,1)S(1)} %get-tuple-element.58), channel_id=1, source_target_pairs={{0,6},{1,7},{2,4},{3,5},{4,2},{5,3},{6,0},{7,1},{8,14},{9,15},{10,... | collective-permute-start | bytes 215048 | tf_op jit(solution)/shard_map/ppermute | solution.py:303
  41.2 6.6 %collective-permute-start.16 = (bf16[40,896]{1,0:T(8,128)(2,1)S(1)}, bf16[40,896]{1,0:T(8,128)(2,1)S(1)}, u32[]{:S(2)}, u32[]{:S(2)}) collective-permute-start(bf16[40,896]{1,0:T(8,128)(2,1)S(1)} %get-tuple-element.59), channel_id=1, source_target_pairs={{0,4},{1,3},{2,6},{3,1},{4,0},{5,7},{6,2},{7,5},{8,12},{9,11},{10,... | collective-permute-start | bytes 215048 | tf_op jit(solution)/shard_map/ppermute | solution.py:303
  43.2 5.1 %collective-permute-start.17 = (bf16[40,896]{1,0:T(8,128)(2,1)S(1)}, bf16[40,896]{1,0:T(8,128)(2,1)S(1)}, u32[]{:S(2)}, u32[]{:S(2)}) collective-permute-start(bf16[40,896]{1,0:T(8,128)(2,1)S(1)} %get-tuple-element.60), channel_id=1, source_target_pairs={{0,2},{1,5},{2,0},{3,7},{4,6},{5,1},{6,4},{7,3},{8,10},{9,13},{10,... | collective-permute-start | bytes 215048 | tf_op jit(solution)/shard_map/ppermute | solution.py:303
  43.8 6.1 %collective-permute-start.19 = (bf16[40,896]{1,0:T(8,128)(2,1)S(1)}, bf16[40,896]{1,0:T(8,128)(2,1)S(1)}, u32[]{:S(2)}, u32[]{:S(2)}) collective-permute-start(bf16[40,896]{1,0:T(8,128)(2,1)S(1)} %get-tuple-element.65), channel_id=1, source_target_pairs={{0,6},{1,7},{2,4},{3,5},{4,2},{5,3},{6,0},{7,1},{8,14},{9,15},{10,... | collective-permute-start | bytes 215048 | tf_op jit(solution)/shard_map/ppermute | solution.py:303
  44.7 5.6 %collective-permute-start.20 = (bf16[40,896]{1,0:T(8,128)(2,1)S(1)}, bf16[40,896]{1,0:T(8,128)(2,1)S(1)}, u32[]{:S(2)}, u32[]{:S(2)}) collective-permute-start(bf16[40,896]{1,0:T(8,128)(2,1)S(1)} %get-tuple-element.66), channel_id=1, source_target_pairs={{0,4},{1,3},{2,6},{3,1},{4,0},{5,7},{6,2},{7,5},{8,12},{9,11},{10,... | collective-permute-start | bytes 215048 | tf_op jit(solution)/shard_map/ppermute | solution.py:303
  46.7 4.3 %collective-permute-start.21 = (bf16[40,896]{1,0:T(8,128)(2,1)S(1)}, bf16[40,896]{1,0:T(8,128)(2,1)S(1)}, u32[]{:S(2)}, u32[]{:S(2)}) collective-permute-start(bf16[40,896]{1,0:T(8,128)(2,1)S(1)} %get-tuple-element.67), channel_id=1, source_target_pairs={{0,2},{1,5},{2,0},{3,7},{4,6},{5,1},{6,4},{7,3},{8,10},{9,13},{10,... | collective-permute-start | bytes 215048 | tf_op jit(solution)/shard_map/ppermute | solution.py:303
  48.8 8.8 %collective-permute-start.18 = (bf16[140,128]{1,0:T(8,128)(2,1)S(1)}, bf16[140,128]{1,0:T(8,128)(2,1)S(1)}, u32[]{:S(2)}, u32[]{:S(2)}) collective-permute-start(bf16[140,128]{1,0:T(8,128)(2,1)S(1)} %get-tuple-element.62), channel_id=1, source_target_pairs={{0,8},{2,10},{4,12},{6,14},{8,0},{10,2},{12,4},{14,6},{16,24},{18,... | collective-permute-start | bytes 107528 | tf_op jit(solution)/shard_map/ppermute | solution.py:296
  51.5 6.5 %collective-permute-start.22 = (bf16[140,128]{1,0:T(8,128)(2,1)S(1)}, bf16[140,128]{1,0:T(8,128)(2,1)S(1)}, u32[]{:S(2)}, u32[]{:S(2)}) collective-permute-start(bf16[140,128]{1,0:T(8,128)(2,1)S(1)} %get-tuple-element.68), channel_id=1, source_target_pairs={{0,16},{2,18},{4,20},{6,22},{8,24},{10,26},{12,28},{14,30},{16,0},... | collective-permute-start | bytes 107528 | tf_op jit(solution)/shard_map/ppermute | solution.py:296
  53.7 5.8 %collective-permute-start.23 = (bf16[140,128]{1,0:T(8,128)(2,1)S(1)}, bf16[140,128]{1,0:T(8,128)(2,1)S(1)}, u32[]{:S(2)}, u32[]{:S(2)}) collective-permute-start(bf16[140,128]{1,0:T(8,128)(2,1)S(1)} %get-tuple-element.69), channel_id=1, source_target_pairs={{0,24},{2,26},{4,28},{6,30},{8,16},{10,18},{12,20},{14,22},{16,8},... | collective-permute-start | bytes 107528 | tf_op jit(solution)/shard_map/ppermute | solution.py:296
  58.0 1.9 %collective-permute-start.24 = (bf16[16,1792]{1,0:T(8,128)(2,1)S(1)}, bf16[16,1792]{1,0:T(8,128)(2,1)S(1)}, u32[]{:S(2)}, u32[]{:S(2)}) collective-permute-start(bf16[16,1792]{1,0:T(8,128)(2,1)S(1)} %get-tuple-element.77), channel_id=1, source_target_pairs={{0,1},{1,0},{2,3},{3,2},{4,5},{5,4},{6,7},{7,6},{8,9},{9,8},{10,11... | collective-permute-start | bytes 172040 | tf_op jit(solution)/shard_map/ppermute | solution.py:292
  59.5 1.6 %copy-start.3 = (f32[32,128]{1,0:T(8,128)S(1)}, f32[32,128]{1,0:T(8,128)}, u32[]{:S(2)}) copy-start(f32[32,128]{1,0:T(8,128)} %get-tuple-element.43.hot_ref) | copy-start | bytes 49156
  59.8 1.3 %collective-permute-start.25 = (bf16[16,1792]{1,0:T(8,128)(2,1)S(1)}, bf16[16,1792]{1,0:T(8,128)(2,1)S(1)}, u32[]{:S(2)}, u32[]{:S(2)}) collective-permute-start(bf16[16,1792]{1,0:T(8,128)(2,1)S(1)} %get-tuple-element.78), channel_id=1, source_target_pairs={{0,1},{1,0},{2,3},{3,2},{4,5},{5,4},{6,7},{7,6},{8,9},{9,8},{10,11... | collective-permute-start | bytes 172040 | tf_op jit(solution)/shard_map/ppermute | solution.py:292

commit v4 on v2

--- a/solution.py
+++ b/solution.py
@@ -263,14 +263,19 @@
 
 
 def place_kernel(hot_ref, *refs):
-    sources, out_ref = refs[:-1], refs[-1]
+    sources, out_ref, held, sems = refs[:-3], refs[-3], refs[-2], refs[-1]
     me = lax.axis_index("dp")
-    half = out_ref.shape[1] // CORES
+    half = held.shape[2]
     hot = hot_ref[...].astype(BF16)
+    copies = []
     for q in range(CORES):
         rows = jnp.concatenate([ref[...] for ref in sources[q * GROUPS : (q + 1) * GROUPS]], axis=0)
+        held[q] = dot(hot, rows, ((0,), (0,))).astype(BF16)
         columns = pl.ds(pl.multiple_of((me ^ q) * half, 128), half)
-        out_ref[:, columns] = dot(hot, rows, ((0,), (0,))).astype(BF16)
+        copies.append(pltpu.make_async_copy(held.at[q], out_ref.at[:, columns], sems.at[q]))
+        copies[q].start()
+    for copy in copies:
+        copy.wait()
 
 
 def like(shape, dtype):
@@ -415,7 +420,15 @@
         )
         back.append(mine)
         over.append(swap_cores(other))
-    input_grad = call(place_kernel, "place_rows", like((tokens, model), BF16), [hot, *back, *over])
+    input_grad = pl.pallas_call(
+        place_kernel,
+        out_shape=like((tokens, model), BF16),
+        in_specs=[vmem] * (1 + CORES * GROUPS),
+        out_specs=hbm,
+        scratch_shapes=[pltpu.VMEM((CORES, tokens, half), BF16), pltpu.SemaphoreType.DMA((CORES,))],
+        compiler_params=params(),
+        name="place_rows",
+    )(hot, *back, *over)
     return (input_grad, gate_grad, up_grad, down_grad)
 
 

time: 56.2 us -> 56.1 us (level)
    pallas_call x11 -> x10, Pallas kernels: 7.14 us -> 5.8 us  [call(): pl.pallas_call(kernel, out_shape=out_shape, in_specs=[vmem] * len(operand...]
    pallas_call x0 -> x1, Pallas kernels: none -> 1.25 us  [body(): pl.pallas_call(place_kernel, out_shape=like((tokens, model), BF16), in_sp...]
where the time goes in v4:
time: 56.1 us; the launch traced here: 55.9 us
  starting transfers between devices  24.6 us (44%)
  waiting for transfers between devices  17.5 us (31%)
  Pallas kernels  12.2 us (22%)
  local copies, waits for them, and re-layouts  0.9 us (2%)
  between operations  0.8 us (1%)
    ppermute x12, starting transfers between devices, in_plane(): return lax.ppermute(array, ('expert', 'dp'), hop)  15 us
    ppermute x6, starting transfers between devices, along_z(): return lax.ppermute(array, 'expert', hop)  8.74 us
    ppermute x12, waiting for transfers between devices, in_plane(): return lax.ppermute(array, ('expert', 'dp'), hop)  7.97 us
    ppermute x6, waiting for transfers between devices, along_z(): return lax.ppermute(array, 'expert', hop)  6.59 us
    pallas_call x10, Pallas kernels, call(): pl.pallas_call(kernel, out_shape=out_shape, in_specs=[vmem] * len(operand...  5.8 us
    ppermute x7, waiting for transfers between devices, swap_cores(): return lax.ppermute(array, 'dp', [(r, r ^ 1) for r in range(CORES)])  2.9 us
    pallas_call x1, Pallas kernels, body(): pl.pallas_call(functools.partial(gather_kernel, live), out_shape=[near_ro...  2.65 us
    pallas_call x1, Pallas kernels, body(): pl.pallas_call(grads_kernel, out_shape=[like((half, width), BF16)] * 3 +...  2.5 us
  transfers between devices with their start and end apart: 25, of which 16 were waited for; matrix products, arithmetic and copies ran while one was open for 0% of the time, Pallas kernels for 12%

profile of v4, /device:TPU:0, one launch (start us, length us, event | category | flops | bytes accessed | tf_op | source)
XLA Modules:
  0.0 55.9 jit_solution(3537716664246519574)
XLA Ops:
  0.6 2.6 %gather_rows.1 = (bf16[20,1792]{1,0:T(8,128)(2,1)}, bf16[20,1792]{1,0:T(8,128)(2,1)}, bf16[40,896]{1,0:T(8,128)(2,1)}, bf16[40,896]{1,0:T(8,128)(2,1)}, f32[32,128]{1,0:T(8,128)}) custom-call(s32[8,128]{1,0:T(8,128)} %bitcast.3, s32[8,128]{1,0:T(8,128)} %bitcast.4, f32[8,128]{1,0:T(8,128)} %bitcast.5, bf16[128,3584]{1,0:T(8,128)(2,1)} %refs_3_.1, ...), custom_call_target="tpu_custom_call" | custom-call | tf_op jit(solution)/shard_map/gather_rows/pallas_call | solution.py:325
  3.3 0.5 collective-permute-start.7
  3.8 3.7 %collective-permute-start = (bf16[40,896]{1,0:T(8,128)(2,1)}, bf16[40,896]{1,0:T(8,128)(2,1)S(1)}, u32[]{:S(2)}, u32[]{:S(2)}) collective-permute-start(bf16[40,896]{1,0:T(8,128)(2,1)} %get-tuple-element.39), channel_id=1, source_target_pairs={{0,16},{2,18},{4,20},{6,22},{8,24},{10,26},{12,28},{14,30},{16,0},... | collective-permute-start | bytes 215048 | tf_op jit(solution)/shard_map/ppermute | solution.py:314
  7.5 1.3 %collective-permute-start.1 = (bf16[40,896]{1,0:T(8,128)(2,1)}, bf16[40,896]{1,0:T(8,128)(2,1)S(1)}, u32[]{:S(2)}, u32[]{:S(2)}) collective-permute-start(bf16[40,896]{1,0:T(8,128)(2,1)} %get-tuple-element.40), channel_id=1, source_target_pairs={{0,24},{2,26},{4,28},{6,30},{8,16},{10,18},{12,20},{14,22},{16,8},... | collective-permute-start | bytes 215048 | tf_op jit(solution)/shard_map/ppermute | solution.py:314
  8.8 0.0 collective-permute-done.7.other_ref
  8.8 0.9 %copy-done.4 = bf16[20,1792]{1,0:T(8,128)(2,1)S(1)} copy-done((bf16[20,1792]{1,0:T(8,128)(2,1)S(1)}, bf16[20,1792]{1,0:T(8,128)(2,1)}, u32[]{:S(2)}) %copy-start.4) | copy-done | bytes 71704
  9.7 0.3 chunk_rows.1
  10.0 0.3 collective-permute-start.8
  10.3 2.0 %collective-permute-done.refs_0_ = bf16[40,896]{1,0:T(8,128)(2,1)S(1)} collective-permute-done((bf16[40,896]{1,0:T(8,128)(2,1)}, bf16[40,896]{1,0:T(8,128)(2,1)S(1)}, u32[]{:S(2)}, u32[]{:S(2)}) %collective-permute-start) | collective-permute-done | bytes 71712 | tf_op jit(solution)/shard_map/ppermute | solution.py:314
  12.3 0.0 collective-permute-start.2
  12.3 1.7 %collective-permute-done.1.refs_1_ = bf16[40,896]{1,0:T(8,128)(2,1)S(1)} collective-permute-done((bf16[40,896]{1,0:T(8,128)(2,1)}, bf16[40,896]{1,0:T(8,128)(2,1)S(1)}, u32[]{:S(2)}, u32[]{:S(2)}) %collective-permute-start.1) | collective-permute-done | bytes 71712 | tf_op jit(solution)/shard_map/ppermute | solution.py:314
  14.0 0.0 collective-permute-start.3
  14.0 1.4 %collective-permute-done.8.refs_1_ = bf16[40,896]{1,0:T(8,128)(2,1)S(1)} collective-permute-done((bf16[40,896]{1,0:T(8,128)(2,1)S(1)}, bf16[40,896]{1,0:T(8,128)(2,1)S(1)}, u32[]{:S(2)}, u32[]{:S(2)}) %collective-permute-start.8) | collective-permute-done | bytes 71712 | tf_op jit(solution)/shard_map/ppermute | solution.py:314
  15.4 0.2 merge_rows.3.refs_0_
  15.6 1.6 %collective-permute-start.9 = (bf16[40,1792]{1,0:T(8,128)(2,1)S(1)}, bf16[40,1792]{1,0:T(8,128)(2,1)S(1)}, u32[]{:S(2)}, u32[]{:S(2)}) collective-permute-start(bf16[40,1792]{1,0:T(8,128)(2,1)S(1)} %merge_rows.3.refs_0_), channel_id=1, source_target_pairs={{0,2},{1,5},{2,0},{3,7},{4,6},{5,1},{6,4},{7,3},{8,10},{9,13},{10,... | collective-permute-start | bytes 430088 | tf_op jit(solution)/shard_map/ppermute | solution.py:321
  17.3 0.0 collective-permute-done.2.refs_2_
  17.3 0.0 collective-permute-done.3.refs_3_
  17.3 0.2 merge_rows.2.refs_0_
  17.5 0.5 collective-permute-start.4
  18.1 1.6 %collective-permute-start.10 = (bf16[40,1792]{1,0:T(8,128)(2,1)S(1)}, bf16[40,1792]{1,0:T(8,128)(2,1)S(1)}, u32[]{:S(2)}, u32[]{:S(2)}) collective-permute-start(bf16[40,1792]{1,0:T(8,128)(2,1)S(1)} %merge_rows.3.refs_0_), channel_id=1, source_target_pairs={{0,4},{1,3},{2,6},{3,1},{4,0},{5,7},{6,2},{7,5},{8,12},{9,11},{10,... | collective-permute-start | bytes 430088 | tf_op jit(solution)/shard_map/ppermute | solution.py:321
  19.7 1.9 %collective-permute-done.9.refs_1_ = bf16[40,1792]{1,0:T(8,128)(2,1)S(1)} collective-permute-done((bf16[40,1792]{1,0:T(8,128)(2,1)S(1)}, bf16[40,1792]{1,0:T(8,128)(2,1)S(1)}, u32[]{:S(2)}, u32[]{:S(2)}) %collective-permute-start.9) | collective-permute-done | bytes 143392 | tf_op jit(solution)/shard_map/ppermute | solution.py:321
  21.5 1.6 %collective-permute-start.11 = (bf16[40,1792]{1,0:T(8,128)(2,1)S(1)}, bf16[40,1792]{1,0:T(8,128)(2,1)S(1)}, u32[]{:S(2)}, u32[]{:S(2)}) collective-permute-start(bf16[40,1792]{1,0:T(8,128)(2,1)S(1)} %collective-permute-done.9.refs_1_), channel_id=1, source_target_pairs={{0,4},{1,3},{2,6},{3,1},{4,0},{5,7},{6,2},{7,5},{8,12},{9,11},{10,... | collective-permute-start | bytes 430088 | tf_op jit(solution)/shard_map/ppermute | solution.py:321
  23.1 0.4 collective-permute-start.5
  23.6 1.0 %collective-permute-done.4.refs_1_ = bf16[40,1792]{1,0:T(8,128)(2,1)S(1)} collective-permute-done((bf16[40,1792]{1,0:T(8,128)(2,1)S(1)}, bf16[40,1792]{1,0:T(8,128)(2,1)S(1)}, u32[]{:S(2)}, u32[]{:S(2)}) %collective-permute-start.4) | collective-permute-done | bytes 143392 | tf_op jit(solution)/shard_map/ppermute | solution.py:321
  24.6 1.6 %collective-permute-start.6 = (bf16[40,1792]{1,0:T(8,128)(2,1)S(1)}, bf16[40,1792]{1,0:T(8,128)(2,1)S(1)}, u32[]{:S(2)}, u32[]{:S(2)}) collective-permute-start(bf16[40,1792]{1,0:T(8,128)(2,1)S(1)} %collective-permute-done.4.refs_1_), channel_id=1, source_target_pairs={{0,4},{1,3},{2,6},{3,1},{4,0},{5,7},{6,2},{7,5},{8,12},{9,11},{10,... | collective-permute-start | bytes 430088 | tf_op jit(solution)/shard_map/ppermute | solution.py:321
  26.2 0.0 collective-permute-done.10.refs_2_
  26.2 0.4 collective-permute-done.11.refs_3_
  26.6 1.0 %partial_products.3 = (f32[80,1152]{1,0:T(8,128)S(1)}, bf16[80,1792]{1,0:T(8,128)(2,1)S(1)}, bf16[80,1792]{1,0:T(8,128)(2,1)S(1)}) custom-call(bf16[40,1792]{1,0:T(8,128)(2,1)S(1)} %merge_rows.3.refs_0_, bf16[40,1792]{1,0:T(8,128)(2,1)S(1)} %collective-permute-done.9.refs_1_, bf16[40,1792]{1,0:T(8,128)(2,1)S(1)} %collective-permute-done.10.refs_2_, ...), custom_call_target="tpu_custom_call" | custom-call | flops 330301440 | bytes 4128768 | tf_op jit(solution)/shard_map/partial_products/pallas_call | solution.py:299
  27.7 0.1 collective-permute-start.13
  27.8 0.5 collective-permute-done.5.refs_2_
  28.2 1.5 %collective-permute-done.6.refs_3_ = bf16[40,1792]{1,0:T(8,128)(2,1)S(1)} collective-permute-done((bf16[40,1792]{1,0:T(8,128)(2,1)S(1)}, bf16[40,1792]{1,0:T(8,128)(2,1)S(1)}, u32[]{:S(2)}, u32[]{:S(2)}) %collective-permute-start.6) | collective-permute-done | bytes 143392 | tf_op jit(solution)/shard_map/ppermute | solution.py:321
  29.8 1.0 %partial_products.2 = (f32[80,1152]{1,0:T(8,128)S(1)}, bf16[80,1792]{1,0:T(8,128)(2,1)S(1)}, bf16[80,1792]{1,0:T(8,128)(2,1)S(1)}) custom-call(bf16[40,1792]{1,0:T(8,128)(2,1)S(1)} %merge_rows.2.refs_0_, bf16[40,1792]{1,0:T(8,128)(2,1)S(1)} %collective-permute-done.4.refs_1_, bf16[40,1792]{1,0:T(8,128)(2,1)S(1)} %collective-permute-done.5.refs_2_, ...), custom_call_target="tpu_custom_call" | custom-call | flops 330301440 | bytes 4128768 | tf_op jit(solution)/shard_map/partial_products/pallas_call | solution.py:299
  30.8 0.1 collective-permute-start.12
  30.9 0.0 collective-permute-done.13.refs_3_
  30.9 1.7 %collective-permute-done.12.refs_2_ = f32[80,1152]{1,0:T(8,128)S(1)} collective-permute-done((f32[80,1152]{1,0:T(8,128)S(1)}, f32[80,1152]{1,0:T(8,128)S(1)}, u32[]{:S(2)}, u32[]{:S(2)}) %collective-permute-start.12) | collective-permute-done | bytes 368672 | tf_op jit(solution)/shard_map/ppermute | solution.py:310
  32.6 1.4 %sides_and_parts.1 = (bf16[40,896]{1,0:T(8,128)(2,1)S(1)}, bf16[40,896]{1,0:T(8,128)(2,1)S(1)}, bf16[40,896]{1,0:T(8,128)(2,1)S(1)}, bf16[40,896]{1,0:T(8,128)(2...) custom-call(f32[80,1152]{1,0:T(8,128)S(1)} %get-tuple-element.41.ref, ...), custom_call_target="tpu_custom_call" | custom-call | flops 440401920 | bytes 2752512 | tf_op jit(solution)/shard_map/sides_and_parts/pallas_call | solution.py:299
  34.0 2.5 %collective-permute-start.14 = (bf16[40,896]{1,0:T(8,128)(2,1)S(1)}, bf16[40,896]{1,0:T(8,128)(2,1)S(1)}, u32[]{:S(2)}, u32[]{:S(2)}) collective-permute-start(bf16[40,896]{1,0:T(8,128)(2,1)S(1)} %get-tuple-element.48), channel_id=1, source_target_pairs={{0,6},{1,7},{2,4},{3,5},{4,2},{5,3},{6,0},{7,1},{8,14},{9,15},{10,... | collective-permute-start | bytes 215048 | tf_op jit(solution)/shard_map/ppermute | solution.py:321
  36.5 0.5 collective-permute-start.15
  37.0 0.5 collective-permute-start.16
  37.5 2.5 %collective-permute-start.18 = (bf16[40,896]{1,0:T(8,128)(2,1)S(1)}, bf16[40,896]{1,0:T(8,128)(2,1)S(1)}, u32[]{:S(2)}, u32[]{:S(2)}) collective-permute-start(bf16[40,896]{1,0:T(8,128)(2,1)S(1)} %get-tuple-element.55), channel_id=1, source_target_pairs={{0,6},{1,7},{2,4},{3,5},{4,2},{5,3},{6,0},{7,1},{8,14},{9,15},{10,... | collective-permute-start | bytes 215048 | tf_op jit(solution)/shard_map/ppermute | solution.py:321
  40.0 0.5 collective-permute-start.19
  40.5 0.0 collective-permute-done.14.refs_1_
  40.5 1.1 %collective-permute-start.20 = (bf16[40,896]{1,0:T(8,128)(2,1)S(1)}, bf16[40,896]{1,0:T(8,128)(2,1)S(1)}, u32[]{:S(2)}, u32[]{:S(2)}) collective-permute-start(bf16[40,896]{1,0:T(8,128)(2,1)S(1)} %get-tuple-element.57), channel_id=1, source_target_pairs={{0,2},{1,5},{2,0},{3,7},{4,6},{5,1},{6,4},{7,3},{8,10},{9,13},{10,... | collective-permute-start | bytes 215048 | tf_op jit(solution)/shard_map/ppermute | solution.py:321
  41.6 0.2 collective-permute-done.15.refs_2_
  41.8 0.3 collective-permute-done.16.refs_3_
  42.1 0.5 sum_parts.2
  42.6 0.1 collective-permute-start.17
  42.7 1.1 %collective-permute-done.18.refs_1_ = bf16[40,896]{1,0:T(8,128)(2,1)S(1)} collective-permute-done((bf16[40,896]{1,0:T(8,128)(2,1)S(1)}, bf16[40,896]{1,0:T(8,128)(2,1)S(1)}, u32[]{:S(2)}, u32[]{:S(2)}) %collective-permute-start.18) | collective-permute-done | bytes 71712 | tf_op jit(solution)/shard_map/ppermute | solution.py:321
  43.9 0.7 %collective-permute-done.19.refs_2_ = bf16[40,896]{1,0:T(8,128)(2,1)S(1)} collective-permute-done((bf16[40,896]{1,0:T(8,128)(2,1)S(1)}, bf16[40,896]{1,0:T(8,128)(2,1)S(1)}, u32[]{:S(2)}, u32[]{:S(2)}) %collective-permute-start.19) | collective-permute-done | bytes 71712 | tf_op jit(solution)/shard_map/ppermute | solution.py:321
  44.6 0.2 collective-permute-done.20.refs_3_
  44.8 0.5 sum_parts.3
  45.3 1.9 %collective-permute-start.21 = (bf16[140,128]{1,0:T(8,128)(2,1)S(1)}, bf16[140,128]{1,0:T(8,128)(2,1)S(1)}, u32[]{:S(2)}, u32[]{:S(2)}) collective-permute-start(bf16[140,128]{1,0:T(8,128)(2,1)S(1)} %get-tuple-element.58), channel_id=1, source_target_pairs={{0,16},{2,18},{4,20},{6,22},{8,24},{10,26},{12,28},{14,30},{16,0},... | collective-permute-start | bytes 107528 | tf_op jit(solution)/shard_map/ppermute | solution.py:314
  47.3 1.4 %collective-permute-start.22 = (bf16[140,128]{1,0:T(8,128)(2,1)S(1)}, bf16[140,128]{1,0:T(8,128)(2,1)S(1)}, u32[]{:S(2)}, u32[]{:S(2)}) collective-permute-start(bf16[140,128]{1,0:T(8,128)(2,1)S(1)} %get-tuple-element.59), channel_id=1, source_target_pairs={{0,24},{2,26},{4,28},{6,30},{8,16},{10,18},{12,20},{14,22},{16,8},... | collective-permute-start | bytes 107528 | tf_op jit(solution)/shard_map/ppermute | solution.py:314
  48.6 2.5 %weight_grads.1 = (bf16[1792,384]{1,0:T(8,128)(2,1)}, bf16[1792,384]{1,0:T(8,128)(2,1)}, bf16[1792,384]{1,0:T(8,128)(2,1)}, f32[8,128]{1,0:T(8,128)S(1)}) custom-call(bf16[80,1792]{1,0:T(8,128)(2,1)S(1)} %get-tuple-element.60.refs_0_, bf16[80,1792]{1,0:T(8,128)(2,1)S(1)} %get-tuple-element.61.refs_1_, bf16[80,1792]{1,0:T(8,128)(2,1)S(1)} %get-tuple-element.62.refs_2_, ...), custom_call_target="tpu_custom_call" | custom-call | flops 660602880 | bytes 5275648 | tf_op jit(solution)/shard_map/weight_grads/pallas_call | solution.py:392
  51.2 0.0 collective-permute-done.17.refs_1_
  51.2 0.3 split_rows.2
  51.5 0.1 collective-permute-start.23
  51.6 0.0 collective-permute-done.21.refs_0_
  51.6 1.5 %collective-permute-done.22.refs_1_ = bf16[140,128]{1,0:T(8,128)(2,1)S(1)} collective-permute-done((bf16[140,128]{1,0:T(8,128)(2,1)S(1)}, bf16[140,128]{1,0:T(8,128)(2,1)S(1)}, u32[]{:S(2)}, u32[]{:S(2)}) %collective-permute-start.22) | collective-permute-done | bytes 35872 | tf_op jit(solution)/shard_map/ppermute | solution.py:314
  53.0 0.3 split_rows.3
  53.3 0.1 collective-permute-start.24
  53.4 0.0 collective-permute-done.23.refs_2_
  53.4 1.2 %collective-permute-done.24.refs_3_ = bf16[16,1792]{1,0:T(8,128)(2,1)S(1)} collective-permute-done((bf16[16,1792]{1,0:T(8,128)(2,1)S(1)}, bf16[16,1792]{1,0:T(8,128)(2,1)S(1)}, u32[]{:S(2)}, u32[]{:S(2)}) %collective-permute-start.24) | collective-permute-done | bytes 57376 | tf_op jit(solution)/shard_map/ppermute | solution.py:310
  54.7 1.3 %place_rows.1 = bf16[128,3584]{1,0:T(8,128)(2,1)} custom-call(f32[32,128]{1,0:T(8,128)S(1)} %copy-done.3, bf16[16,1792]{1,0:T(8,128)(2,1)S(1)} %get-tuple-element.53.refs_0_, bf16[16,1792]{1,0:T(8,128)(2,1)S(1)} %get-tuple-element.66.refs_1_, bf16[16,1792]{1,0:T(8,128)(2,1)S(1)} %collective-permute-done.23.refs_2_, ...), custom_call_target="tpu_custom_call" | custom-call | tf_op jit(solution)/shard_map/place_rows/pallas_call | solution.py:423
  (9 shorter events, 0.0 us)
Async XLA Ops:
  3.3 5.5 %collective-permute-start.7 = (bf16[20,1792]{1,0:T(8,128)(2,1)}, bf16[20,1792]{1,0:T(8,128)(2,1)S(1)}, u32[]{:S(2)}, u32[]{:S(2)}) collective-permute-start(bf16[20,1792]{1,0:T(8,128)(2,1)} %get-tuple-element.43), channel_id=1, source_target_pairs={{0,1},{1,0},{2,3},{3,2},{4,5},{5,4},{6,7},{7,6},{8,9},{9,8},{10,11... | collective-permute-start | bytes 215048 | tf_op jit(solution)/shard_map/ppermute | solution.py:310
  3.8 8.5 %collective-permute-start = (bf16[40,896]{1,0:T(8,128)(2,1)}, bf16[40,896]{1,0:T(8,128)(2,1)S(1)}, u32[]{:S(2)}, u32[]{:S(2)}) collective-permute-start(bf16[40,896]{1,0:T(8,128)(2,1)} %get-tuple-element.39), channel_id=1, source_target_pairs={{0,16},{2,18},{4,20},{6,22},{8,24},{10,26},{12,28},{14,30},{16,0},... | collective-permute-start | bytes 215048 | tf_op jit(solution)/shard_map/ppermute | solution.py:314
  7.5 6.6 %collective-permute-start.1 = (bf16[40,896]{1,0:T(8,128)(2,1)}, bf16[40,896]{1,0:T(8,128)(2,1)S(1)}, u32[]{:S(2)}, u32[]{:S(2)}) collective-permute-start(bf16[40,896]{1,0:T(8,128)(2,1)} %get-tuple-element.40), channel_id=1, source_target_pairs={{0,24},{2,26},{4,28},{6,30},{8,16},{10,18},{12,20},{14,22},{16,8},... | collective-permute-start | bytes 215048 | tf_op jit(solution)/shard_map/ppermute | solution.py:314
  8.8 0.9 %copy-start.4 = (bf16[20,1792]{1,0:T(8,128)(2,1)S(1)}, bf16[20,1792]{1,0:T(8,128)(2,1)}, u32[]{:S(2)}) copy-start(bf16[20,1792]{1,0:T(8,128)(2,1)} %get-tuple-element.42.mine_ref) | copy-start | bytes 215044
  9.7 16.9 %copy-start = (bf16[1792,384]{1,0:T(8,128)(2,1)S(1)}, bf16[1792,384]{1,0:T(8,128)(2,1)}, u32[]{:S(2)}) copy-start(bf16[1792,384]{1,0:T(8,128)(2,1)} %refs_4_.7) | copy-start | bytes 4128772
  9.7 16.9 %copy-start.1 = (bf16[1792,384]{1,0:T(8,128)(2,1)S(1)}, bf16[1792,384]{1,0:T(8,128)(2,1)}, u32[]{:S(2)}) copy-start(bf16[1792,384]{1,0:T(8,128)(2,1)} %refs_5_.5) | copy-start | bytes 4128772
  9.7 16.9 %copy-start.2 = (bf16[1792,384]{1,0:T(8,128)(2,1)S(1)}, bf16[1792,384]{1,0:T(8,128)(2,1)}, u32[]{:S(2)}) copy-start(bf16[1792,384]{1,0:T(8,128)(2,1)} %refs_6_.3) | copy-start | bytes 4128772
  10.0 5.4 %collective-permute-start.8 = (bf16[40,896]{1,0:T(8,128)(2,1)S(1)}, bf16[40,896]{1,0:T(8,128)(2,1)S(1)}, u32[]{:S(2)}, u32[]{:S(2)}) collective-permute-start(bf16[40,896]{1,0:T(8,128)(2,1)S(1)} %get-tuple-element.45), channel_id=1, source_target_pairs={{0,8},{2,10},{4,12},{6,14},{8,0},{10,2},{12,4},{14,6},{16,24},{18,... | collective-permute-start | bytes 215048 | tf_op jit(solution)/shard_map/ppermute | solution.py:314
  12.3 5.0 %collective-permute-start.2 = (bf16[40,896]{1,0:T(8,128)(2,1)S(1)}, bf16[40,896]{1,0:T(8,128)(2,1)S(1)}, u32[]{:S(2)}, u32[]{:S(2)}) collective-permute-start(bf16[40,896]{1,0:T(8,128)(2,1)S(1)} %collective-permute-done.refs_0_), channel_id=1, source_target_pairs={{0,1},{1,0},{2,3},{3,2},{4,5},{5,4},{6,7},{7,6},{8,9},{9,8},{10,11... | collective-permute-start | bytes 215048 | tf_op jit(solution)/shard_map/ppermute | solution.py:310
  14.0 3.2 %collective-permute-start.3 = (bf16[40,896]{1,0:T(8,128)(2,1)S(1)}, bf16[40,896]{1,0:T(8,128)(2,1)S(1)}, u32[]{:S(2)}, u32[]{:S(2)}) collective-permute-start(bf16[40,896]{1,0:T(8,128)(2,1)S(1)} %collective-permute-done.1.refs_1_), channel_id=1, source_target_pairs={{0,1},{1,0},{2,3},{3,2},{4,5},{5,4},{6,7},{7,6},{8,9},{9,8},{10,11... | collective-permute-start | bytes 215048 | tf_op jit(solution)/shard_map/ppermute | solution.py:310
  15.6 5.9 %collective-permute-start.9 = (bf16[40,1792]{1,0:T(8,128)(2,1)S(1)}, bf16[40,1792]{1,0:T(8,128)(2,1)S(1)}, u32[]{:S(2)}, u32[]{:S(2)}) collective-permute-start(bf16[40,1792]{1,0:T(8,128)(2,1)S(1)} %merge_rows.3.refs_0_), channel_id=1, source_target_pairs={{0,2},{1,5},{2,0},{3,7},{4,6},{5,1},{6,4},{7,3},{8,10},{9,13},{10,... | collective-permute-start | bytes 430088 | tf_op jit(solution)/shard_map/ppermute | solution.py:321
  17.5 7.1 %collective-permute-start.4 = (bf16[40,1792]{1,0:T(8,128)(2,1)S(1)}, bf16[40,1792]{1,0:T(8,128)(2,1)S(1)}, u32[]{:S(2)}, u32[]{:S(2)}) collective-permute-start(bf16[40,1792]{1,0:T(8,128)(2,1)S(1)} %merge_rows.2.refs_0_), channel_id=1, source_target_pairs={{0,2},{1,5},{2,0},{3,7},{4,6},{5,1},{6,4},{7,3},{8,10},{9,13},{10,... | collective-permute-start | bytes 430088 | tf_op jit(solution)/shard_map/ppermute | solution.py:321
  18.1 8.2 %collective-permute-start.10 = (bf16[40,1792]{1,0:T(8,128)(2,1)S(1)}, bf16[40,1792]{1,0:T(8,128)(2,1)S(1)}, u32[]{:S(2)}, u32[]{:S(2)}) collective-permute-start(bf16[40,1792]{1,0:T(8,128)(2,1)S(1)} %merge_rows.3.refs_0_), channel_id=1, source_target_pairs={{0,4},{1,3},{2,6},{3,1},{4,0},{5,7},{6,2},{7,5},{8,12},{9,11},{10,... | collective-permute-start | bytes 430088 | tf_op jit(solution)/shard_map/ppermute | solution.py:321
  21.5 5.1 %collective-permute-start.11 = (bf16[40,1792]{1,0:T(8,128)(2,1)S(1)}, bf16[40,1792]{1,0:T(8,128)(2,1)S(1)}, u32[]{:S(2)}, u32[]{:S(2)}) collective-permute-start(bf16[40,1792]{1,0:T(8,128)(2,1)S(1)} %collective-permute-done.9.refs_1_), channel_id=1, source_target_pairs={{0,4},{1,3},{2,6},{3,1},{4,0},{5,7},{6,2},{7,5},{8,12},{9,11},{10,... | collective-permute-start | bytes 430088 | tf_op jit(solution)/shard_map/ppermute | solution.py:321
  23.1 5.1 %collective-permute-start.5 = (bf16[40,1792]{1,0:T(8,128)(2,1)S(1)}, bf16[40,1792]{1,0:T(8,128)(2,1)S(1)}, u32[]{:S(2)}, u32[]{:S(2)}) collective-permute-start(bf16[40,1792]{1,0:T(8,128)(2,1)S(1)} %merge_rows.2.refs_0_), channel_id=1, source_target_pairs={{0,4},{1,3},{2,6},{3,1},{4,0},{5,7},{6,2},{7,5},{8,12},{9,11},{10,... | collective-permute-start | bytes 430088 | tf_op jit(solution)/shard_map/ppermute | solution.py:321
  24.6 5.2 %collective-permute-start.6 = (bf16[40,1792]{1,0:T(8,128)(2,1)S(1)}, bf16[40,1792]{1,0:T(8,128)(2,1)S(1)}, u32[]{:S(2)}, u32[]{:S(2)}) collective-permute-start(bf16[40,1792]{1,0:T(8,128)(2,1)S(1)} %collective-permute-done.4.refs_1_), channel_id=1, source_target_pairs={{0,4},{1,3},{2,6},{3,1},{4,0},{5,7},{6,2},{7,5},{8,12},{9,11},{10,... | collective-permute-start | bytes 430088 | tf_op jit(solution)/shard_map/ppermute | solution.py:321
  27.7 3.2 %collective-permute-start.13 = (f32[80,1152]{1,0:T(8,128)S(1)}, f32[80,1152]{1,0:T(8,128)S(1)}, u32[]{:S(2)}, u32[]{:S(2)}) collective-permute-start(f32[80,1152]{1,0:T(8,128)S(1)} %get-tuple-element.46.refs_1_), channel_id=1, source_target_pairs={{0,1},{1,0},{2,3},{3,2},{4,5},{5,4},{6,7},{7,6},{8,9},{9,8},{10,11... | collective-permute-start | bytes 1105928 | tf_op jit(solution)/shard_map/ppermute | solution.py:310
  30.8 1.8 %collective-permute-start.12 = (f32[80,1152]{1,0:T(8,128)S(1)}, f32[80,1152]{1,0:T(8,128)S(1)}, u32[]{:S(2)}, u32[]{:S(2)}) collective-permute-start(f32[80,1152]{1,0:T(8,128)S(1)} %get-tuple-element.41.refs_0_), channel_id=1, source_target_pairs={{0,1},{1,0},{2,3},{3,2},{4,5},{5,4},{6,7},{7,6},{8,9},{9,8},{10,11... | collective-permute-start | bytes 1105928 | tf_op jit(solution)/shard_map/ppermute | solution.py:310
  34.0 6.5 %collective-permute-start.14 = (bf16[40,896]{1,0:T(8,128)(2,1)S(1)}, bf16[40,896]{1,0:T(8,128)(2,1)S(1)}, u32[]{:S(2)}, u32[]{:S(2)}) collective-permute-start(bf16[40,896]{1,0:T(8,128)(2,1)S(1)} %get-tuple-element.48), channel_id=1, source_target_pairs={{0,6},{1,7},{2,4},{3,5},{4,2},{5,3},{6,0},{7,1},{8,14},{9,15},{10,... | collective-permute-start | bytes 215048 | tf_op jit(solution)/shard_map/ppermute | solution.py:321
  36.5 5.3 %collective-permute-start.15 = (bf16[40,896]{1,0:T(8,128)(2,1)S(1)}, bf16[40,896]{1,0:T(8,128)(2,1)S(1)}, u32[]{:S(2)}, u32[]{:S(2)}) collective-permute-start(bf16[40,896]{1,0:T(8,128)(2,1)S(1)} %get-tuple-element.49), channel_id=1, source_target_pairs={{0,4},{1,3},{2,6},{3,1},{4,0},{5,7},{6,2},{7,5},{8,12},{9,11},{10,... | collective-permute-start | bytes 215048 | tf_op jit(solution)/shard_map/ppermute | solution.py:321
  37.0 5.1 %collective-permute-start.16 = (bf16[40,896]{1,0:T(8,128)(2,1)S(1)}, bf16[40,896]{1,0:T(8,128)(2,1)S(1)}, u32[]{:S(2)}, u32[]{:S(2)}) collective-permute-start(bf16[40,896]{1,0:T(8,128)(2,1)S(1)} %get-tuple-element.50), channel_id=1, source_target_pairs={{0,2},{1,5},{2,0},{3,7},{4,6},{5,1},{6,4},{7,3},{8,10},{9,13},{10,... | collective-permute-start | bytes 215048 | tf_op jit(solution)/shard_map/ppermute | solution.py:321
  37.5 6.3 %collective-permute-start.18 = (bf16[40,896]{1,0:T(8,128)(2,1)S(1)}, bf16[40,896]{1,0:T(8,128)(2,1)S(1)}, u32[]{:S(2)}, u32[]{:S(2)}) collective-permute-start(bf16[40,896]{1,0:T(8,128)(2,1)S(1)} %get-tuple-element.55), channel_id=1, source_target_pairs={{0,6},{1,7},{2,4},{3,5},{4,2},{5,3},{6,0},{7,1},{8,14},{9,15},{10,... | collective-permute-start | bytes 215048 | tf_op jit(solution)/shard_map/ppermute | solution.py:321
  40.0 4.6 %collective-permute-start.19 = (bf16[40,896]{1,0:T(8,128)(2,1)S(1)}, bf16[40,896]{1,0:T(8,128)(2,1)S(1)}, u32[]{:S(2)}, u32[]{:S(2)}) collective-permute-start(bf16[40,896]{1,0:T(8,128)(2,1)S(1)} %get-tuple-element.56), channel_id=1, source_target_pairs={{0,4},{1,3},{2,6},{3,1},{4,0},{5,7},{6,2},{7,5},{8,12},{9,11},{10,... | collective-permute-start | bytes 215048 | tf_op jit(solution)/shard_map/ppermute | solution.py:321
  40.5 4.3 %collective-permute-start.20 = (bf16[40,896]{1,0:T(8,128)(2,1)S(1)}, bf16[40,896]{1,0:T(8,128)(2,1)S(1)}, u32[]{:S(2)}, u32[]{:S(2)}) collective-permute-start(bf16[40,896]{1,0:T(8,128)(2,1)S(1)} %get-tuple-element.57), channel_id=1, source_target_pairs={{0,2},{1,5},{2,0},{3,7},{4,6},{5,1},{6,4},{7,3},{8,10},{9,13},{10,... | collective-permute-start | bytes 215048 | tf_op jit(solution)/shard_map/ppermute | solution.py:321
  42.6 8.6 %collective-permute-start.17 = (bf16[140,128]{1,0:T(8,128)(2,1)S(1)}, bf16[140,128]{1,0:T(8,128)(2,1)S(1)}, u32[]{:S(2)}, u32[]{:S(2)}) collective-permute-start(bf16[140,128]{1,0:T(8,128)(2,1)S(1)} %get-tuple-element.52), channel_id=1, source_target_pairs={{0,8},{2,10},{4,12},{6,14},{8,0},{10,2},{12,4},{14,6},{16,24},{18,... | collective-permute-start | bytes 107528 | tf_op jit(solution)/shard_map/ppermute | solution.py:314
  45.3 6.2 %collective-permute-start.21 = (bf16[140,128]{1,0:T(8,128)(2,1)S(1)}, bf16[140,128]{1,0:T(8,128)(2,1)S(1)}, u32[]{:S(2)}, u32[]{:S(2)}) collective-permute-start(bf16[140,128]{1,0:T(8,128)(2,1)S(1)} %get-tuple-element.58), channel_id=1, source_target_pairs={{0,16},{2,18},{4,20},{6,22},{8,24},{10,26},{12,28},{14,30},{16,0},... | collective-permute-start | bytes 107528 | tf_op jit(solution)/shard_map/ppermute | solution.py:314
  47.3 5.8 %collective-permute-start.22 = (bf16[140,128]{1,0:T(8,128)(2,1)S(1)}, bf16[140,128]{1,0:T(8,128)(2,1)S(1)}, u32[]{:S(2)}, u32[]{:S(2)}) collective-permute-start(bf16[140,128]{1,0:T(8,128)(2,1)S(1)} %get-tuple-element.59), channel_id=1, source_target_pairs={{0,24},{2,26},{4,28},{6,30},{8,16},{10,18},{12,20},{14,22},{16,8},... | collective-permute-start | bytes 107528 | tf_op jit(solution)/shard_map/ppermute | solution.py:314
  51.5 2.0 %collective-permute-start.23 = (bf16[16,1792]{1,0:T(8,128)(2,1)S(1)}, bf16[16,1792]{1,0:T(8,128)(2,1)S(1)}, u32[]{:S(2)}, u32[]{:S(2)}) collective-permute-start(bf16[16,1792]{1,0:T(8,128)(2,1)S(1)} %get-tuple-element.67), channel_id=1, source_target_pairs={{0,1},{1,0},{2,3},{3,2},{4,5},{5,4},{6,7},{7,6},{8,9},{9,8},{10,11... | collective-permute-start | bytes 172040 | tf_op jit(solution)/shard_map/ppermute | solution.py:310
  53.0 1.6 %copy-start.3 = (f32[32,128]{1,0:T(8,128)S(1)}, f32[32,128]{1,0:T(8,128)}, u32[]{:S(2)}) copy-start(f32[32,128]{1,0:T(8,128)} %get-tuple-element.38.hot_ref) | copy-start | bytes 49156
  53.3 1.3 %collective-permute-start.24 = (bf16[16,1792]{1,0:T(8,128)(2,1)S(1)}, bf16[16,1792]{1,0:T(8,128)(2,1)S(1)}, u32[]{:S(2)}, u32[]{:S(2)}) collective-permute-start(bf16[16,1792]{1,0:T(8,128)(2,1)S(1)} %get-tuple-element.68), channel_id=1, source_target_pairs={{0,1},{1,0},{2,3},{3,2},{4,5},{5,4},{6,7},{7,6},{8,9},{9,8},{10,11... | collective-permute-start | bytes 172040 | tf_op jit(solution)/shard_map/ppermute | solution.py:310

commit v5 on v4

--- a/solution.py
+++ b/solution.py
@@ -388,7 +388,7 @@
     parts, sides = [], sided[-1]
     for group in range(GROUPS):
         mine = sided[group * SPLIT : (group + 1) * SPLIT]
-        parts.append([mine[0]] + [in_plane(mine[k], k) for k in reversed(range(1, SPLIT))])
+        parts.append([mine[0]] + [in_plane(mine[k], k) for k in range(1, SPLIT)])
     gate_grad, up_grad, down_grad, token = pl.pallas_call(
         grads_kernel,
         out_shape=[like((half, width), BF16)] * 3 + [like((8, 128), F32)],

time: 56.1 us -> 57.1 us (1.018)
  waiting for transfers between devices: 17.5 us -> 18.6 us
    ppermute x12, waiting for transfers between devices: 7.97 us -> 9.13 us  [in_plane(): return lax.ppermute(array, ('expert', 'dp'), hop)]
  transfers between devices with their start and end apart: 25 -> 25, of which waited for: 16 -> 15; matrix products, arithmetic and copies ran while one was open for 0% -> 0% of each run, Pallas kernels for 12% -> 12%
where the time goes in v5:
time: 57.1 us; the launch traced here: 56.9 us
  starting transfers between devices  24.4 us (43%)
  waiting for transfers between devices  18.6 us (33%)
  Pallas kernels  12.2 us (21%)
  local copies, waits for them, and re-layouts  0.9 us (2%)
  between operations  0.8 us (1%)
    ppermute x12, starting transfers between devices, in_plane(): return lax.ppermute(array, ('expert', 'dp'), hop)  14.8 us
    ppermute x12, waiting for transfers between devices, in_plane(): return lax.ppermute(array, ('expert', 'dp'), hop)  9.13 us
    ppermute x6, starting transfers between devices, along_z(): return lax.ppermute(array, 'expert', hop)  8.74 us
    ppermute x6, waiting for transfers between devices, along_z(): return lax.ppermute(array, 'expert', hop)  6.6 us
    pallas_call x10, Pallas kernels, call(): pl.pallas_call(kernel, out_shape=out_shape, in_specs=[vmem] * len(operand...  5.8 us
    ppermute x7, waiting for transfers between devices, swap_cores(): return lax.ppermute(array, 'dp', [(r, r ^ 1) for r in range(CORES)])  2.9 us
    pallas_call x1, Pallas kernels, body(): pl.pallas_call(functools.partial(gather_kernel, live), out_shape=[near_ro...  2.65 us
    pallas_call x1, Pallas kernels, body(): pl.pallas_call(grads_kernel, out_shape=[like((half, width), BF16)] * 3 +...  2.5 us
  transfers between devices with their start and end apart: 25, of which 15 were waited for; matrix products, arithmetic and copies ran while one was open for 0% of the time, Pallas kernels for 12%

profile of v5, /device:TPU:0, one launch (start us, length us, event | category | flops | bytes accessed | tf_op | source)
XLA Modules:
  0.0 56.9 jit_solution(1511301239806815509)
XLA Ops:
  0.6 2.6 %gather_rows.1 = (bf16[20,1792]{1,0:T(8,128)(2,1)}, bf16[20,1792]{1,0:T(8,128)(2,1)}, bf16[40,896]{1,0:T(8,128)(2,1)}, bf16[40,896]{1,0:T(8,128)(2,1)}, f32[32,128]{1,0:T(8,128)}) custom-call(s32[8,128]{1,0:T(8,128)} %bitcast.3, s32[8,128]{1,0:T(8,128)} %bitcast.4, f32[8,128]{1,0:T(8,128)} %bitcast.5, bf16[128,3584]{1,0:T(8,128)(2,1)} %refs_3_.1, ...), custom_call_target="tpu_custom_call" | custom-call | tf_op jit(solution)/shard_map/gather_rows/pallas_call | solution.py:325
  3.3 0.5 collective-permute-start.7
  3.8 3.7 %collective-permute-start = (bf16[40,896]{1,0:T(8,128)(2,1)}, bf16[40,896]{1,0:T(8,128)(2,1)S(1)}, u32[]{:S(2)}, u32[]{:S(2)}) collective-permute-start(bf16[40,896]{1,0:T(8,128)(2,1)} %get-tuple-element.39), channel_id=1, source_target_pairs={{0,16},{2,18},{4,20},{6,22},{8,24},{10,26},{12,28},{14,30},{16,0},... | collective-permute-start | bytes 215048 | tf_op jit(solution)/shard_map/ppermute | solution.py:314
  7.5 1.3 %collective-permute-start.1 = (bf16[40,896]{1,0:T(8,128)(2,1)}, bf16[40,896]{1,0:T(8,128)(2,1)S(1)}, u32[]{:S(2)}, u32[]{:S(2)}) collective-permute-start(bf16[40,896]{1,0:T(8,128)(2,1)} %get-tuple-element.40), channel_id=1, source_target_pairs={{0,24},{2,26},{4,28},{6,30},{8,16},{10,18},{12,20},{14,22},{16,8},... | collective-permute-start | bytes 215048 | tf_op jit(solution)/shard_map/ppermute | solution.py:314
  8.8 0.0 collective-permute-done.7.other_ref
  8.8 0.9 %copy-done.4 = bf16[20,1792]{1,0:T(8,128)(2,1)S(1)} copy-done((bf16[20,1792]{1,0:T(8,128)(2,1)S(1)}, bf16[20,1792]{1,0:T(8,128)(2,1)}, u32[]{:S(2)}) %copy-start.4) | copy-done | bytes 71704
  9.7 0.3 chunk_rows.1
  10.0 0.3 collective-permute-start.8
  10.3 2.0 %collective-permute-done.refs_0_ = bf16[40,896]{1,0:T(8,128)(2,1)S(1)} collective-permute-done((bf16[40,896]{1,0:T(8,128)(2,1)}, bf16[40,896]{1,0:T(8,128)(2,1)S(1)}, u32[]{:S(2)}, u32[]{:S(2)}) %collective-permute-start) | collective-permute-done | bytes 71712 | tf_op jit(solution)/shard_map/ppermute | solution.py:314
  12.3 0.0 collective-permute-start.2
  12.3 1.7 %collective-permute-done.1.refs_1_ = bf16[40,896]{1,0:T(8,128)(2,1)S(1)} collective-permute-done((bf16[40,896]{1,0:T(8,128)(2,1)}, bf16[40,896]{1,0:T(8,128)(2,1)S(1)}, u32[]{:S(2)}, u32[]{:S(2)}) %collective-permute-start.1) | collective-permute-done | bytes 71712 | tf_op jit(solution)/shard_map/ppermute | solution.py:314
  14.0 0.0 collective-permute-start.3
  14.0 1.4 %collective-permute-done.8.refs_1_ = bf16[40,896]{1,0:T(8,128)(2,1)S(1)} collective-permute-done((bf16[40,896]{1,0:T(8,128)(2,1)S(1)}, bf16[40,896]{1,0:T(8,128)(2,1)S(1)}, u32[]{:S(2)}, u32[]{:S(2)}) %collective-permute-start.8) | collective-permute-done | bytes 71712 | tf_op jit(solution)/shard_map/ppermute | solution.py:314
  15.4 0.2 merge_rows.3.refs_0_
  15.6 1.6 %collective-permute-start.9 = (bf16[40,1792]{1,0:T(8,128)(2,1)S(1)}, bf16[40,1792]{1,0:T(8,128)(2,1)S(1)}, u32[]{:S(2)}, u32[]{:S(2)}) collective-permute-start(bf16[40,1792]{1,0:T(8,128)(2,1)S(1)} %merge_rows.3.refs_0_), channel_id=1, source_target_pairs={{0,2},{1,5},{2,0},{3,7},{4,6},{5,1},{6,4},{7,3},{8,10},{9,13},{10,... | collective-permute-start | bytes 430088 | tf_op jit(solution)/shard_map/ppermute | solution.py:321
  17.3 0.0 collective-permute-done.2.refs_2_
  17.3 0.0 collective-permute-done.3.refs_3_
  17.3 0.2 merge_rows.2.refs_0_
  17.5 0.5 collective-permute-start.4
  18.1 1.6 %collective-permute-start.10 = (bf16[40,1792]{1,0:T(8,128)(2,1)S(1)}, bf16[40,1792]{1,0:T(8,128)(2,1)S(1)}, u32[]{:S(2)}, u32[]{:S(2)}) collective-permute-start(bf16[40,1792]{1,0:T(8,128)(2,1)S(1)} %merge_rows.3.refs_0_), channel_id=1, source_target_pairs={{0,4},{1,3},{2,6},{3,1},{4,0},{5,7},{6,2},{7,5},{8,12},{9,11},{10,... | collective-permute-start | bytes 430088 | tf_op jit(solution)/shard_map/ppermute | solution.py:321
  19.7 1.9 %collective-permute-done.9.refs_1_ = bf16[40,1792]{1,0:T(8,128)(2,1)S(1)} collective-permute-done((bf16[40,1792]{1,0:T(8,128)(2,1)S(1)}, bf16[40,1792]{1,0:T(8,128)(2,1)S(1)}, u32[]{:S(2)}, u32[]{:S(2)}) %collective-permute-start.9) | collective-permute-done | bytes 143392 | tf_op jit(solution)/shard_map/ppermute | solution.py:321
  21.5 1.6 %collective-permute-start.11 = (bf16[40,1792]{1,0:T(8,128)(2,1)S(1)}, bf16[40,1792]{1,0:T(8,128)(2,1)S(1)}, u32[]{:S(2)}, u32[]{:S(2)}) collective-permute-start(bf16[40,1792]{1,0:T(8,128)(2,1)S(1)} %collective-permute-done.9.refs_1_), channel_id=1, source_target_pairs={{0,4},{1,3},{2,6},{3,1},{4,0},{5,7},{6,2},{7,5},{8,12},{9,11},{10,... | collective-permute-start | bytes 430088 | tf_op jit(solution)/shard_map/ppermute | solution.py:321
  23.1 0.4 collective-permute-start.5
  23.6 1.0 %collective-permute-done.4.refs_1_ = bf16[40,1792]{1,0:T(8,128)(2,1)S(1)} collective-permute-done((bf16[40,1792]{1,0:T(8,128)(2,1)S(1)}, bf16[40,1792]{1,0:T(8,128)(2,1)S(1)}, u32[]{:S(2)}, u32[]{:S(2)}) %collective-permute-start.4) | collective-permute-done | bytes 143392 | tf_op jit(solution)/shard_map/ppermute | solution.py:321
  24.6 1.6 %collective-permute-start.6 = (bf16[40,1792]{1,0:T(8,128)(2,1)S(1)}, bf16[40,1792]{1,0:T(8,128)(2,1)S(1)}, u32[]{:S(2)}, u32[]{:S(2)}) collective-permute-start(bf16[40,1792]{1,0:T(8,128)(2,1)S(1)} %collective-permute-done.4.refs_1_), channel_id=1, source_target_pairs={{0,4},{1,3},{2,6},{3,1},{4,0},{5,7},{6,2},{7,5},{8,12},{9,11},{10,... | collective-permute-start | bytes 430088 | tf_op jit(solution)/shard_map/ppermute | solution.py:321
  26.2 0.0 collective-permute-done.10.refs_2_
  26.2 0.4 collective-permute-done.11.refs_3_
  26.6 1.0 %partial_products.3 = (f32[80,1152]{1,0:T(8,128)S(1)}, bf16[80,1792]{1,0:T(8,128)(2,1)S(1)}, bf16[80,1792]{1,0:T(8,128)(2,1)S(1)}) custom-call(bf16[40,1792]{1,0:T(8,128)(2,1)S(1)} %merge_rows.3.refs_0_, bf16[40,1792]{1,0:T(8,128)(2,1)S(1)} %collective-permute-done.9.refs_1_, bf16[40,1792]{1,0:T(8,128)(2,1)S(1)} %collective-permute-done.10.refs_2_, ...), custom_call_target="tpu_custom_call" | custom-call | flops 330301440 | bytes 4128768 | tf_op jit(solution)/shard_map/partial_products/pallas_call | solution.py:299
  27.7 0.1 collective-permute-start.13
  27.8 0.5 collective-permute-done.5.refs_2_
  28.2 1.5 %collective-permute-done.6.refs_3_ = bf16[40,1792]{1,0:T(8,128)(2,1)S(1)} collective-permute-done((bf16[40,1792]{1,0:T(8,128)(2,1)S(1)}, bf16[40,1792]{1,0:T(8,128)(2,1)S(1)}, u32[]{:S(2)}, u32[]{:S(2)}) %collective-permute-start.6) | collective-permute-done | bytes 143392 | tf_op jit(solution)/shard_map/ppermute | solution.py:321
  29.8 1.0 %partial_products.2 = (f32[80,1152]{1,0:T(8,128)S(1)}, bf16[80,1792]{1,0:T(8,128)(2,1)S(1)}, bf16[80,1792]{1,0:T(8,128)(2,1)S(1)}) custom-call(bf16[40,1792]{1,0:T(8,128)(2,1)S(1)} %merge_rows.2.refs_0_, bf16[40,1792]{1,0:T(8,128)(2,1)S(1)} %collective-permute-done.4.refs_1_, bf16[40,1792]{1,0:T(8,128)(2,1)S(1)} %collective-permute-done.5.refs_2_, ...), custom_call_target="tpu_custom_call" | custom-call | flops 330301440 | bytes 4128768 | tf_op jit(solution)/shard_map/partial_products/pallas_call | solution.py:299
  30.8 0.1 collective-permute-start.12
  30.9 0.0 collective-permute-done.13.refs_3_
  30.9 1.7 %collective-permute-done.12.refs_2_ = f32[80,1152]{1,0:T(8,128)S(1)} collective-permute-done((f32[80,1152]{1,0:T(8,128)S(1)}, f32[80,1152]{1,0:T(8,128)S(1)}, u32[]{:S(2)}, u32[]{:S(2)}) %collective-permute-start.12) | collective-permute-done | bytes 368672 | tf_op jit(solution)/shard_map/ppermute | solution.py:310
  32.6 1.4 %sides_and_parts.1 = (bf16[40,896]{1,0:T(8,128)(2,1)S(1)}, bf16[40,896]{1,0:T(8,128)(2,1)S(1)}, bf16[40,896]{1,0:T(8,128)(2,1)S(1)}, bf16[40,896]{1,0:T(8,128)(2...) custom-call(f32[80,1152]{1,0:T(8,128)S(1)} %get-tuple-element.41.ref, ...), custom_call_target="tpu_custom_call" | custom-call | flops 440401920 | bytes 2752512 | tf_op jit(solution)/shard_map/sides_and_parts/pallas_call | solution.py:299
  34.0 1.6 %collective-permute-start.14 = (bf16[40,896]{1,0:T(8,128)(2,1)S(1)}, bf16[40,896]{1,0:T(8,128)(2,1)S(1)}, u32[]{:S(2)}, u32[]{:S(2)}) collective-permute-start(bf16[40,896]{1,0:T(8,128)(2,1)S(1)} %get-tuple-element.48), channel_id=1, source_target_pairs={{0,2},{1,5},{2,0},{3,7},{4,6},{5,1},{6,4},{7,3},{8,10},{9,13},{10,... | collective-permute-start | bytes 215048 | tf_op jit(solution)/shard_map/ppermute | solution.py:321
  35.6 1.5 %collective-permute-start.15 = (bf16[40,896]{1,0:T(8,128)(2,1)S(1)}, bf16[40,896]{1,0:T(8,128)(2,1)S(1)}, u32[]{:S(2)}, u32[]{:S(2)}) collective-permute-start(bf16[40,896]{1,0:T(8,128)(2,1)S(1)} %get-tuple-element.49), channel_id=1, source_target_pairs={{0,4},{1,3},{2,6},{3,1},{4,0},{5,7},{6,2},{7,5},{8,12},{9,11},{10,... | collective-permute-start | bytes 215048 | tf_op jit(solution)/shard_map/ppermute | solution.py:321
  37.1 0.4 collective-permute-start.16
  37.5 1.5 %collective-permute-start.18 = (bf16[40,896]{1,0:T(8,128)(2,1)S(1)}, bf16[40,896]{1,0:T(8,128)(2,1)S(1)}, u32[]{:S(2)}, u32[]{:S(2)}) collective-permute-start(bf16[40,896]{1,0:T(8,128)(2,1)S(1)} %get-tuple-element.55), channel_id=1, source_target_pairs={{0,2},{1,5},{2,0},{3,7},{4,6},{5,1},{6,4},{7,3},{8,10},{9,13},{10,... | collective-permute-start | bytes 215048 | tf_op jit(solution)/shard_map/ppermute | solution.py:321
  39.0 1.5 %collective-permute-start.19 = (bf16[40,896]{1,0:T(8,128)(2,1)S(1)}, bf16[40,896]{1,0:T(8,128)(2,1)S(1)}, u32[]{:S(2)}, u32[]{:S(2)}) collective-permute-start(bf16[40,896]{1,0:T(8,128)(2,1)S(1)} %get-tuple-element.56), channel_id=1, source_target_pairs={{0,4},{1,3},{2,6},{3,1},{4,0},{5,7},{6,2},{7,5},{8,12},{9,11},{10,... | collective-permute-start | bytes 215048 | tf_op jit(solution)/shard_map/ppermute | solution.py:321
  40.6 0.0 collective-permute-done.14.refs_1_
  40.6 0.8 %collective-permute-start.20 = (bf16[40,896]{1,0:T(8,128)(2,1)S(1)}, bf16[40,896]{1,0:T(8,128)(2,1)S(1)}, u32[]{:S(2)}, u32[]{:S(2)}) collective-permute-start(bf16[40,896]{1,0:T(8,128)(2,1)S(1)} %get-tuple-element.57), channel_id=1, source_target_pairs={{0,6},{1,7},{2,4},{3,5},{4,2},{5,3},{6,0},{7,1},{8,14},{9,15},{10,... | collective-permute-start | bytes 215048 | tf_op jit(solution)/shard_map/ppermute | solution.py:321
  41.4 0.0 collective-permute-done.15.refs_2_
  41.4 1.1 %collective-permute-done.16.refs_3_ = bf16[40,896]{1,0:T(8,128)(2,1)S(1)} collective-permute-done((bf16[40,896]{1,0:T(8,128)(2,1)S(1)}, bf16[40,896]{1,0:T(8,128)(2,1)S(1)}, u32[]{:S(2)}, u32[]{:S(2)}) %collective-permute-start.16) | collective-permute-done | bytes 71712 | tf_op jit(solution)/shard_map/ppermute | solution.py:321
  42.4 0.5 sum_parts.2
  42.9 0.1 collective-permute-start.17
  43.1 0.5 collective-permute-done.18.refs_1_
  43.5 0.6 %collective-permute-done.19.refs_2_ = bf16[40,896]{1,0:T(8,128)(2,1)S(1)} collective-permute-done((bf16[40,896]{1,0:T(8,128)(2,1)S(1)}, bf16[40,896]{1,0:T(8,128)(2,1)S(1)}, u32[]{:S(2)}, u32[]{:S(2)}) %collective-permute-start.19) | collective-permute-done | bytes 71712 | tf_op jit(solution)/shard_map/ppermute | solution.py:321
  44.1 1.7 %collective-permute-done.20.refs_3_ = bf16[40,896]{1,0:T(8,128)(2,1)S(1)} collective-permute-done((bf16[40,896]{1,0:T(8,128)(2,1)S(1)}, bf16[40,896]{1,0:T(8,128)(2,1)S(1)}, u32[]{:S(2)}, u32[]{:S(2)}) %collective-permute-start.20) | collective-permute-done | bytes 71712 | tf_op jit(solution)/shard_map/ppermute | solution.py:321
  45.8 0.5 sum_parts.3
  46.3 1.9 %collective-permute-start.21 = (bf16[140,128]{1,0:T(8,128)(2,1)S(1)}, bf16[140,128]{1,0:T(8,128)(2,1)S(1)}, u32[]{:S(2)}, u32[]{:S(2)}) collective-permute-start(bf16[140,128]{1,0:T(8,128)(2,1)S(1)} %get-tuple-element.58), channel_id=1, source_target_pairs={{0,16},{2,18},{4,20},{6,22},{8,24},{10,26},{12,28},{14,30},{16,0},... | collective-permute-start | bytes 107528 | tf_op jit(solution)/shard_map/ppermute | solution.py:314
  48.3 1.4 %collective-permute-start.22 = (bf16[140,128]{1,0:T(8,128)(2,1)S(1)}, bf16[140,128]{1,0:T(8,128)(2,1)S(1)}, u32[]{:S(2)}, u32[]{:S(2)}) collective-permute-start(bf16[140,128]{1,0:T(8,128)(2,1)S(1)} %get-tuple-element.59), channel_id=1, source_target_pairs={{0,24},{2,26},{4,28},{6,30},{8,16},{10,18},{12,20},{14,22},{16,8},... | collective-permute-start | bytes 107528 | tf_op jit(solution)/shard_map/ppermute | solution.py:314
  49.6 2.5 %weight_grads.1 = (bf16[1792,384]{1,0:T(8,128)(2,1)}, bf16[1792,384]{1,0:T(8,128)(2,1)}, bf16[1792,384]{1,0:T(8,128)(2,1)}, f32[8,128]{1,0:T(8,128)S(1)}) custom-call(bf16[80,1792]{1,0:T(8,128)(2,1)S(1)} %get-tuple-element.60.refs_0_, bf16[80,1792]{1,0:T(8,128)(2,1)S(1)} %get-tuple-element.61.refs_1_, bf16[80,1792]{1,0:T(8,128)(2,1)S(1)} %get-tuple-element.62.refs_2_, ...), custom_call_target="tpu_custom_call" | custom-call | flops 660602880 | bytes 5275648 | tf_op jit(solution)/shard_map/weight_grads/pallas_call | solution.py:392
  52.1 0.0 collective-permute-done.17.refs_1_
  52.1 0.3 split_rows.2
  52.4 0.1 collective-permute-start.23
  52.5 0.0 collective-permute-done.21.refs_0_
  52.5 1.5 %collective-permute-done.22.refs_1_ = bf16[140,128]{1,0:T(8,128)(2,1)S(1)} collective-permute-done((bf16[140,128]{1,0:T(8,128)(2,1)S(1)}, bf16[140,128]{1,0:T(8,128)(2,1)S(1)}, u32[]{:S(2)}, u32[]{:S(2)}) %collective-permute-start.22) | collective-permute-done | bytes 35872 | tf_op jit(solution)/shard_map/ppermute | solution.py:314
  54.0 0.3 split_rows.3
  54.3 0.1 collective-permute-start.24
  54.4 0.0 collective-permute-done.23.refs_2_
  54.4 1.2 %collective-permute-done.24.refs_3_ = bf16[16,1792]{1,0:T(8,128)(2,1)S(1)} collective-permute-done((bf16[16,1792]{1,0:T(8,128)(2,1)S(1)}, bf16[16,1792]{1,0:T(8,128)(2,1)S(1)}, u32[]{:S(2)}, u32[]{:S(2)}) %collective-permute-start.24) | collective-permute-done | bytes 57376 | tf_op jit(solution)/shard_map/ppermute | solution.py:310
  55.6 1.3 %place_rows.1 = bf16[128,3584]{1,0:T(8,128)(2,1)} custom-call(f32[32,128]{1,0:T(8,128)S(1)} %copy-done.3, bf16[16,1792]{1,0:T(8,128)(2,1)S(1)} %get-tuple-element.53.refs_0_, bf16[16,1792]{1,0:T(8,128)(2,1)S(1)} %get-tuple-element.66.refs_1_, bf16[16,1792]{1,0:T(8,128)(2,1)S(1)} %collective-permute-done.23.refs_2_, ...), custom_call_target="tpu_custom_call" | custom-call | tf_op jit(solution)/shard_map/place_rows/pallas_call | solution.py:423
  (9 shorter events, 0.0 us)
Async XLA Ops:
  3.3 5.5 %collective-permute-start.7 = (bf16[20,1792]{1,0:T(8,128)(2,1)}, bf16[20,1792]{1,0:T(8,128)(2,1)S(1)}, u32[]{:S(2)}, u32[]{:S(2)}) collective-permute-start(bf16[20,1792]{1,0:T(8,128)(2,1)} %get-tuple-element.43), channel_id=1, source_target_pairs={{0,1},{1,0},{2,3},{3,2},{4,5},{5,4},{6,7},{7,6},{8,9},{9,8},{10,11... | collective-permute-start | bytes 215048 | tf_op jit(solution)/shard_map/ppermute | solution.py:310
  3.8 8.5 %collective-permute-start = (bf16[40,896]{1,0:T(8,128)(2,1)}, bf16[40,896]{1,0:T(8,128)(2,1)S(1)}, u32[]{:S(2)}, u32[]{:S(2)}) collective-permute-start(bf16[40,896]{1,0:T(8,128)(2,1)} %get-tuple-element.39), channel_id=1, source_target_pairs={{0,16},{2,18},{4,20},{6,22},{8,24},{10,26},{12,28},{14,30},{16,0},... | collective-permute-start | bytes 215048 | tf_op jit(solution)/shard_map/ppermute | solution.py:314
  7.5 6.6 %collective-permute-start.1 = (bf16[40,896]{1,0:T(8,128)(2,1)}, bf16[40,896]{1,0:T(8,128)(2,1)S(1)}, u32[]{:S(2)}, u32[]{:S(2)}) collective-permute-start(bf16[40,896]{1,0:T(8,128)(2,1)} %get-tuple-element.40), channel_id=1, source_target_pairs={{0,24},{2,26},{4,28},{6,30},{8,16},{10,18},{12,20},{14,22},{16,8},... | collective-permute-start | bytes 215048 | tf_op jit(solution)/shard_map/ppermute | solution.py:314
  8.8 0.9 %copy-start.4 = (bf16[20,1792]{1,0:T(8,128)(2,1)S(1)}, bf16[20,1792]{1,0:T(8,128)(2,1)}, u32[]{:S(2)}) copy-start(bf16[20,1792]{1,0:T(8,128)(2,1)} %get-tuple-element.42.mine_ref) | copy-start | bytes 215044
  9.7 16.9 %copy-start = (bf16[1792,384]{1,0:T(8,128)(2,1)S(1)}, bf16[1792,384]{1,0:T(8,128)(2,1)}, u32[]{:S(2)}) copy-start(bf16[1792,384]{1,0:T(8,128)(2,1)} %refs_4_.7) | copy-start | bytes 4128772
  9.7 16.9 %copy-start.1 = (bf16[1792,384]{1,0:T(8,128)(2,1)S(1)}, bf16[1792,384]{1,0:T(8,128)(2,1)}, u32[]{:S(2)}) copy-start(bf16[1792,384]{1,0:T(8,128)(2,1)} %refs_5_.5) | copy-start | bytes 4128772
  9.7 16.9 %copy-start.2 = (bf16[1792,384]{1,0:T(8,128)(2,1)S(1)}, bf16[1792,384]{1,0:T(8,128)(2,1)}, u32[]{:S(2)}) copy-start(bf16[1792,384]{1,0:T(8,128)(2,1)} %refs_6_.3) | copy-start | bytes 4128772
  10.0 5.4 %collective-permute-start.8 = (bf16[40,896]{1,0:T(8,128)(2,1)S(1)}, bf16[40,896]{1,0:T(8,128)(2,1)S(1)}, u32[]{:S(2)}, u32[]{:S(2)}) collective-permute-start(bf16[40,896]{1,0:T(8,128)(2,1)S(1)} %get-tuple-element.45), channel_id=1, source_target_pairs={{0,8},{2,10},{4,12},{6,14},{8,0},{10,2},{12,4},{14,6},{16,24},{18,... | collective-permute-start | bytes 215048 | tf_op jit(solution)/shard_map/ppermute | solution.py:314
  12.3 5.0 %collective-permute-start.2 = (bf16[40,896]{1,0:T(8,128)(2,1)S(1)}, bf16[40,896]{1,0:T(8,128)(2,1)S(1)}, u32[]{:S(2)}, u32[]{:S(2)}) collective-permute-start(bf16[40,896]{1,0:T(8,128)(2,1)S(1)} %collective-permute-done.refs_0_), channel_id=1, source_target_pairs={{0,1},{1,0},{2,3},{3,2},{4,5},{5,4},{6,7},{7,6},{8,9},{9,8},{10,11... | collective-permute-start | bytes 215048 | tf_op jit(solution)/shard_map/ppermute | solution.py:310
  14.0 3.2 %collective-permute-start.3 = (bf16[40,896]{1,0:T(8,128)(2,1)S(1)}, bf16[40,896]{1,0:T(8,128)(2,1)S(1)}, u32[]{:S(2)}, u32[]{:S(2)}) collective-permute-start(bf16[40,896]{1,0:T(8,128)(2,1)S(1)} %collective-permute-done.1.refs_1_), channel_id=1, source_target_pairs={{0,1},{1,0},{2,3},{3,2},{4,5},{5,4},{6,7},{7,6},{8,9},{9,8},{10,11... | collective-permute-start | bytes 215048 | tf_op jit(solution)/shard_map/ppermute | solution.py:310
  15.6 5.9 %collective-permute-start.9 = (bf16[40,1792]{1,0:T(8,128)(2,1)S(1)}, bf16[40,1792]{1,0:T(8,128)(2,1)S(1)}, u32[]{:S(2)}, u32[]{:S(2)}) collective-permute-start(bf16[40,1792]{1,0:T(8,128)(2,1)S(1)} %merge_rows.3.refs_0_), channel_id=1, source_target_pairs={{0,2},{1,5},{2,0},{3,7},{4,6},{5,1},{6,4},{7,3},{8,10},{9,13},{10,... | collective-permute-start | bytes 430088 | tf_op jit(solution)/shard_map/ppermute | solution.py:321
  17.5 7.1 %collective-permute-start.4 = (bf16[40,1792]{1,0:T(8,128)(2,1)S(1)}, bf16[40,1792]{1,0:T(8,128)(2,1)S(1)}, u32[]{:S(2)}, u32[]{:S(2)}) collective-permute-start(bf16[40,1792]{1,0:T(8,128)(2,1)S(1)} %merge_rows.2.refs_0_), channel_id=1, source_target_pairs={{0,2},{1,5},{2,0},{3,7},{4,6},{5,1},{6,4},{7,3},{8,10},{9,13},{10,... | collective-permute-start | bytes 430088 | tf_op jit(solution)/shard_map/ppermute | solution.py:321
  18.1 8.2 %collective-permute-start.10 = (bf16[40,1792]{1,0:T(8,128)(2,1)S(1)}, bf16[40,1792]{1,0:T(8,128)(2,1)S(1)}, u32[]{:S(2)}, u32[]{:S(2)}) collective-permute-start(bf16[40,1792]{1,0:T(8,128)(2,1)S(1)} %merge_rows.3.refs_0_), channel_id=1, source_target_pairs={{0,4},{1,3},{2,6},{3,1},{4,0},{5,7},{6,2},{7,5},{8,12},{9,11},{10,... | collective-permute-start | bytes 430088 | tf_op jit(solution)/shard_map/ppermute | solution.py:321
  21.5 5.1 %collective-permute-start.11 = (bf16[40,1792]{1,0:T(8,128)(2,1)S(1)}, bf16[40,1792]{1,0:T(8,128)(2,1)S(1)}, u32[]{:S(2)}, u32[]{:S(2)}) collective-permute-start(bf16[40,1792]{1,0:T(8,128)(2,1)S(1)} %collective-permute-done.9.refs_1_), channel_id=1, source_target_pairs={{0,4},{1,3},{2,6},{3,1},{4,0},{5,7},{6,2},{7,5},{8,12},{9,11},{10,... | collective-permute-start | bytes 430088 | tf_op jit(solution)/shard_map/ppermute | solution.py:321
  23.1 5.1 %collective-permute-start.5 = (bf16[40,1792]{1,0:T(8,128)(2,1)S(1)}, bf16[40,1792]{1,0:T(8,128)(2,1)S(1)}, u32[]{:S(2)}, u32[]{:S(2)}) collective-permute-start(bf16[40,1792]{1,0:T(8,128)(2,1)S(1)} %merge_rows.2.refs_0_), channel_id=1, source_target_pairs={{0,4},{1,3},{2,6},{3,1},{4,0},{5,7},{6,2},{7,5},{8,12},{9,11},{10,... | collective-permute-start | bytes 430088 | tf_op jit(solution)/shard_map/ppermute | solution.py:321
  24.6 5.2 %collective-permute-start.6 = (bf16[40,1792]{1,0:T(8,128)(2,1)S(1)}, bf16[40,1792]{1,0:T(8,128)(2,1)S(1)}, u32[]{:S(2)}, u32[]{:S(2)}) collective-permute-start(bf16[40,1792]{1,0:T(8,128)(2,1)S(1)} %collective-permute-done.4.refs_1_), channel_id=1, source_target_pairs={{0,4},{1,3},{2,6},{3,1},{4,0},{5,7},{6,2},{7,5},{8,12},{9,11},{10,... | collective-permute-start | bytes 430088 | tf_op jit(solution)/shard_map/ppermute | solution.py:321
  27.7 3.2 %collective-permute-start.13 = (f32[80,1152]{1,0:T(8,128)S(1)}, f32[80,1152]{1,0:T(8,128)S(1)}, u32[]{:S(2)}, u32[]{:S(2)}) collective-permute-start(f32[80,1152]{1,0:T(8,128)S(1)} %get-tuple-element.46.refs_1_), channel_id=1, source_target_pairs={{0,1},{1,0},{2,3},{3,2},{4,5},{5,4},{6,7},{7,6},{8,9},{9,8},{10,11... | collective-permute-start | bytes 1105928 | tf_op jit(solution)/shard_map/ppermute | solution.py:310
  30.8 1.8 %collective-permute-start.12 = (f32[80,1152]{1,0:T(8,128)S(1)}, f32[80,1152]{1,0:T(8,128)S(1)}, u32[]{:S(2)}, u32[]{:S(2)}) collective-permute-start(f32[80,1152]{1,0:T(8,128)S(1)} %get-tuple-element.41.refs_0_), channel_id=1, source_target_pairs={{0,1},{1,0},{2,3},{3,2},{4,5},{5,4},{6,7},{7,6},{8,9},{9,8},{10,11... | collective-permute-start | bytes 1105928 | tf_op jit(solution)/shard_map/ppermute | solution.py:310
  34.0 6.6 %collective-permute-start.14 = (bf16[40,896]{1,0:T(8,128)(2,1)S(1)}, bf16[40,896]{1,0:T(8,128)(2,1)S(1)}, u32[]{:S(2)}, u32[]{:S(2)}) collective-permute-start(bf16[40,896]{1,0:T(8,128)(2,1)S(1)} %get-tuple-element.48), channel_id=1, source_target_pairs={{0,2},{1,5},{2,0},{3,7},{4,6},{5,1},{6,4},{7,3},{8,10},{9,13},{10,... | collective-permute-start | bytes 215048 | tf_op jit(solution)/shard_map/ppermute | solution.py:321
  35.6 5.8 %collective-permute-start.15 = (bf16[40,896]{1,0:T(8,128)(2,1)S(1)}, bf16[40,896]{1,0:T(8,128)(2,1)S(1)}, u32[]{:S(2)}, u32[]{:S(2)}) collective-permute-start(bf16[40,896]{1,0:T(8,128)(2,1)S(1)} %get-tuple-element.49), channel_id=1, source_target_pairs={{0,4},{1,3},{2,6},{3,1},{4,0},{5,7},{6,2},{7,5},{8,12},{9,11},{10,... | collective-permute-start | bytes 215048 | tf_op jit(solution)/shard_map/ppermute | solution.py:321
  37.1 5.4 %collective-permute-start.16 = (bf16[40,896]{1,0:T(8,128)(2,1)S(1)}, bf16[40,896]{1,0:T(8,128)(2,1)S(1)}, u32[]{:S(2)}, u32[]{:S(2)}) collective-permute-start(bf16[40,896]{1,0:T(8,128)(2,1)S(1)} %get-tuple-element.50), channel_id=1, source_target_pairs={{0,6},{1,7},{2,4},{3,5},{4,2},{5,3},{6,0},{7,1},{8,14},{9,15},{10,... | collective-permute-start | bytes 215048 | tf_op jit(solution)/shard_map/ppermute | solution.py:321
  37.5 6.0 %collective-permute-start.18 = (bf16[40,896]{1,0:T(8,128)(2,1)S(1)}, bf16[40,896]{1,0:T(8,128)(2,1)S(1)}, u32[]{:S(2)}, u32[]{:S(2)}) collective-permute-start(bf16[40,896]{1,0:T(8,128)(2,1)S(1)} %get-tuple-element.55), channel_id=1, source_target_pairs={{0,2},{1,5},{2,0},{3,7},{4,6},{5,1},{6,4},{7,3},{8,10},{9,13},{10,... | collective-permute-start | bytes 215048 | tf_op jit(solution)/shard_map/ppermute | solution.py:321
  39.0 5.1 %collective-permute-start.19 = (bf16[40,896]{1,0:T(8,128)(2,1)S(1)}, bf16[40,896]{1,0:T(8,128)(2,1)S(1)}, u32[]{:S(2)}, u32[]{:S(2)}) collective-permute-start(bf16[40,896]{1,0:T(8,128)(2,1)S(1)} %get-tuple-element.56), channel_id=1, source_target_pairs={{0,4},{1,3},{2,6},{3,1},{4,0},{5,7},{6,2},{7,5},{8,12},{9,11},{10,... | collective-permute-start | bytes 215048 | tf_op jit(solution)/shard_map/ppermute | solution.py:321
  40.6 5.2 %collective-permute-start.20 = (bf16[40,896]{1,0:T(8,128)(2,1)S(1)}, bf16[40,896]{1,0:T(8,128)(2,1)S(1)}, u32[]{:S(2)}, u32[]{:S(2)}) collective-permute-start(bf16[40,896]{1,0:T(8,128)(2,1)S(1)} %get-tuple-element.57), channel_id=1, source_target_pairs={{0,6},{1,7},{2,4},{3,5},{4,2},{5,3},{6,0},{7,1},{8,14},{9,15},{10,... | collective-permute-start | bytes 215048 | tf_op jit(solution)/shard_map/ppermute | solution.py:321
  42.9 9.2 %collective-permute-start.17 = (bf16[140,128]{1,0:T(8,128)(2,1)S(1)}, bf16[140,128]{1,0:T(8,128)(2,1)S(1)}, u32[]{:S(2)}, u32[]{:S(2)}) collective-permute-start(bf16[140,128]{1,0:T(8,128)(2,1)S(1)} %get-tuple-element.52), channel_id=1, source_target_pairs={{0,8},{2,10},{4,12},{6,14},{8,0},{10,2},{12,4},{14,6},{16,24},{18,... | collective-permute-start | bytes 107528 | tf_op jit(solution)/shard_map/ppermute | solution.py:314
  46.3 6.2 %collective-permute-start.21 = (bf16[140,128]{1,0:T(8,128)(2,1)S(1)}, bf16[140,128]{1,0:T(8,128)(2,1)S(1)}, u32[]{:S(2)}, u32[]{:S(2)}) collective-permute-start(bf16[140,128]{1,0:T(8,128)(2,1)S(1)} %get-tuple-element.58), channel_id=1, source_target_pairs={{0,16},{2,18},{4,20},{6,22},{8,24},{10,26},{12,28},{14,30},{16,0},... | collective-permute-start | bytes 107528 | tf_op jit(solution)/shard_map/ppermute | solution.py:314
  48.3 5.8 %collective-permute-start.22 = (bf16[140,128]{1,0:T(8,128)(2,1)S(1)}, bf16[140,128]{1,0:T(8,128)(2,1)S(1)}, u32[]{:S(2)}, u32[]{:S(2)}) collective-permute-start(bf16[140,128]{1,0:T(8,128)(2,1)S(1)} %get-tuple-element.59), channel_id=1, source_target_pairs={{0,24},{2,26},{4,28},{6,30},{8,16},{10,18},{12,20},{14,22},{16,8},... | collective-permute-start | bytes 107528 | tf_op jit(solution)/shard_map/ppermute | solution.py:314
  52.4 2.0 %collective-permute-start.23 = (bf16[16,1792]{1,0:T(8,128)(2,1)S(1)}, bf16[16,1792]{1,0:T(8,128)(2,1)S(1)}, u32[]{:S(2)}, u32[]{:S(2)}) collective-permute-start(bf16[16,1792]{1,0:T(8,128)(2,1)S(1)} %get-tuple-element.67), channel_id=1, source_target_pairs={{0,1},{1,0},{2,3},{3,2},{4,5},{5,4},{6,7},{7,6},{8,9},{9,8},{10,11... | collective-permute-start | bytes 172040 | tf_op jit(solution)/shard_map/ppermute | solution.py:310
  54.0 1.6 %copy-start.3 = (f32[32,128]{1,0:T(8,128)S(1)}, f32[32,128]{1,0:T(8,128)}, u32[]{:S(2)}) copy-start(f32[32,128]{1,0:T(8,128)} %get-tuple-element.38.hot_ref) | copy-start | bytes 49156
  54.3 1.3 %collective-permute-start.24 = (bf16[16,1792]{1,0:T(8,128)(2,1)S(1)}, bf16[16,1792]{1,0:T(8,128)(2,1)S(1)}, u32[]{:S(2)}, u32[]{:S(2)}) collective-permute-start(bf16[16,1792]{1,0:T(8,128)(2,1)S(1)} %get-tuple-element.68), channel_id=1, source_target_pairs={{0,1},{1,0},{2,3},{3,2},{4,5},{5,4},{6,7},{7,6},{8,9},{9,8},{10,11... | collective-permute-start | bytes 172040 | tf_op jit(solution)/shard_map/ppermute | solution.py:310
